TPU v7x, 32 devices: a whole 2x2x4 slice. The times are simulated.
32 devices in a mesh: pool: 2 (over y), ctx: 4 (over x, core), head: 4 (over z).
Axes of the slice: x: 2, y: 2, z: 4, core: 2. Of those that a mesh axis runs over, the one named last changes fastest.
Arguments:
- kv_pool: bfloat16 [4, 64, 2, 32, 1024], P('ctx', 'pool', None, None, 'head'), may hold values from -6 to 6
- state_pool: bfloat16 [64, 64, 1024], P('pool', 'ctx', 'head'), may hold values from -0.59765625 to 0.59765625
- block_owner: int32 [4, 64], P('ctx'), may hold values from 0 to 1, as said below
- block_index: int32 [4, 64], P('ctx'), may hold values from 0 to 31, as said below
- history_len: int32 [2], P('pool'), may hold values from 1 to 4096, as said below
- turn_len: int32 [2], P('pool'), may hold values from 256 to 512, as said below
- mixer_in: bfloat16 [2, 128, 64, 512], P('pool', 'head', 'ctx'), may hold values from -6 to 6
- input_proj: bfloat16 [2, 8, 256, 512], P('pool', 'head'), may hold values from -1.5 to 1.5
- output_proj: bfloat16 [2, 8, 256, 512], P('pool', 'head'), may hold values from -6 to 6
- step_size: float32 [2, 128, 512], P('pool', 'head'), may hold values from 0 to 2, as said below
- decay_rate: float32 [128], P('head'), may hold values from 0 to 4, as said below
- bypass_factor: float32 [128], P('head'), may hold values from 0.5 to 1.5
- queries: bfloat16 [2, 512, 8192], P('pool', 'ctx', 'head'), may hold values from -300 to 300
- turn_kv: bfloat16 [2, 2, 512, 1024], P('pool', None, 'ctx', 'head'), may hold values from -6 to 6
Outputs:
- mixer_out: bfloat16 [2, 128, 64, 512], P('pool', 'head', 'ctx')
- next_state: float32 [2, 128, 64, 256], P('pool', 'head', 'ctx')
- attn_out: bfloat16 [2, 512, 8192], P('pool', 'ctx', 'head')
Inputs may be any that keep to these rules, and one draw needn't show every extreme that they name: `block_owner`: in each row c, every session owns exactly 32 slots, and each aligned run of 32 slots (one pool shard) holds at most 32 blocks of any one session; in every row some shard holds exactly 32 blocks of some session. `block_index`: in each row, the slots of one session carry the indices 0 to 31, each once. `history_len`: some session has exactly 4096. `turn_len`: every value is at least 256 and some session has exactly 512. `step_size`: Positive. `decay_rate`: Positive.
All inputs are finite; a program needn't handle non-finite values.
Results may differ from a plain program's by a relative error of at most 0.008.
Values may be sent and summed in bfloat16 or wider, within the bound.
No kernel may reach another device: no remote copies, remote signals or barrier semaphores. Data moves between devices by JAX's collectives and lax.ppermute only.
A program may use at most 64 MiB of HBM per device.

v0:
```python
import jax
import jax.numpy as jnp
from jax import lax
from jax.sharding import PartitionSpec as P

Q_HEADS = 64
KV_HEADS = 8
HEAD_DIM = 128
PAGE = 32
BLK = 128


floor_score = -1e30


def spanned_ssd(
    values, input_proj, output_proj, step_sizes, rates, bypass_factor, start_state, valid_len
):
    heads, channels, total = values.shape
    groups = input_proj.shape[0]
    per_group = heads // groups
    count = total // BLK
    positions = jnp.arange(total, dtype=jnp.int32)
    live = positions < valid_len
    step_sizes = jnp.where(live[None, :], step_sizes, jnp.float32(0.0))
    value_blocks = values.reshape(heads, channels, count, BLK).transpose(2, 0, 1, 3)
    input_blocks = input_proj.reshape(groups, -1, count, BLK).transpose(2, 0, 1, 3)
    output_blocks = output_proj.reshape(groups, -1, count, BLK).transpose(2, 0, 1, 3)
    step_blocks = step_sizes.reshape(heads, count, BLK).transpose(1, 0, 2)
    offsets = jnp.arange(BLK, dtype=jnp.int32)
    lower = offsets[:, None] >= offsets[None, :]
    exact = lax.Precision.HIGHEST

    def advance(carried, item):
        value_blk, input_blk, output_blk, step_blk = item
        value_blk = value_blk.astype(jnp.float32)
        input_blk = input_blk.astype(jnp.float32)
        output_blk = output_blk.astype(jnp.float32)
        running = jnp.cumsum(-rates[:, None] * step_blk, axis=1)
        pairs = jnp.einsum("gnt,gns->gts", output_blk, input_blk, precision=exact)
        pairs = jnp.repeat(pairs, per_group, axis=0)
        gaps = jnp.minimum(running[:, :, None] - running[:, None, :], 0.0)
        mixing = jnp.where(lower[None], jnp.exp(gaps), 0.0) * pairs * step_blk[:, None, :]
        result = jnp.einsum("hts,hps->hpt", mixing, value_blk, precision=exact)
        read_out = jnp.repeat(output_blk, per_group, axis=0)
        result = result + jnp.exp(running)[:, None, :] * jnp.einsum(
            "hpn,hnt->hpt", carried, read_out, precision=exact
        )
        result = result + bypass_factor[:, None, None] * value_blk
        weights = jnp.exp(running[:, -1:] - running) * step_blk
        write_in = jnp.repeat(input_blk, per_group, axis=0)
        carried = jnp.exp(running[:, -1])[:, None, None] * carried + jnp.einsum(
            "hps,hns->hpn", value_blk * weights[:, None, :], write_in, precision=exact
        )
        return (carried, result)

    final_state, results = lax.scan(
        advance, start_state, (value_blocks, input_blocks, output_blocks, step_blocks)
    )
    results = results.transpose(1, 2, 0, 3).reshape(heads, channels, total)
    return (jnp.where(live[None, None, :], results, 0.0), final_state)


def route_blocks(kv_local, state_local, owner_row, index_row):
    parties = lax.axis_size("pool")
    myself = lax.axis_index("pool")
    pages = kv_local.shape[1]
    capacity = 2 * pages // parties
    sessions = jnp.arange(parties, dtype=jnp.int32)
    table = (
        (owner_row[:, None] == sessions[None, :]).astype(jnp.int32).reshape(parties, pages, parties)
    )
    before = jnp.cumsum(table, axis=1) - table
    ranks = jnp.sum(before * table, axis=2)
    owners = owner_row.reshape(parties, pages)
    my_owner = lax.dynamic_index_in_dim(owners, myself, 0, keepdims=False)
    device_rank = lax.dynamic_index_in_dim(ranks, myself, 0, keepdims=False)
    send_kv = (
        jnp.zeros((parties, capacity) + kv_local.shape[2:], kv_local.dtype)
        .at[my_owner, device_rank]
        .set(kv_local[0])
    )
    send_state = (
        jnp.zeros((parties, capacity) + state_local.shape[1:], state_local.dtype)
        .at[my_owner, device_rank]
        .set(state_local)
    )
    recv_kv, recv_state = (
        lax.all_to_all(send_kv, "pool", split_axis=0, concat_axis=0, tiled=True),
        lax.all_to_all(send_state, "pool", split_axis=0, concat_axis=0, tiled=True),
    )
    flat_place = (sessions[:, None] * capacity + ranks).reshape(-1)
    target = jnp.where(owner_row == myself, index_row, pages)
    where_from = jnp.zeros((pages,), jnp.int32).at[target].set(flat_place, mode="drop")
    hist_pages = recv_kv.reshape((parties * capacity,) + recv_kv.shape[2:])[where_from]
    start_slabs = recv_state.reshape((parties * capacity,) + recv_state.shape[2:])[where_from]
    return (hist_pages, start_slabs)


def attend_block(carried, query_rows, query_index, block, seg_id, hist_rows, history_len):
    rows = query_rows.shape[0]
    key_rows = block.shape[1]
    width = block.shape[2]
    groups = width // HEAD_DIM
    per_group = Q_HEADS // KV_HEADS
    turn_rows = key_rows - hist_rows
    offsets = jnp.arange(key_rows, dtype=jnp.int32)
    in_history = offsets < hist_rows
    placed = jnp.where(
        in_history, seg_id * hist_rows + offsets, seg_id * turn_rows + offsets - hist_rows
    )
    seen_mask = jnp.where(
        in_history[None, :],
        (placed < history_len)[None, :],
        placed[None, :] <= query_index[:, None],
    )
    score_scale = HEAD_DIM ** (-0.5)
    peak, totals, summed = carried
    query_heads = query_rows.reshape(rows, groups, per_group, HEAD_DIM)
    key_heads = block[0].reshape(key_rows, groups, HEAD_DIM)
    value_heads = block[1].reshape(key_rows, groups, HEAD_DIM)
    scores = (
        jnp.einsum("rgqd,kgd->rgqk", query_heads, key_heads, preferred_element_type=jnp.float32)
        * score_scale
    )
    mask = seen_mask[:, None, None, :]
    fresh = jnp.maximum(peak, jnp.max(jnp.where(mask, scores, floor_score), axis=-1))
    weights = jnp.where(mask, jnp.exp(scores - fresh[..., None]), 0.0)
    fade = jnp.exp(peak - fresh)
    totals = fade * totals + jnp.sum(weights, axis=-1)
    summed = fade[..., None] * summed + jnp.einsum(
        "rgqk,kgd->rgqd",
        weights.astype(jnp.bfloat16),
        value_heads,
        preferred_element_type=jnp.float32,
    )
    return (fresh, totals, summed)


def context_attention(query_rows, history, turn_keys, history_len, turn_len):
    turn_rows = query_rows.shape[0]
    hist_rows = history.shape[1]
    seg_rows = hist_rows + turn_rows
    width = history.shape[-1]
    groups = width // HEAD_DIM
    per_group = Q_HEADS // KV_HEADS
    segment = lax.axis_index("ctx")
    local_keys = jnp.concatenate([history, turn_keys], axis=1)
    row_ids = jnp.arange(turn_rows, dtype=jnp.int32)
    own_index = segment * turn_rows + row_ids
    carried = (
        jnp.full((turn_rows, groups, per_group), floor_score, jnp.float32),
        jnp.zeros((turn_rows, groups, per_group), jnp.float32),
        jnp.zeros((turn_rows, groups, per_group, HEAD_DIM), jnp.float32),
    )
    piece = lax.all_gather(local_keys, "ctx", axis=1, tiled=True)
    count = piece.shape[1] // seg_rows
    blocks = piece.reshape(2, count, seg_rows, width).transpose(1, 0, 2, 3)

    def visit(inner, item):
        block, offset = item
        return (
            attend_block(inner, query_rows, own_index, block, offset, hist_rows, history_len),
            None,
        )

    carried, _ = lax.scan(visit, carried, (blocks, jnp.arange(count, dtype=jnp.int32)))
    peak, totals, summed = carried
    result = (summed / totals[..., None]).reshape(turn_rows, groups * per_group * HEAD_DIM)
    return jnp.where((own_index < turn_len)[:, None], result, 0.0).astype(jnp.bfloat16)


def local(
    kv_pool,
    state_pool,
    block_owner,
    block_index,
    history_len,
    turn_len,
    mixer_in,
    input_proj,
    output_proj,
    step_size,
    decay_rate,
    bypass_factor,
    queries,
    turn_kv,
):
    hist_pages, start_slabs = route_blocks(kv_pool, state_pool, block_owner[0], block_index[0])
    pages = hist_pages.shape[0]
    width = hist_pages.shape[-1]
    history = hist_pages.transpose(1, 0, 2, 3).reshape(2, pages * PAGE, width)
    mixed, final = spanned_ssd(
        mixer_in[0],
        input_proj[0],
        output_proj[0],
        step_size[0],
        decay_rate,
        bypass_factor,
        start_slabs.astype(jnp.float32),
        turn_len[0],
    )
    attended = context_attention(queries[0], history, turn_kv[0], history_len[0], turn_len[0])
    return (mixed.astype(jnp.bfloat16)[None], final[None], attended[None])


def solution(mesh):
    return jax.shard_map(
        local,
        mesh=mesh,
        in_specs=(
            P("ctx", "pool", None, None, "head"),
            P("pool", "ctx", "head"),
            P("ctx", None),
            P("ctx", None),
            P("pool"),
            P("pool"),
            P("pool", "head", "ctx", None),
            P("pool", "head", None, None),
            P("pool", "head", None, None),
            P("pool", "head", None),
            P("head"),
            P("head"),
            P("pool", "ctx", "head"),
            P("pool", None, "ctx", "head"),
        ),
        out_specs=(
            P("pool", "head", "ctx", None),
            P("pool", "head", "ctx", None),
            P("pool", "ctx", "head"),
        ),
        check_vma=False,
    )
```

profile of v0, /device:TPU:0, one launch (start us, length us, event | category | flops | bytes accessed | tf_op | source)
XLA Modules:
  0.0 222.4 jit_solution(8317113022157147958)
XLA Ops:
  7.7 1.3 reduce.5
  10.3 4.3 %scatter_fusion = bf16[2,32,16,256]{3,2,1,0:T(8,128)(2,1)} fusion(bf16[2,32,16,256]{3,2,1,0:T(8,128)(2,1)} %broadcast_in_dim.176, s32[32]{0:T(128)S(1)} %fusion.46, bf16[32,16,256]{2,1,0:T(8,128)(2,1)} %param.19), kind=kCustom, calls=%fused_computation.2 | custom fusion | bytes 786688 | tf_op jit(solution)/shard_map/scatter | solution.py:86
  14.6 4.2 %all-to-all-start = ((bf16[2,32,16,256]{3,2,1,0:T(8,128)(2,1)}), bf16[2,32,16,256]{3,2,1,0:T(8,128)(2,1)S(1)}, u32[]{:S(2)}, u32[]{:S(2)}) async-start(bf16[2,32,16,256]{3,2,1,0:T(8,128)(2,1)} %scatter_fusion), calls=%async_computation | async-start | bytes 1048576 | tf_op jit(solution)/shard_map/all_to_all | solution.py:90
  20.2 1.6 broadcast_in_dim.189
  21.7 4.9 %scatter_fusion.1 = bf16[2,32,2,32,256]{4,3,2,1,0:T(8,128)(2,1)} fusion(bf16[2,32,2,32,256]{4,3,2,1,0:T(8,128)(2,1)} %broadcast_in_dim.189, s32[32]{0:T(128)S(1)} %fusion.46, bf16[32,2,32,256]{3,2,1,0:T(8,128)(2,1)S(1)} %bitcast.213), kind=kCustom, calls=%fused_computation.4 | custom fusion | bytes 3145984 | tf_op jit(solution)/shard_map/scatter | solution.py:81
  27.6 4.8 %all-to-all-start.1 = ((bf16[2,32,2,32,256]{4,3,2,1,0:T(8,128)(2,1)}), bf16[2,32,2,32,256]{4,3,2,1,0:T(8,128)(2,1)}, u32[]{:S(2)}, u32[]{:S(2)}) async-start(bf16[2,32,2,32,256]{4,3,2,1,0:T(8,128)(2,1)} %scatter_fusion.1), calls=%async_computation.1 | async-start | bytes 4194304 | tf_op jit(solution)/shard_map/all_to_all | solution.py:89
  36.0 21.5 %all-to-all-done.1 = bf16[2,32,2,32,256]{4,3,2,1,0:T(8,128)(2,1)} async-done(((bf16[2,32,2,32,256]{4,3,2,1,0:T(8,128)(2,1)}), bf16[2,32,2,32,256]{4,3,2,1,0:T(8,128)(2,1)}, u32[]{:S(2)}, u32[]{:S(2)}) %all-to-all-start.1) | async-done | bytes 2097184 | tf_op jit(solution)/shard_map/all_to_all | solution.py:89
  57.4 3.2 %gather_fusion.1 = bf16[32,2,32,256]{3,2,1,0:T(8,128)(2,1)} fusion(bf16[64,2,32,256]{3,2,1,0:T(8,128)(2,1)} %bitcast.18, s32[1024]{0:T(1024)S(1)} %pad_clamp_fusion), kind=kCustom, calls=%fused_computation.1 | custom fusion | bytes 2097280 | tf_op jit(solution)/shard_map/gather | solution.py:95
  60.6 1.3 copy.46
  61.9 1.1 pad_maximum_fusion
  63.1 52.2 %while.32 = (s32[]{:T(128)}, f32[32,16,256]{2,1,0:T(8,128)S(1)}, bf16[4,32,16,128]{3,2,1,0:T(8,128)(2,1)}, f32[32,1]{0,1:T(1,128)S(1)}, f32[4,32,128]{2,0,1:T(4,...) while((s32[]{:T(128)}, f32[32,16,256]{2,1,0:T(8,128)S(1)}, ...), condition=%wide.region_6.7_spmd.clone, body=%wide.region_4.6_spmd.clone.sunk | while | flops 524115968 | bytes 31068848 | solution.py:57
  64.3 1.7 fusion.85
  68.0 3.1 %fusion.86 = bf16[4,32,16,128]{3,2,1,0:T(8,128)(2,1)S(1)} fusion(bf16[4,32,16,128]{3,2,1,0:T(8,128)(2,1)S(1)} %copy-done.8, s32[]{:T(128)} %get-tuple-element.514, f32[32,16,128]{2,1,0:T(8,128)S(1)} %fusion.85, f32[32,256,128]{2,1,0:T(8,128)S(1)} %bitcast.195, f32[32,16,256]{2,1,0:T(8,128)S(1)} %get-tuple-element.515, f32[32]{0:T(128)} %get-tuple-element.533, ...), kind=kOutput, calls=%fused_computation.42.clone.1 | convolution fusion | flops 201654272 | bytes 5390468 | tf_op jit(solution)/shard_map/while/body/eval_jaxpr/hpn,hnt->hpt/dot_general | solution.py:46
  72.5 3.6 %convolution_add_fusion.2 = f32[32,16,256]{2,1,0:T(8,128)S(1)} fusion(f32[32,256,128]{2,1,0:T(8,128)S(1)} %bitcast.196, f32[32,16,256]{2,1,0:T(8,128)S(1)} %get-tuple-element.515, f32[32]{0:T(128)S(1)} %exp.74, f32[32,128]{1,0:T(8,128)S(1)} %get-tuple-element.484, bf16[4,32,16,128]{3,2,1,0:T(8,128)(2,1)S(1)} %get-tuple-element.530, ...), kind=kOutput, calls=%fused_computation.36.clone.1 | convolution fusion | flops 201719808 | bytes 5390852 | tf_op jit(solution)/shard_map/while/body/eval_jaxpr/hps,hns->hpn/dot_general | solution.py:52
  77.4 1.7 fusion.85
  81.0 3.1 %fusion.86 = bf16[4,32,16,128]{3,2,1,0:T(8,128)(2,1)S(1)} fusion(bf16[4,32,16,128]{3,2,1,0:T(8,128)(2,1)S(1)} %copy-done.8, s32[]{:T(128)} %get-tuple-element.514, f32[32,16,128]{2,1,0:T(8,128)S(1)} %fusion.85, f32[32,256,128]{2,1,0:T(8,128)S(1)} %bitcast.195, f32[32,16,256]{2,1,0:T(8,128)S(1)} %get-tuple-element.515, f32[32]{0:T(128)} %get-tuple-element.533, ...), kind=kOutput, calls=%fused_computation.42.clone.1 | convolution fusion | flops 201654272 | bytes 5390468 | tf_op jit(solution)/shard_map/while/body/eval_jaxpr/hpn,hnt->hpt/dot_general | solution.py:46
  85.5 3.6 %convolution_add_fusion.2 = f32[32,16,256]{2,1,0:T(8,128)S(1)} fusion(f32[32,256,128]{2,1,0:T(8,128)S(1)} %bitcast.196, f32[32,16,256]{2,1,0:T(8,128)S(1)} %get-tuple-element.515, f32[32]{0:T(128)S(1)} %exp.74, f32[32,128]{1,0:T(8,128)S(1)} %get-tuple-element.484, bf16[4,32,16,128]{3,2,1,0:T(8,128)(2,1)S(1)} %get-tuple-element.530, ...), kind=kOutput, calls=%fused_computation.36.clone.1 | convolution fusion | flops 201719808 | bytes 5390852 | tf_op jit(solution)/shard_map/while/body/eval_jaxpr/hps,hns->hpn/dot_general | solution.py:52
  90.4 1.7 fusion.85
  94.0 3.1 %fusion.86 = bf16[4,32,16,128]{3,2,1,0:T(8,128)(2,1)S(1)} fusion(bf16[4,32,16,128]{3,2,1,0:T(8,128)(2,1)S(1)} %copy-done.8, s32[]{:T(128)} %get-tuple-element.514, f32[32,16,128]{2,1,0:T(8,128)S(1)} %fusion.85, f32[32,256,128]{2,1,0:T(8,128)S(1)} %bitcast.195, f32[32,16,256]{2,1,0:T(8,128)S(1)} %get-tuple-element.515, f32[32]{0:T(128)} %get-tuple-element.533, ...), kind=kOutput, calls=%fused_computation.42.clone.1 | convolution fusion | flops 201654272 | bytes 5390468 | tf_op jit(solution)/shard_map/while/body/eval_jaxpr/hpn,hnt->hpt/dot_general | solution.py:46
  98.6 3.6 %convolution_add_fusion.2 = f32[32,16,256]{2,1,0:T(8,128)S(1)} fusion(f32[32,256,128]{2,1,0:T(8,128)S(1)} %bitcast.196, f32[32,16,256]{2,1,0:T(8,128)S(1)} %get-tuple-element.515, f32[32]{0:T(128)S(1)} %exp.74, f32[32,128]{1,0:T(8,128)S(1)} %get-tuple-element.484, bf16[4,32,16,128]{3,2,1,0:T(8,128)(2,1)S(1)} %get-tuple-element.530, ...), kind=kOutput, calls=%fused_computation.36.clone.1 | convolution fusion | flops 201719808 | bytes 5390852 | tf_op jit(solution)/shard_map/while/body/eval_jaxpr/hps,hns->hpn/dot_general | solution.py:52
  103.4 1.7 fusion.85
  107.1 3.1 %fusion.86 = bf16[4,32,16,128]{3,2,1,0:T(8,128)(2,1)S(1)} fusion(bf16[4,32,16,128]{3,2,1,0:T(8,128)(2,1)S(1)} %copy-done.8, s32[]{:T(128)} %get-tuple-element.514, f32[32,16,128]{2,1,0:T(8,128)S(1)} %fusion.85, f32[32,256,128]{2,1,0:T(8,128)S(1)} %bitcast.195, f32[32,16,256]{2,1,0:T(8,128)S(1)} %get-tuple-element.515, f32[32]{0:T(128)} %get-tuple-element.533, ...), kind=kOutput, calls=%fused_computation.42.clone.1 | convolution fusion | flops 201654272 | bytes 5390468 | tf_op jit(solution)/shard_map/while/body/eval_jaxpr/hpn,hnt->hpt/dot_general | solution.py:46
  111.6 3.6 %convolution_add_fusion.2 = f32[32,16,256]{2,1,0:T(8,128)S(1)} fusion(f32[32,256,128]{2,1,0:T(8,128)S(1)} %bitcast.196, f32[32,16,256]{2,1,0:T(8,128)S(1)} %get-tuple-element.515, f32[32]{0:T(128)S(1)} %exp.74, f32[32,128]{1,0:T(8,128)S(1)} %get-tuple-element.484, bf16[4,32,16,128]{3,2,1,0:T(8,128)(2,1)S(1)} %get-tuple-element.530, ...), kind=kOutput, calls=%fused_computation.36.clone.1 | convolution fusion | flops 201719808 | bytes 5390852 | tf_op jit(solution)/shard_map/while/body/eval_jaxpr/hps,hns->hpn/dot_general | solution.py:52
  115.2 1.6 copy.45
  117.1 1.5 select_convert_fusion.1
  118.7 94.4 %while.33 = (s32[]{:T(128)}, f32[128,2,8]{0,2,1:T(8,128)S(1)}, f32[128,2,8]{0,2,1:T(8,128)S(1)}, f32[128,2,8,128]{0,3,2,1:T(8,128)}, s32[4]{0:T(128)S(1)}, /*ind...) while((s32[]{:T(128)}, f32[128,2,8]{0,2,1:T(8,128)S(1)}, ...), condition=%wide.region_11.12_spmd.clone, body=%wide.region_8.11_spmd.clone.sunk | while | flops 1235016192 | bytes 47004440 | solution.py:167
  121.5 1.1 compare_select_fusion.7
  122.5 1.3 constant_dynamic-slice_fusion.10
  124.3 5.3 %fusion.90 = (f32[128,2,8]{0,2,1:T(8,128)S(1)}, f32[2,1152,128,8]{2,1,3,0:T(8,128)}) fusion(pred[128,1152]{0,1:T(8,128)(4,1)S(1)} %compare_select_fusion.7, bf16[1152,2,128,1]{0,2,3,1:T(8,128)(2,1)S(1)} %bitcast.199, bf16[128,2,8,128]{3,2,1,0:T(8,128)(2,1)S(1)} %bitcast.197), kind=kOutput, calls=%fused_computation.9.clone.1 | convolution fusion | flops 611055616 | bytes 10706944 | tf_op jit(solution)/shard_map/while/body/eval_jaxpr/rgqd,kgd->rgqk/dot_general | solution.py:123
  129.6 5.6 %fusion.91 = f32[128,2,8]{0,2,1:T(8,128)S(1)} fusion(f32[2,1152,128,8]{2,1,3,0:T(8,128)} %get-tuple-element.499, f32[128,2,8]{0,2,1:T(8,128)S(1)} %select_maximum_fusion.2, pred[128,1152]{0,1:T(8,128)(4,1)S(1)} %compare_select_fusion.7), kind=kLoop, calls=%fused_computation.13.clone.1 | loop fusion | flops 9435136 | bytes 9601024 | tf_op jit(solution)/shard_map/while/body/eval_jaxpr/reduce_sum | solution.py:130
  135.5 5.9 %fusion.93 = f32[128,2,8,128]{0,3,2,1:T(8,128)S(1)} fusion(bf16[1152,2,128,1]{0,2,3,1:T(8,128)(2,1)S(1)} %bitcast.200, f32[2,1152,128,8]{2,1,3,0:T(8,128)} %get-tuple-element.499, f32[128,2,8]{0,2,1:T(8,128)S(1)} %select_maximum_fusion.2, pred[128,1152]{0,1:T(8,128)(4,1)S(1)} %compare_select_fusion.7, f32[128,2,8,128]{0,3,2,1:T(8,128)S(1)} %copy-done.3, ...), kind=kOutput, calls=%fused_computation.17.clone.1 | convolution fusion | flops 614203392 | bytes 12288001 | tf_op jit(solution)/shard_map/while/body/eval_jaxpr/rgqk,kgd->rgqd/dot_general | solution.py:131
  141.5 1.0 copy-done.4
  145.0 1.1 compare_select_fusion.7
  146.1 1.3 constant_dynamic-slice_fusion.10
  147.8 5.3 %fusion.90 = (f32[128,2,8]{0,2,1:T(8,128)S(1)}, f32[2,1152,128,8]{2,1,3,0:T(8,128)}) fusion(pred[128,1152]{0,1:T(8,128)(4,1)S(1)} %compare_select_fusion.7, bf16[1152,2,128,1]{0,2,3,1:T(8,128)(2,1)S(1)} %bitcast.199, bf16[128,2,8,128]{3,2,1,0:T(8,128)(2,1)S(1)} %bitcast.197), kind=kOutput, calls=%fused_computation.9.clone.1 | convolution fusion | flops 611055616 | bytes 10706944 | tf_op jit(solution)/shard_map/while/body/eval_jaxpr/rgqd,kgd->rgqk/dot_general | solution.py:123
  153.1 5.6 %fusion.91 = f32[128,2,8]{0,2,1:T(8,128)S(1)} fusion(f32[2,1152,128,8]{2,1,3,0:T(8,128)} %get-tuple-element.499, f32[128,2,8]{0,2,1:T(8,128)S(1)} %select_maximum_fusion.2, pred[128,1152]{0,1:T(8,128)(4,1)S(1)} %compare_select_fusion.7), kind=kLoop, calls=%fused_computation.13.clone.1 | loop fusion | flops 9435136 | bytes 9601024 | tf_op jit(solution)/shard_map/while/body/eval_jaxpr/reduce_sum | solution.py:130
  159.1 5.9 %fusion.93 = f32[128,2,8,128]{0,3,2,1:T(8,128)S(1)} fusion(bf16[1152,2,128,1]{0,2,3,1:T(8,128)(2,1)S(1)} %bitcast.200, f32[2,1152,128,8]{2,1,3,0:T(8,128)} %get-tuple-element.499, f32[128,2,8]{0,2,1:T(8,128)S(1)} %select_maximum_fusion.2, pred[128,1152]{0,1:T(8,128)(4,1)S(1)} %compare_select_fusion.7, f32[128,2,8,128]{0,3,2,1:T(8,128)S(1)} %copy-done.3, ...), kind=kOutput, calls=%fused_computation.17.clone.1 | convolution fusion | flops 614203392 | bytes 12288001 | tf_op jit(solution)/shard_map/while/body/eval_jaxpr/rgqk,kgd->rgqd/dot_general | solution.py:131
  168.5 1.1 compare_select_fusion.7
  169.6 1.3 constant_dynamic-slice_fusion.10
  171.4 5.3 %fusion.90 = (f32[128,2,8]{0,2,1:T(8,128)S(1)}, f32[2,1152,128,8]{2,1,3,0:T(8,128)}) fusion(pred[128,1152]{0,1:T(8,128)(4,1)S(1)} %compare_select_fusion.7, bf16[1152,2,128,1]{0,2,3,1:T(8,128)(2,1)S(1)} %bitcast.199, bf16[128,2,8,128]{3,2,1,0:T(8,128)(2,1)S(1)} %bitcast.197), kind=kOutput, calls=%fused_computation.9.clone.1 | convolution fusion | flops 611055616 | bytes 10706944 | tf_op jit(solution)/shard_map/while/body/eval_jaxpr/rgqd,kgd->rgqk/dot_general | solution.py:123
  176.6 5.6 %fusion.91 = f32[128,2,8]{0,2,1:T(8,128)S(1)} fusion(f32[2,1152,128,8]{2,1,3,0:T(8,128)} %get-tuple-element.499, f32[128,2,8]{0,2,1:T(8,128)S(1)} %select_maximum_fusion.2, pred[128,1152]{0,1:T(8,128)(4,1)S(1)} %compare_select_fusion.7), kind=kLoop, calls=%fused_computation.13.clone.1 | loop fusion | flops 9435136 | bytes 9601024 | tf_op jit(solution)/shard_map/while/body/eval_jaxpr/reduce_sum | solution.py:130
  182.6 5.9 %fusion.93 = f32[128,2,8,128]{0,3,2,1:T(8,128)S(1)} fusion(bf16[1152,2,128,1]{0,2,3,1:T(8,128)(2,1)S(1)} %bitcast.200, f32[2,1152,128,8]{2,1,3,0:T(8,128)} %get-tuple-element.499, f32[128,2,8]{0,2,1:T(8,128)S(1)} %select_maximum_fusion.2, pred[128,1152]{0,1:T(8,128)(4,1)S(1)} %compare_select_fusion.7, f32[128,2,8,128]{0,3,2,1:T(8,128)S(1)} %copy-done.3, ...), kind=kOutput, calls=%fused_computation.17.clone.1 | convolution fusion | flops 614203392 | bytes 12288001 | tf_op jit(solution)/shard_map/while/body/eval_jaxpr/rgqk,kgd->rgqd/dot_general | solution.py:131
  192.1 1.1 compare_select_fusion.7
  193.1 1.3 constant_dynamic-slice_fusion.10
  194.9 5.3 %fusion.90 = (f32[128,2,8]{0,2,1:T(8,128)S(1)}, f32[2,1152,128,8]{2,1,3,0:T(8,128)}) fusion(pred[128,1152]{0,1:T(8,128)(4,1)S(1)} %compare_select_fusion.7, bf16[1152,2,128,1]{0,2,3,1:T(8,128)(2,1)S(1)} %bitcast.199, bf16[128,2,8,128]{3,2,1,0:T(8,128)(2,1)S(1)} %bitcast.197), kind=kOutput, calls=%fused_computation.9.clone.1 | convolution fusion | flops 611055616 | bytes 10706944 | tf_op jit(solution)/shard_map/while/body/eval_jaxpr/rgqd,kgd->rgqk/dot_general | solution.py:123
  200.1 5.6 %fusion.91 = f32[128,2,8]{0,2,1:T(8,128)S(1)} fusion(f32[2,1152,128,8]{2,1,3,0:T(8,128)} %get-tuple-element.499, f32[128,2,8]{0,2,1:T(8,128)S(1)} %select_maximum_fusion.2, pred[128,1152]{0,1:T(8,128)(4,1)S(1)} %compare_select_fusion.7), kind=kLoop, calls=%fused_computation.13.clone.1 | loop fusion | flops 9435136 | bytes 9601024 | tf_op jit(solution)/shard_map/while/body/eval_jaxpr/reduce_sum | solution.py:130
  206.1 5.9 %fusion.93 = f32[128,2,8,128]{0,3,2,1:T(8,128)S(1)} fusion(bf16[1152,2,128,1]{0,2,3,1:T(8,128)(2,1)S(1)} %bitcast.200, f32[2,1152,128,8]{2,1,3,0:T(8,128)} %get-tuple-element.499, f32[128,2,8]{0,2,1:T(8,128)S(1)} %select_maximum_fusion.2, pred[128,1152]{0,1:T(8,128)(4,1)S(1)} %compare_select_fusion.7, f32[128,2,8,128]{0,3,2,1:T(8,128)S(1)} %copy-done.3, ...), kind=kOutput, calls=%fused_computation.17.clone.1 | convolution fusion | flops 614203392 | bytes 12288001 | tf_op jit(solution)/shard_map/while/body/eval_jaxpr/rgqk,kgd->rgqd/dot_general | solution.py:131
  213.0 1.3 broadcast_divide_fusion
  (225 shorter events, 36.8 us)
Async XLA Ops:
  7.2 14.6 %copy-start.2 = (bf16[1,32,2,32,256]{4,3,2,1,0:T(8,128)(2,1)S(1)}, bf16[1,32,2,32,256]{4,3,2,1,0:T(8,128)(2,1)}, u32[]{:S(2)}) copy-start(bf16[1,32,2,32,256]{4,3,2,1,0:T(8,128)(2,1)} %param.18) | copy-start | bytes 3145732
  14.6 13.0 %all-to-all-start = ((bf16[2,32,16,256]{3,2,1,0:T(8,128)(2,1)}), bf16[2,32,16,256]{3,2,1,0:T(8,128)(2,1)S(1)}, u32[]{:S(2)}, u32[]{:S(2)}) async-start(bf16[2,32,16,256]{3,2,1,0:T(8,128)(2,1)} %scatter_fusion), calls=%async_computation | async-start | bytes 1048576 | tf_op jit(solution)/shard_map/all_to_all | solution.py:90
  21.7 10.8 %copy-start.11 = (f32[1,32,512]{2,1,0:T(8,128)S(1)}, f32[1,32,512]{2,1,0:T(8,128)}, u32[]{:S(2)}) copy-start(f32[1,32,512]{2,1,0:T(8,128)} %param.27) | copy-start | bytes 196612
  21.7 10.9 %copy-start.5 = (bf16[1,32,16,512]{3,2,1,0:T(8,128)(2,1)S(1)}, bf16[1,32,16,512]{3,2,1,0:T(8,128)(2,1)}, u32[]{:S(2)}) copy-start(bf16[1,32,16,512]{3,2,1,0:T(8,128)(2,1)} %param.24) | copy-start | bytes 1572868
  21.7 11.1 %copy-start.6 = (bf16[1,2,256,512]{3,2,1,0:T(8,128)(2,1)S(1)}, bf16[1,2,256,512]{3,2,1,0:T(8,128)(2,1)}, u32[]{:S(2)}) copy-start(bf16[1,2,256,512]{3,2,1,0:T(8,128)(2,1)} %param.25) | copy-start | bytes 1572868
  26.7 6.4 %copy-start.7 = (bf16[1,2,256,512]{3,2,1,0:T(8,128)(2,1)S(1)}, bf16[1,2,256,512]{3,2,1,0:T(8,128)(2,1)}, u32[]{:S(2)}) copy-start(bf16[1,2,256,512]{3,2,1,0:T(8,128)(2,1)} %param.26) | copy-start | bytes 1572868
  26.8 8.5 %copy-start.17 = (f32[32]{0:T(128)S(1)}, f32[32]{0:T(128)}, u32[]{:S(2)}) copy-start(f32[32]{0:T(128)} %param.28) | copy-start | bytes 388
  27.6 29.9 %all-to-all-start.1 = ((bf16[2,32,2,32,256]{4,3,2,1,0:T(8,128)(2,1)}), bf16[2,32,2,32,256]{4,3,2,1,0:T(8,128)(2,1)}, u32[]{:S(2)}, u32[]{:S(2)}) async-start(bf16[2,32,2,32,256]{4,3,2,1,0:T(8,128)(2,1)} %scatter_fusion.1), calls=%async_computation.1 | async-start | bytes 4194304 | tf_op jit(solution)/shard_map/all_to_all | solution.py:89
  32.4 86.3 %all-gather.2.cloned.1.call-start = ((), (), s32[]{:S(2)}) async-start(), calls=%async_computation.2 | async-start | bytes 5898240 | tf_op jit(solution)/shard_map/all_gather | solution.py:156
  32.7 29.2 %copy-start.10 = (bf16[1,2,128,256]{3,2,1,0:T(8,128)(2,1)S(1)}, bf16[1,2,128,256]{3,2,1,0:T(8,128)(2,1)}, u32[]{:S(2)}) copy-start(bf16[1,2,128,256]{3,2,1,0:T(8,128)(2,1)} %param.31) | copy-start | bytes 393220
  63.1 55.6 %copy-start.1 = (bf16[1,128,2048]{2,1,0:T(8,128)(2,1)S(1)}, bf16[1,128,2048]{2,1,0:T(8,128)(2,1)}, u32[]{:S(2)}) copy-start(bf16[1,128,2048]{2,1,0:T(8,128)(2,1)} %param.30) | copy-start | bytes 1572868
  63.1 3.3 %copy-start.14 = (f32[32,1]{0,1:T(1,128)}, f32[32,1]{0,1:T(1,128)S(1)}, u32[]{:S(2)}) copy-start(f32[32,1]{0,1:T(1,128)S(1)} %get-tuple-element.528) | copy-start | bytes 388 | tf_op jit(solution)/shard_map/while
  66.2 0.5 copy-start.12
  66.9 1.0 copy-start.8
  66.9 4.1 %copy-start.13 = (f32[32]{0:T(128)S(1)}, f32[32]{0:T(128)}, u32[]{:S(2)}) copy-start(f32[32]{0:T(128)} %copy-done.12) | copy-start | bytes 388 | tf_op jit(solution)/shard_map/while
  71.0 0.8 copy-start.9
  72.0 4.1 %copy-start.15 = (f32[32,1]{0,1:T(1,128)S(1)}, f32[32,1]{0,1:T(1,128)}, u32[]{:S(2)}) copy-start(f32[32,1]{0,1:T(1,128)} %copy-done.14) | copy-start | bytes 388 | tf_op jit(solution)/shard_map/while
  76.1 3.3 %copy-start.14 = (f32[32,1]{0,1:T(1,128)}, f32[32,1]{0,1:T(1,128)S(1)}, u32[]{:S(2)}) copy-start(f32[32,1]{0,1:T(1,128)S(1)} %get-tuple-element.528) | copy-start | bytes 388 | tf_op jit(solution)/shard_map/while
  79.3 0.5 copy-start.12
  80.0 1.0 copy-start.8
  80.0 4.1 %copy-start.13 = (f32[32]{0:T(128)S(1)}, f32[32]{0:T(128)}, u32[]{:S(2)}) copy-start(f32[32]{0:T(128)} %copy-done.12) | copy-start | bytes 388 | tf_op jit(solution)/shard_map/while
  84.1 0.8 copy-start.9
  85.0 4.1 %copy-start.15 = (f32[32,1]{0,1:T(1,128)S(1)}, f32[32,1]{0,1:T(1,128)}, u32[]{:S(2)}) copy-start(f32[32,1]{0,1:T(1,128)} %copy-done.14) | copy-start | bytes 388 | tf_op jit(solution)/shard_map/while
  89.2 3.3 %copy-start.14 = (f32[32,1]{0,1:T(1,128)}, f32[32,1]{0,1:T(1,128)S(1)}, u32[]{:S(2)}) copy-start(f32[32,1]{0,1:T(1,128)S(1)} %get-tuple-element.528) | copy-start | bytes 388 | tf_op jit(solution)/shard_map/while
  92.3 0.5 copy-start.12
  93.0 1.0 copy-start.8
  93.0 4.1 %copy-start.13 = (f32[32]{0:T(128)S(1)}, f32[32]{0:T(128)}, u32[]{:S(2)}) copy-start(f32[32]{0:T(128)} %copy-done.12) | copy-start | bytes 388 | tf_op jit(solution)/shard_map/while
  97.1 0.8 copy-start.9
  98.1 4.1 %copy-start.15 = (f32[32,1]{0,1:T(1,128)S(1)}, f32[32,1]{0,1:T(1,128)}, u32[]{:S(2)}) copy-start(f32[32,1]{0,1:T(1,128)} %copy-done.14) | copy-start | bytes 388 | tf_op jit(solution)/shard_map/while
  102.2 3.3 %copy-start.14 = (f32[32,1]{0,1:T(1,128)}, f32[32,1]{0,1:T(1,128)S(1)}, u32[]{:S(2)}) copy-start(f32[32,1]{0,1:T(1,128)S(1)} %get-tuple-element.528) | copy-start | bytes 388 | tf_op jit(solution)/shard_map/while
  105.4 0.5 copy-start.12
  106.0 1.0 copy-start.8
  106.0 4.1 %copy-start.13 = (f32[32]{0:T(128)S(1)}, f32[32]{0:T(128)}, u32[]{:S(2)}) copy-start(f32[32]{0:T(128)} %copy-done.12) | copy-start | bytes 388 | tf_op jit(solution)/shard_map/while
  110.2 0.8 copy-start.9
  111.1 4.1 %copy-start.15 = (f32[32,1]{0,1:T(1,128)S(1)}, f32[32,1]{0,1:T(1,128)}, u32[]{:S(2)}) copy-start(f32[32,1]{0,1:T(1,128)} %copy-done.14) | copy-start | bytes 388 | tf_op jit(solution)/shard_map/while
  115.2 3.4 %copy-start = (f32[32,16,256]{2,1,0:T(8,128)}, f32[32,16,256]{2,1,0:T(8,128)S(1)}, u32[]{:S(2)}) copy-start(f32[32,16,256]{2,1,0:T(8,128)S(1)} %get-tuple-element.235) | copy-start | bytes 1572868
  118.7 95.9 %copy-start.16 = (pred[128]{0:T(512)(128)(4,1)S(1)}, pred[128]{0:T(512)(128)(4,1)}, u32[]{:S(2)}) copy-start(pred[128]{0:T(512)(128)(4,1)} %add_compare_fusion.1) | copy-start | bytes 388
  129.6 6.0 %copy-start.3 = (f32[128,2,8,128]{0,3,2,1:T(8,128)S(1)}, f32[128,2,8,128]{0,3,2,1:T(8,128)}, u32[]{:S(2)}) copy-start(f32[128,2,8,128]{0,3,2,1:T(8,128)} %get-tuple-element.553) | copy-start | bytes 3145732 | tf_op jit(solution)/shard_map/while
  141.5 1.0 copy-start.4
  153.1 6.0 %copy-start.3 = (f32[128,2,8,128]{0,3,2,1:T(8,128)S(1)}, f32[128,2,8,128]{0,3,2,1:T(8,128)}, u32[]{:S(2)}) copy-start(f32[128,2,8,128]{0,3,2,1:T(8,128)} %get-tuple-element.553) | copy-start | bytes 3145732 | tf_op jit(solution)/shard_map/while
  165.0 1.0 copy-start.4
  176.6 6.0 %copy-start.3 = (f32[128,2,8,128]{0,3,2,1:T(8,128)S(1)}, f32[128,2,8,128]{0,3,2,1:T(8,128)}, u32[]{:S(2)}) copy-start(f32[128,2,8,128]{0,3,2,1:T(8,128)} %get-tuple-element.553) | copy-start | bytes 3145732 | tf_op jit(solution)/shard_map/while
  188.5 1.0 copy-start.4
  200.1 6.0 %copy-start.3 = (f32[128,2,8,128]{0,3,2,1:T(8,128)S(1)}, f32[128,2,8,128]{0,3,2,1:T(8,128)}, u32[]{:S(2)}) copy-start(f32[128,2,8,128]{0,3,2,1:T(8,128)} %get-tuple-element.553) | copy-start | bytes 3145732 | tf_op jit(solution)/shard_map/while
  212.0 1.0 copy-start.4
Sparse Core Ops, SparseCore 0:
  63.2 37.9 all-gather.1
where the time goes:
time: 224 us; the launch traced here: 222 us
  matrix products  79.1 us (35%)
  local copies, waits for them, and re-layouts  48 us (21%)
  other arithmetic  42.5 us (19%)
  waiting for transfers between devices  22.3 us (10%)
  between operations  14.9 us (7%)
  starting transfers between devices  9.08 us (4%)
  loops' own time  6.43 us (3%)
    dot_general x4, matrix products, attend_block(): jnp.einsum('rgqk,kgd->rgqd', weights.astype(jnp.bfloat16), value_heads, p...  23.7 us
    reduce_sum x4, other arithmetic, attend_block(): totals = fade * totals + jnp.sum(weights, axis=-1)  22.6 us
    all_to_all x1, waiting for transfers between devices, route_blocks(): lax.all_to_all(send_kv, 'pool', split_axis=0, concat_axis=0, tiled=True)  21.5 us
    dot_general x4, matrix products, attend_block(): jnp.einsum('rgqd,kgd->rgqk', query_heads, key_heads, preferred_element_ty...  21 us
    dot_general x4, matrix products, advance(): jnp.einsum('hps,hns->hpn', value_blk * weights[:, None, :], write_in, pre...  14.5 us
    while x80, local copies, waits for them, and re-layouts  13.7 us
    dot_general x4, matrix products, advance(): jnp.einsum('hpn,hnt->hpt', carried, read_out, precision=exact)  12.3 us
    dot_general x4, matrix products, advance(): result = jnp.einsum('hts,hps->hpt', mixing, value_blk, precision=exact)  6.92 us
  transfers between devices with their start and end apart: 3, of which 2 were waited for; matrix products, arithmetic and copies ran while one was open for 26% of the time, Pallas kernels for 0%

commit v1 on v0

v1 whole, which is shorter than its diff:
```python
import functools

import jax
import jax.numpy as jnp
from jax import lax
from jax.experimental import pallas as pl
from jax.experimental.pallas import tpu as pltpu
from jax.sharding import PartitionSpec as P

Q_HEADS = 64
KV_HEADS = 8
HEAD_DIM = 128
PER_GROUP = Q_HEADS // KV_HEADS
BLK = 128
HIDDEN = -1e30
TO_POWER = (HEAD_DIM**-0.5) * 1.4426950408889634
STAT_ROWS = 32
VMEM_BYTES = 56 * 2**20

whole = pl.BlockSpec(memory_space=pltpu.VMEM)
scalar = pl.BlockSpec(memory_space=pltpu.SMEM)
outside = pl.BlockSpec(memory_space=pl.ANY)


def params():
    return pltpu.CompilerParams(vmem_limit_bytes=VMEM_BYTES)


def mixer_kernel(valid_ref, x_ref, b_ref, c_ref, dt_ref, rate_ref, gain_ref, y_ref, s_ref, run_ref):
    heads, chans, total = x_ref.shape
    states = b_ref.shape[1]
    rows = heads * chans
    place = lax.broadcasted_iota(jnp.int32, (heads, total), 1)
    steps = jnp.where(place < valid_ref[0], dt_ref[...], 0.0)
    falls = -rate_ref[...] * steps
    gains = gain_ref[...]
    first = lax.broadcasted_iota(jnp.int32, (BLK, BLK), 0)
    second = lax.broadcasted_iota(jnp.int32, (BLK, BLK), 1)
    upper = first <= second
    ones_upper = jnp.where(upper, 1.0, 0.0).astype(jnp.float32)
    turned = b_ref[0].T
    state = jnp.zeros((rows, states), jnp.float32)
    base = jnp.zeros((heads, 1), jnp.float32)
    for blk in range(total // BLK):
        span = slice(blk * BLK, (blk + 1) * BLK)
        run = jnp.dot(
            falls[:, span],
            ones_upper,
            precision=lax.Precision.HIGHEST,
            preferred_element_type=jnp.float32,
        )
        run_col = run.T
        last = run[:, BLK - 1 :]
        pairs = jnp.dot(turned[span], c_ref[0, :, span], preferred_element_type=jnp.float32)
        pairs = jnp.where(upper, pairs, 0.0)
        x_blk = x_ref[:, :, span].astype(jnp.float32)
        stepped = (x_blk * steps[:, None, span]).astype(jnp.bfloat16)
        inside = []
        for head in range(heads):
            gap = jnp.minimum(run[head : head + 1, :] - run_col[:, head : head + 1], 0.0)
            mixing = (jnp.exp(gap) * pairs).astype(jnp.bfloat16)
            inside.append(jnp.dot(stepped[head], mixing, preferred_element_type=jnp.float32))
        result = jnp.stack(inside) + gains[:, :, None] * x_blk
        if blk:
            read = jnp.dot(
                state.astype(jnp.bfloat16), c_ref[0, :, span], preferred_element_type=jnp.float32
            )
            result = result + jnp.exp(run)[:, None, :] * read.reshape(heads, chans, BLK)
        y_ref[:, :, span] = result
        weights = jnp.exp(last - run) * steps[:, span]
        weighted = (x_blk * weights[:, None, :]).astype(jnp.bfloat16).reshape(rows, BLK)
        added = jnp.dot(weighted, turned[span], preferred_element_type=jnp.float32)
        kept = jnp.broadcast_to(jnp.exp(last)[:, :, None], (heads, chans, 1)).reshape(rows, 1)
        state = kept * state + added
        run_ref[:, span] = base + run
        base = base + last
    s_ref[...] = state.reshape(heads, chans, states)


def mixer_from_zero(x, b, c, dt, rates, gains, valid):
    heads, chans, total = x.shape
    groups, states, _ = b.shape
    per = heads // groups
    return pl.pallas_call(
        mixer_kernel,
        grid=(groups,),
        in_specs=[
            scalar,
            pl.BlockSpec((per, chans, total), lambda g: (g, 0, 0)),
            pl.BlockSpec((1, states, total), lambda g: (g, 0, 0)),
            pl.BlockSpec((1, states, total), lambda g: (g, 0, 0)),
            pl.BlockSpec((per, total), lambda g: (g, 0)),
            pl.BlockSpec((per, 1), lambda g: (g, 0)),
            pl.BlockSpec((per, 1), lambda g: (g, 0)),
        ],
        out_specs=[
            pl.BlockSpec((per, chans, total), lambda g: (g, 0, 0)),
            pl.BlockSpec((per, chans, states), lambda g: (g, 0, 0)),
            pl.BlockSpec((per, total), lambda g: (g, 0)),
        ],
        out_shape=[
            jax.ShapeDtypeStruct((heads, chans, total), jnp.float32),
            jax.ShapeDtypeStruct((heads, chans, states), jnp.float32),
            jax.ShapeDtypeStruct((heads, total), jnp.float32),
        ],
        compiler_params=params(),
        cost_estimate=pl.CostEstimate(
            flops=10**9, bytes_accessed=6 * 2**20, transcendentals=heads * total * BLK
        ),
        name="mixer_from_zero",
    )(valid, x, b, c, dt, rates[:, None], gains[:, None])


def saved_kernel(kinds, info_ref, *refs):
    slabs = refs[:kinds]
    y_ref, s_ref, run_ref, c_ref, out_ref, final_ref, start = refs[kinds:]
    heads, chans, total = y_ref.shape
    groups, states, _ = c_ref.shape
    per = heads // groups
    for kind in range(kinds):

        @pl.when(info_ref[0] == kind)
        def _():
            for slot in range(heads):
                start[info_ref[2 + slot]] = slabs[kind][slot]

    live = lax.broadcasted_iota(jnp.int32, (1, 1, total), 2) < info_ref[1]
    for group in range(groups):
        mine = slice(group * per, (group + 1) * per)
        saved = start[mine]
        fade = jnp.exp(run_ref[mine, :])
        read = jnp.dot(
            saved.reshape(per * chans, states), c_ref[group], preferred_element_type=jnp.float32
        ).reshape(per, chans, total)
        result = y_ref[mine] + fade[:, None, :] * read
        out_ref[mine] = jnp.where(live, result, 0.0).astype(jnp.bfloat16)
        kept = fade[:, None, total - 1 :]
        final_ref[mine] = s_ref[mine] + kept * saved.astype(jnp.float32)


def add_saved(slabs, kind, order, y, s, run, c, valid):
    heads, chans, total = y.shape
    states = c.shape[1]
    info = jnp.concatenate([kind[None], valid, order]).astype(jnp.int32)
    return pl.pallas_call(
        functools.partial(saved_kernel, len(slabs)),
        in_specs=[scalar] + [whole] * (len(slabs) + 4),
        out_specs=[whole, whole],
        out_shape=[
            jax.ShapeDtypeStruct((heads, chans, total), jnp.bfloat16),
            jax.ShapeDtypeStruct((heads, chans, states), jnp.float32),
        ],
        scratch_shapes=[pltpu.VMEM((heads, chans, states), jnp.bfloat16)],
        compiler_params=params(),
        cost_estimate=pl.CostEstimate(
            flops=10**8, bytes_accessed=5 * 2**20, transcendentals=heads * total
        ),
        name="add_saved",
    )(info, *slabs, y, s, run, c)


def attend_kernel(kinds, head, info_ref, *refs):
    q_refs = refs[:2]
    kv_refs = (refs[2 : 2 + kinds], refs[2 + kinds : 2 + 2 * kinds])
    turn_refs = refs[2 + 2 * kinds : 4 + 2 * kinds]
    o_ref, l_ref, sent_ref, queries, keys, turn_keys, turn_raw, values, sems = refs[
        4 + 2 * kinds :
    ]
    pages, page = kv_refs[0][0].shape[0], kv_refs[0][0].shape[2]
    rows = q_refs[0].shape[0]
    history = pages * page
    width = PER_GROUP * HEAD_DIM
    columns = pl.ds(head * HEAD_DIM, HEAD_DIM)
    copies = []
    for side in range(2):
        copies.append(
            pltpu.make_async_copy(
                q_refs[side].at[:, pl.ds(head * width, width)], queries.at[side], sems.at[side]
            )
        )
        copies.append(
            pltpu.make_async_copy(
                turn_refs[side].at[:, :, columns], turn_raw.at[side], sems.at[2 + side]
            )
        )
    for copy in copies:
        copy.start()
    slot = [2 + side * (2 + pages) for side in range(2)]
    base = [1 + side * (2 + pages) for side in range(2)]
    for side in range(2):
        for kind in range(kinds):

            @pl.when(info_ref[base[side] + 1] == kind)
            def _():
                pltpu.make_async_copy(
                    kv_refs[side][kind].at[:, 0],
                    keys.at[pl.ds(side * pages, pages), :, pl.ds(0, HEAD_DIM)],
                    sems.at[4 + side],
                ).start()
                pltpu.make_async_copy(
                    kv_refs[side][kind].at[:, 1],
                    values.at[pl.ds(side * pages, pages), :, pl.ds(0, HEAD_DIM)],
                    sems.at[6 + side],
                ).start()

    in_page = lax.broadcasted_iota(jnp.int32, (page, HEAD_DIM), 0)
    seen = info_ref[0]
    for side in range(2):
        start = info_ref[base[side]] * history
        for number in range(pages):
            left = seen - start - info_ref[base[side] + 2 + number] * page
            keys[side * pages + number, :, HEAD_DIM:] = jnp.where(
                in_page < left, 0.0, HIDDEN
            ).astype(jnp.bfloat16)
    values[:, :, HEAD_DIM:] = jnp.ones(
        (values.shape[0], page, HEAD_DIM), jnp.bfloat16
    )
    first = lax.broadcasted_iota(jnp.int32, (rows, rows), 0)
    second = lax.broadcasted_iota(jnp.int32, (rows, rows), 1)
    eye = jnp.where(first == second, 1.0, 0.0).astype(jnp.bfloat16)
    asking = (info_ref[base[0]], info_ref[base[0]] ^ 2)
    for asked in range(2):
        for side in range(2):
            ahead = first + info_ref[base[side]] * rows
            turn_keys[asked, pl.ds(side * rows, rows), HEAD_DIM:] = jnp.where(
                ahead <= second + asking[asked] * rows, 0.0, HIDDEN
            ).astype(jnp.bfloat16)
    for copy in copies:
        copy.wait()
    turn_pages = rows // page
    for side in range(2):
        for asked in range(2):
            turn_keys[asked, pl.ds(side * rows, rows), pl.ds(0, HEAD_DIM)] = turn_raw[side, 0]
        values[
            pl.ds(2 * pages + side * turn_pages, turn_pages), :, pl.ds(0, HEAD_DIM)
        ] = turn_raw[side, 1].reshape(turn_pages, page, HEAD_DIM)
    for side in range(2):
        pltpu.make_async_copy(
            kv_refs[side][0].at[:, 0],
            keys.at[pl.ds(side * pages, pages), :, pl.ds(0, HEAD_DIM)],
            sems.at[4 + side],
        ).wait()
        pltpu.make_async_copy(
            kv_refs[side][0].at[:, 1],
            values.at[pl.ds(side * pages, pages), :, pl.ds(0, HEAD_DIM)],
            sems.at[6 + side],
        ).wait()
    depth = 2 * HEAD_DIM
    all_keys = 2 * history
    lane = lax.broadcasted_iota(jnp.int32, (rows, HEAD_DIM), 1)
    across = (((1,), (1,)), ((), ()))
    at_once = 2
    for asked in (1, 0):
        stats = jnp.zeros((rows, HEAD_DIM), jnp.float32)
        for batch in range(PER_GROUP // at_once):
            asks = jnp.concatenate(
                [
                    jnp.concatenate(
                        [
                            queries[asked, :, pl.ds((batch * at_once + i) * HEAD_DIM, HEAD_DIM)],
                            eye,
                        ],
                        axis=1,
                    )
                    for i in range(at_once)
                ],
                axis=0,
            )
            scores = jnp.concatenate(
                [
                    lax.dot_general(
                        asks,
                        keys[...].reshape(all_keys, depth),
                        across,
                        preferred_element_type=jnp.float32,
                    ),
                    lax.dot_general(
                        asks, turn_keys[asked], across, preferred_element_type=jnp.float32
                    ),
                ],
                axis=1,
            )
            peak = jnp.max(scores, axis=1, keepdims=True)
            weights = jnp.exp2((scores - peak) * TO_POWER).astype(jnp.bfloat16)
            summed = jnp.dot(
                weights,
                values[...].reshape(all_keys + 2 * rows, depth),
                preferred_element_type=jnp.float32,
            )
            totals = summed[:, HEAD_DIM:]
            mixed = (summed[:, :HEAD_DIM] / totals).astype(jnp.bfloat16)
            level = peak * TO_POWER + jnp.log2(totals)
            span = pl.ds(batch * at_once * rows, at_once * rows)
            if asked:
                sent_ref[span] = mixed
            else:
                o_ref[span] = mixed
            for i in range(at_once):
                stats = jnp.where(
                    lane == batch * at_once + i, level[i * rows : (i + 1) * rows], stats
                )
        stats = stats.T[:PER_GROUP]
        if asked:
            high = stats.astype(jnp.bfloat16).astype(jnp.float32)
            middle = (stats - high).astype(jnp.bfloat16).astype(jnp.float32)
            low = stats - high - middle
            sent_ref[pl.ds(PER_GROUP * rows, STAT_ROWS)] = jnp.concatenate(
                [high, middle, low, jnp.zeros_like(low)], axis=0
            ).astype(jnp.bfloat16)
        else:
            l_ref[...] = stats


def attend(head, info, queries, own_kv, partner_kv, turns):
    rows = queries[0].shape[0]
    pages, _, page, _ = own_kv[0].shape
    kinds = len(own_kv)
    all_rows = PER_GROUP * rows
    return pl.pallas_call(
        functools.partial(attend_kernel, kinds, head),
        in_specs=[scalar] + [outside] * (4 + 2 * kinds),
        out_specs=[whole] * 3,
        out_shape=[
            jax.ShapeDtypeStruct((all_rows, HEAD_DIM), jnp.bfloat16),
            jax.ShapeDtypeStruct((PER_GROUP, rows), jnp.float32),
            jax.ShapeDtypeStruct((all_rows + STAT_ROWS, HEAD_DIM), jnp.bfloat16),
        ],
        scratch_shapes=[
            pltpu.VMEM((2, rows, PER_GROUP * HEAD_DIM), jnp.bfloat16),
            pltpu.VMEM((2 * pages, page, 2 * HEAD_DIM), jnp.bfloat16),
            pltpu.VMEM((2, 2 * rows, 2 * HEAD_DIM), jnp.bfloat16),
            pltpu.VMEM((2, 2, rows, HEAD_DIM), jnp.bfloat16),
            pltpu.VMEM((2 * pages + 2 * rows // page, page, 2 * HEAD_DIM), jnp.bfloat16),
            pltpu.SemaphoreType.DMA((8,)),
        ],
        compiler_params=params(),
        cost_estimate=pl.CostEstimate(
            flops=8 * all_rows * 2 * pages * page * HEAD_DIM,
            bytes_accessed=3 * 2**20,
            transcendentals=4 * all_rows * pages * page,
        ),
        name=f"attend_{head}",
    )(info, *queries, *own_kv, *partner_kv, *turns)


def merge_kernel(heads, info_ref, *refs):
    out_ref = refs[-1]
    rows = out_ref.shape[0]
    live = lax.broadcasted_iota(jnp.int32, (rows, HEAD_DIM), 0) < info_ref[0]
    for head in range(heads):
        o_ref, l_ref, got_ref = refs[3 * head : 3 * head + 3]
        parts = got_ref[pl.ds(PER_GROUP * rows, STAT_ROWS)].astype(jnp.float32)
        level = parts[:PER_GROUP] + parts[PER_GROUP : 2 * PER_GROUP]
        level = level + parts[2 * PER_GROUP : 3 * PER_GROUP]
        share = 1.0 / (1.0 + jnp.exp2(level - l_ref[...]))
        share = jnp.concatenate(
            [share, jnp.zeros((rows - PER_GROUP, rows), jnp.float32)], axis=0
        ).T
        for member in range(PER_GROUP):
            span = pl.ds(member * rows, rows)
            here = o_ref[span].astype(jnp.float32)
            there = got_ref[span].astype(jnp.float32)
            result = there + share[:, member : member + 1] * (here - there)
            out_ref[:, pl.ds((head * PER_GROUP + member) * HEAD_DIM, HEAD_DIM)] = jnp.where(
                live, result, 0.0
            ).astype(jnp.bfloat16)


def merge(parts, live, rows):
    heads = len(parts)
    flat = [array for part in parts for array in part]
    return pl.pallas_call(
        functools.partial(merge_kernel, heads),
        in_specs=[scalar] + [whole] * len(flat),
        out_specs=whole,
        out_shape=jax.ShapeDtypeStruct((rows, heads * PER_GROUP * HEAD_DIM), jnp.bfloat16),
        compiler_params=params(),
        name="merge",
    )(live, *flat)


def route_blocks(kv_local, state_local, owner_row, index_row):
    parties = lax.axis_size("pool")
    myself = lax.axis_index("pool")
    pages = kv_local.shape[0]
    capacity = max(1, 2 * pages // parties)
    sessions = jnp.arange(parties, dtype=jnp.int32)
    table = (
        (owner_row[:, None] == sessions[None, :]).astype(jnp.int32).reshape(parties, pages, parties)
    )
    before = jnp.cumsum(table, axis=1) - table
    ranks = jnp.sum(before * table, axis=2)
    owners = owner_row.reshape(parties, pages)
    my_owner = lax.dynamic_index_in_dim(owners, myself, 0, keepdims=False)
    device_rank = lax.dynamic_index_in_dim(ranks, myself, 0, keepdims=False)

    def spread(array):
        empty = jnp.zeros((parties, capacity) + array.shape[1:], array.dtype)
        sent = empty.at[my_owner, device_rank].set(array)
        return lax.all_to_all(sent, "pool", split_axis=0, concat_axis=0, tiled=True)

    got_kv, got_state = spread(kv_local), spread(state_local)
    flat_place = (sessions[:, None] * capacity + ranks).reshape(-1)
    target = jnp.where(owner_row == myself, index_row, pages)
    where_from = jnp.zeros((pages,), jnp.int32).at[target].set(flat_place, mode="drop")
    return (
        got_kv.reshape((parties * capacity,) + kv_local.shape[1:])[where_from],
        got_state.reshape((parties * capacity,) + state_local.shape[1:])[where_from],
    )


def local(
    kv_pool,
    state_pool,
    block_owner,
    block_index,
    history_len,
    turn_len,
    mixer_in,
    input_proj,
    output_proj,
    step_size,
    decay_rate,
    bypass_factor,
    queries,
    turn_kv,
):
    parties = lax.axis_size("pool")
    myself = lax.axis_index("pool")
    segment = lax.axis_index("ctx")
    segments = lax.axis_size("ctx")
    kv = kv_pool[0]
    pages = kv.shape[0]
    rows = queries.shape[1]
    heads = kv.shape[-1] // HEAD_DIM
    partner = [(i, i ^ 1) for i in range(segments)]
    opposite = [(i, i ^ 2) for i in range(segments)]

    def to_partner(array):
        return lax.ppermute(array, "ctx", partner)

    def to_opposite(array):
        return lax.ppermute(array, "ctx", opposite)

    owners, places = block_owner[0], block_index[0]
    if parties == 2:
        swap = [(0, 1), (1, 0)]
        kind = (lax.dynamic_index_in_dim(owners, myself * pages, 0, keepdims=False) != myself).astype(
            jnp.int32
        )
        order = lax.dynamic_slice_in_dim(places, jnp.where(kind == 0, myself, 1 - myself) * pages, pages)
        slices = [kv[..., h * HEAD_DIM : (h + 1) * HEAD_DIM] for h in range(heads)]
        own_kv = [(piece, lax.ppermute(piece, "pool", swap)) for piece in slices]
        slabs = (state_pool, lax.ppermute(state_pool, "pool", swap))
    else:
        kind = jnp.zeros((), jnp.int32)
        order = jnp.arange(pages, dtype=jnp.int32)
        routed, slab = route_blocks(kv, state_pool, owners, places)
        own_kv = [(routed[..., h * HEAD_DIM : (h + 1) * HEAD_DIM],) for h in range(heads)]
        slabs = (slab,)
    partner_kv = [tuple(to_partner(piece) for piece in choice) for choice in own_kv]
    turns = (turn_kv[0], to_partner(turn_kv[0]))
    asks = (queries[0], to_opposite(queries[0]))
    own_info = jnp.concatenate([segment[None].astype(jnp.int32), kind[None], order])
    info = jnp.concatenate([history_len, own_info, to_partner(own_info)]).astype(jnp.int32)

    y, s, run = mixer_from_zero(
        mixer_in[0], input_proj[0], output_proj[0], step_size[0], decay_rate, bypass_factor, turn_len
    )
    parts = []
    for head in range(heads):
        o, level, sent = attend(head, info, asks, own_kv[head], partner_kv[head], turns)
        parts.append((o, level, to_opposite(sent)))
    mixed, final = add_saved(slabs, kind, order, y, s, run, output_proj[0], turn_len)
    live = turn_len - segment.astype(jnp.int32) * rows
    attended = merge(parts, live, rows)
    return (mixed[None], final[None], attended[None])


def solution(mesh):
    return jax.shard_map(
        local,
        mesh=mesh,
        in_specs=(
            P("ctx", "pool", None, None, "head"),
            P("pool", "ctx", "head"),
            P("ctx", None),
            P("ctx", None),
            P("pool"),
            P("pool"),
            P("pool", "head", "ctx", None),
            P("pool", "head", None, None),
            P("pool", "head", None, None),
            P("pool", "head", None),
            P("head"),
            P("head"),
            P("pool", "ctx", "head"),
            P("pool", None, "ctx", "head"),
        ),
        out_specs=(
            P("pool", "head", "ctx", None),
            P("pool", "head", "ctx", None),
            P("pool", "ctx", "head"),
        ),
        check_vma=False,
    )
```

time: 224 us -> 71.6 us (0.32)
  matrix products: 79.1 us -> 0 us
  other arithmetic: 42.5 us -> 0.65 us
  local copies, waits for them, and re-layouts: 48 us -> 8.36 us
  Pallas kernels: 0 us -> 32.6 us
  between operations: 14.9 us -> 2.76 us
  loops' own time: 6.43 us -> 0 us
  waiting for transfers between devices: 22.3 us -> 16.8 us
    dot_general x24 -> x0, matrix products: 79.1 us -> none  [the longest x4 23.7 us: attend_block(): jnp.einsum('rgqk,kgd->rgqd', weights.astype(jnp.bfloat16), value_heads, p...]
    pallas_call x0 -> x5, Pallas kernels: none -> 32.6 us  [the longest x2 18.6 us: attend(): pl.pallas_call(functools.partial(attend_kernel, kinds, head), in_specs=[s...]
    reduce_sum x5 -> x0, other arithmetic: 22.8 us -> none  [the longest x4 22.6 us: attend_block(): totals = fade * totals + jnp.sum(weights, axis=-1)]
    all_to_all x2 -> x0, waiting for transfers between devices: 22.3 us -> none  [the longest x1 21.5 us: route_blocks(): lax.all_to_all(send_kv, 'pool', split_axis=0, concat_axis=0, tiled=True)]
    ppermute x0 -> x12, waiting for transfers between devices: none -> 16.8 us  [the longest x2 14.9 us: local(): own_kv = [(piece, lax.ppermute(piece, 'pool', swap)) for piece in slices]]
    while x80 -> x0, local copies, waits for them, and re-layouts: 13.7 us -> none
    scatter x3 -> x0, local copies, waits for them, and re-layouts: 10.2 us -> none  [the longest x1 4.95 us: route_blocks(): send_kv = jnp.zeros((parties, capacity) + kv_local.shape[2:], kv_local.dt...]
    ppermute x0 -> x12, starting transfers between devices: none -> 10 us  [the longest x3 4.07 us: to_opposite(): return lax.ppermute(array, 'ctx', opposite)]
  transfers between devices with their start and end apart: 3 -> 12, of which waited for: 2 -> 4; matrix products, arithmetic and copies ran while one was open for 26% -> 5% of each run, Pallas kernels for 0% -> 42%
where the time goes in v1:
time: 71.6 us; the launch traced here: 71.2 us
  Pallas kernels  32.6 us (46%)
  waiting for transfers between devices  16.8 us (23%)
  starting transfers between devices  10 us (14%)
  local copies, waits for them, and re-layouts  8.36 us (12%)
  between operations  2.76 us (4%)
    pallas_call x2, Pallas kernels, attend(): pl.pallas_call(functools.partial(attend_kernel, kinds, head), in_specs=[s...  18.6 us
    ppermute x2, waiting for transfers between devices, local(): own_kv = [(piece, lax.ppermute(piece, 'pool', swap)) for piece in slices]  14.9 us
    pallas_call x1, Pallas kernels, mixer_from_zero(): pl.pallas_call(mixer_kernel, grid=(groups,), in_specs=[scalar, pl.BlockSp...  8.49 us
    unnamed x30, local copies, waits for them, and re-layouts  4.29 us
    ppermute x3, starting transfers between devices, to_opposite(): return lax.ppermute(array, 'ctx', opposite)  4.07 us
    ppermute x2, starting transfers between devices, local(): own_kv = [(piece, lax.ppermute(piece, 'pool', swap)) for piece in slices]  3.11 us
    pallas_call x1, Pallas kernels, add_saved(): pl.pallas_call(functools.partial(saved_kernel, len(slabs)), in_specs=[sca...  3.06 us
    pallas_call x1, Pallas kernels, merge(): pl.pallas_call(functools.partial(merge_kernel, heads), in_specs=[scalar]...  2.45 us
  transfers between devices with their start and end apart: 12, of which 4 were waited for; matrix products, arithmetic and copies ran while one was open for 5% of the time, Pallas kernels for 42%

profile of v1, /device:TPU:0, one launch (start us, length us, event | category | flops | bytes accessed | tf_op | source)
XLA Modules:
  0.0 71.2 jit_solution(13644996370829925173)
XLA Ops:
  0.6 0.0 copy-start
  0.6 0.0 copy-start.9
  0.7 0.0 copy-start.12
  0.7 0.0 copy-start.5
  0.7 1.3 %fusion = (bf16[32,2,32,128]{3,2,1,0:T(8,128)(2,1)S(1)}, bf16[32,2,32,128]{3,2,1,0:T(8,128)(2,1)S(1)}) fusion(bf16[32,2,32,256]{3,2,1,0:T(8,128)(2,1)} %bitcast.18), kind=kLoop, calls=%fused_computation.4 | loop fusion | bytes 2097152 | tf_op jit(solution)/shard_map/slice | solution.py:452
  2.0 0.0 copy-start.1
  2.1 3.0 %collective-permute-start.8 = (bf16[32,2,32,128]{3,2,1,0:T(8,128)(2,1)S(1)}, bf16[32,2,32,128]{3,2,1,0:T(8,128)(2,1)}, u32[]{:S(2)}, u32[]{:S(2)}) collective-permute-start(bf16[32,2,32,128]{3,2,1,0:T(8,128)(2,1)S(1)} %get-tuple-element.25.refs_2_), channel_id=1, source_target_pairs={{0,16},{16,0},{1,17},{17,1},{2,18},{18,2},{3,19},{19,3},{4,20},{20... | collective-permute-start | bytes 1572872 | tf_op jit(solution)/shard_map/ppermute | solution.py:453
  5.1 0.1 collective-permute-start.3
  5.2 0.0 collective-permute-start.9
  5.2 1.9 %collective-permute-start.2 = (bf16[128,2048]{1,0:T(8,128)(2,1)S(1)}, bf16[128,2048]{1,0:T(8,128)(2,1)S(1)}, u32[]{:S(2)}, u32[]{:S(2)}) collective-permute-start(bf16[128,2048]{1,0:T(8,128)(2,1)S(1)} %bitcast.26), channel_id=1, source_target_pairs={{0,8},{4,12},{8,0},{12,4},{1,9},{5,13},{9,1},{13,5},{2,10},{6,14},... | collective-permute-start | bytes 1572872 | tf_op jit(solution)/shard_map/ppermute | solution.py:443
  7.1 0.7 copy-done.14
  7.7 0.6 constant_dynamic-slice_fusion
  9.6 0.1 dynamic-slice_bitcast_fusion
  9.7 8.2 %collective-permute-done.8.refs_3_ = bf16[32,2,32,128]{3,2,1,0:T(8,128)(2,1)} collective-permute-done((bf16[32,2,32,128]{3,2,1,0:T(8,128)(2,1)S(1)}, bf16[32,2,32,128]{3,2,1,0:T(8,128)(2,1)}, u32[]{:S(2)}, u32[]{:S(2)}) %collective-permute-start.8) | collective-permute-done | bytes 524320 | tf_op jit(solution)/shard_map/ppermute | solution.py:453
  17.9 0.0 collective-permute-start.10
  17.9 0.7 add_add_fusion.1
  18.6 0.5 collective-permute-start.1
  19.1 0.8 %collective-permute-done.1 = s32[34]{0:T(128)S(1)} collective-permute-done((s32[34]{0:T(128)S(1)}, s32[34]{0:T(128)S(1)}, u32[]{:S(2)}, u32[]{:S(2)}) %collective-permute-start.1) | collective-permute-done | bytes 168 | tf_op jit(solution)/shard_map/ppermute | solution.py:440
  19.9 0.3 collective-permute-start.6
  20.2 1.0 %collective-permute-done.6.refs_7_ = bf16[2,128,256]{2,1,0:T(8,128)(2,1)S(1)} collective-permute-done((bf16[2,128,256]{2,1,0:T(8,128)(2,1)S(1)}, bf16[2,128,256]{2,1,0:T(8,128)(2,1)S(1)}, u32[]{:S(2)}, u32[]{:S(2)}) %collective-permute-start.6) | collective-permute-done | bytes 131104 | tf_op jit(solution)/shard_map/ppermute | solution.py:440
  21.3 0.3 collective-permute-start.4
  21.6 6.7 %collective-permute-done.3.refs_3_ = bf16[32,2,32,128]{3,2,1,0:T(8,128)(2,1)S(1)} collective-permute-done((bf16[32,2,32,128]{3,2,1,0:T(8,128)(2,1)S(1)}, bf16[32,2,32,128]{3,2,1,0:T(8,128)(2,1)S(1)}, u32[]{:S(2)}, u32[]{:S(2)}) %collective-permute-start.3) | collective-permute-done | bytes 524320 | tf_op jit(solution)/shard_map/ppermute | solution.py:453
  28.2 0.0 collective-permute-start.5
  28.9 0.7 concatenate.12.info_ref
  29.6 0.0 collective-permute-done.9.refs_4_
  29.6 1.7 %collective-permute-start = (bf16[32,16,256]{2,1,0:T(8,128)(2,1)S(1)}, bf16[32,16,256]{2,1,0:T(8,128)(2,1)S(1)}, u32[]{:S(2)}, u32[]{:S(2)}) collective-permute-start(bf16[32,16,256]{2,1,0:T(8,128)(2,1)S(1)} %copy-done.5), channel_id=1, source_target_pairs={{0,16},{16,0},{1,17},{17,1},{2,18},{18,2},{3,19},{19,3},{4,20},{20... | collective-permute-start | bytes 786440 | tf_op jit(solution)/shard_map/ppermute | solution.py:454
  31.3 0.0 collective-permute-done.2.refs_1_
  31.3 0.0 collective-permute-done.10.refs_5_
  31.4 0.8 %copy-done.11 = bf16[128,2048]{1,0:T(8,128)(2,1)} copy-done((bf16[128,2048]{1,0:T(8,128)(2,1)}, bf16[128,2048]{1,0:T(8,128)(2,1)S(1)}, u32[]{:S(2)}) %copy-start.11) | copy-done | bytes 524312
  32.1 9.2 %attend_1.1 = (bf16[1024,128]{1,0:T(8,128)(2,1)}, f32[8,128]{1,0:T(8,128)}, bf16[1056,128]{1,0:T(8,128)(2,1)}) custom-call(s32[69]{0:T(128)} %concatenate.12.info_ref, bf16[128,2048]{1,0:T(8,128)(2,1)} %bitcast.24, bf16[128,2048]{1,0:T(8,128)(2,1)} %copy-done.11, bf16[32,2,32,128]{3,2,1,0:T(8,128)(2,1)} %copy-done.2, ...), custom_call_target="tpu_custom_call" | custom-call | flops 2147483648 | bytes 3145728 | tf_op jit(solution)/shard_map/attend_1/pallas_call | solution.py:319
  41.4 1.6 %collective-permute-start.11 = (bf16[1056,128]{1,0:T(8,128)(2,1)}, bf16[1056,128]{1,0:T(8,128)(2,1)S(1)}, u32[]{:S(2)}, u32[]{:S(2)}) collective-permute-start(bf16[1056,128]{1,0:T(8,128)(2,1)} %get-tuple-element.24), channel_id=1, source_target_pairs={{0,8},{4,12},{8,0},{12,4},{1,9},{5,13},{9,1},{13,5},{2,10},{6,14},... | collective-permute-start | bytes 811016 | tf_op jit(solution)/shard_map/ppermute | solution.py:443
  42.9 0.0 collective-permute-done.4.refs_4_
  42.9 0.0 collective-permute-done.5.refs_5_
  43.0 9.4 %attend_0.1 = (bf16[1024,128]{1,0:T(8,128)(2,1)}, f32[8,128]{1,0:T(8,128)}, bf16[1056,128]{1,0:T(8,128)(2,1)}) custom-call(s32[69]{0:T(128)} %concatenate.12.info_ref, bf16[128,2048]{1,0:T(8,128)(2,1)} %bitcast.25, bf16[128,2048]{1,0:T(8,128)(2,1)} %copy-done.11, bf16[32,2,32,128]{3,2,1,0:T(8,128)(2,1)} %copy-done.1, bf16[32,2,32,128]{3,2,1,0:T(8,128)(2,1)} %copy-done.10, ...), custom_call_target="tpu_custom_call" | custom-call | flops 2147483648 | bytes 3145728 | tf_op jit(solution)/shard_map/attend_0/pallas_call | solution.py:319
  52.4 0.6 collective-permute-start.7
  53.0 0.7 copy-done.7
  53.6 0.7 copy.17.rate_ref
  54.3 0.7 copy-done.8
  55.0 0.7 copy.18.gain_ref
  55.7 8.5 %mixer_from_zero.1 = (f32[32,16,512]{2,1,0:T(8,128)}, f32[32,16,256]{2,1,0:T(8,128)}, f32[32,512]{1,0:T(8,128)}) custom-call(s32[1]{0:T(128)S(6)} %copy.20.valid_ref, bf16[32,16,512]{2,1,0:T(8,128)(2,1)} %bitcast.27, bf16[2,256,512]{2,1,0:T(8,128)(2,1)} %bitcast.28, bf16[2,256,512]{2,1,0:T(8,128)(2,1)} %bitcast.20, f32[32,512]{1,0:T(8,128)} %bitcast.34, ...), custom_call_target="tpu_custom_call" | custom-call | flops 1000000000 | bytes 6291456 | tf_op jit(solution)/shard_map/mixer_from_zero/pallas_call | solution.py:84
  64.2 0.0 collective-permute-done.refs_1_
  64.2 0.7 %copy-done.6 = bf16[32,16,256]{2,1,0:T(8,128)(2,1)} copy-done((bf16[32,16,256]{2,1,0:T(8,128)(2,1)}, bf16[32,16,256]{2,1,0:T(8,128)(2,1)S(1)}, u32[]{:S(2)}) %copy-start.6) | copy-done | bytes 262168
  64.9 3.1 %add_saved.1 = (bf16[32,16,512]{2,1,0:T(8,128)(2,1)}, f32[32,16,256]{2,1,0:T(8,128)}) custom-call(s32[34]{0:T(128)} %get-tuple-element.28.info_ref, bf16[32,16,256]{2,1,0:T(8,128)(2,1)} %refs_0_.1, bf16[32,16,256]{2,1,0:T(8,128)(2,1)} %copy-done.6, f32[32,16,512]{2,1,0:T(8,128)} %get-tuple-element.14.refs_2_, f32[32,16,256]{2,1,0:T(8,128)} %get-tuple-element.15.refs_3_, ...), custom_call_target="tpu_custom_call" | custom-call | flops 100000000 | bytes 5242880 | tf_op jit(solution)/shard_map/add_saved/pallas_call | solution.py:145
  68.0 0.0 collective-permute-done.11.refs_5_
  68.0 0.0 collective-permute-done.7.refs_2_
  68.0 0.7 copy-done.3
  68.7 0.1 copy-done.4
  68.8 2.5 %merge.1 = bf16[128,2048]{1,0:T(8,128)(2,1)} custom-call(s32[1]{0:T(128)S(6)} %sub.11.info_ref, bf16[1024,128]{1,0:T(8,128)(2,1)} %get-tuple-element.19.refs_0_, f32[8,128]{1,0:T(8,128)} %get-tuple-element.20.refs_1_, bf16[1056,128]{1,0:T(8,128)(2,1)} %copy-done.4, bf16[1024,128]{1,0:T(8,128)(2,1)} %get-tuple-element.22.refs_3_, ...), custom_call_target="tpu_custom_call" | custom-call | tf_op jit(solution)/shard_map/merge/pallas_call | solution.py:372
  (18 shorter events, 0.0 us)
Async XLA Ops:
  0.6 9.0 %copy-start = (s32[1,64]{1,0:T(1,128)S(1)}, s32[1,64]{1,0:T(1,128)}, u32[]{:S(2)}) copy-start(s32[1,64]{1,0:T(1,128)} %param.17) | copy-start | bytes 772
  0.6 4.5 %copy-start.9 = (bf16[1,128,2048]{2,1,0:T(8,128)(2,1)S(1)}, bf16[1,128,2048]{2,1,0:T(8,128)(2,1)}, u32[]{:S(2)}) copy-start(bf16[1,128,2048]{2,1,0:T(8,128)(2,1)} %param.26) | copy-start | bytes 1572868
  0.7 19.3 %copy-start.12 = (bf16[1,2,128,256]{3,2,1,0:T(8,128)(2,1)S(1)}, bf16[1,2,128,256]{3,2,1,0:T(8,128)(2,1)}, u32[]{:S(2)}) copy-start(bf16[1,2,128,256]{3,2,1,0:T(8,128)(2,1)} %param.27) | copy-start | bytes 393220
  0.7 28.9 %copy-start.5 = (bf16[32,16,256]{2,1,0:T(8,128)(2,1)S(1)}, bf16[32,16,256]{2,1,0:T(8,128)(2,1)}, u32[]{:S(2)}) copy-start(bf16[32,16,256]{2,1,0:T(8,128)(2,1)} %refs_0_.1) | copy-start | bytes 786436
  2.0 29.3 %copy-start.2 = (bf16[32,2,32,128]{3,2,1,0:T(8,128)(2,1)}, bf16[32,2,32,128]{3,2,1,0:T(8,128)(2,1)S(1)}, u32[]{:S(2)}) copy-start(bf16[32,2,32,128]{3,2,1,0:T(8,128)(2,1)S(1)} %get-tuple-element.25.refs_2_) | copy-start | bytes 1572868
  2.0 39.3 %copy-start.1 = (bf16[32,2,32,128]{3,2,1,0:T(8,128)(2,1)}, bf16[32,2,32,128]{3,2,1,0:T(8,128)(2,1)S(1)}, u32[]{:S(2)}) copy-start(bf16[32,2,32,128]{3,2,1,0:T(8,128)(2,1)S(1)} %get-tuple-element.26.refs_2_) | copy-start | bytes 1572868
  2.1 15.9 %collective-permute-start.8 = (bf16[32,2,32,128]{3,2,1,0:T(8,128)(2,1)S(1)}, bf16[32,2,32,128]{3,2,1,0:T(8,128)(2,1)}, u32[]{:S(2)}, u32[]{:S(2)}) collective-permute-start(bf16[32,2,32,128]{3,2,1,0:T(8,128)(2,1)S(1)} %get-tuple-element.25.refs_2_), channel_id=1, source_target_pairs={{0,16},{16,0},{1,17},{17,1},{2,18},{18,2},{3,19},{19,3},{4,20},{20... | collective-permute-start | bytes 1572872 | tf_op jit(solution)/shard_map/ppermute | solution.py:453
  5.1 23.2 %collective-permute-start.3 = (bf16[32,2,32,128]{3,2,1,0:T(8,128)(2,1)S(1)}, bf16[32,2,32,128]{3,2,1,0:T(8,128)(2,1)S(1)}, u32[]{:S(2)}, u32[]{:S(2)}) collective-permute-start(bf16[32,2,32,128]{3,2,1,0:T(8,128)(2,1)S(1)} %get-tuple-element.26.refs_2_), channel_id=1, source_target_pairs={{0,16},{16,0},{1,17},{17,1},{2,18},{18,2},{3,19},{19,3},{4,20},{20... | collective-permute-start | bytes 1572872 | tf_op jit(solution)/shard_map/ppermute | solution.py:453
  5.2 24.4 %collective-permute-start.9 = (bf16[32,2,32,128]{3,2,1,0:T(8,128)(2,1)S(1)}, bf16[32,2,32,128]{3,2,1,0:T(8,128)(2,1)}, u32[]{:S(2)}, u32[]{:S(2)}) collective-permute-start(bf16[32,2,32,128]{3,2,1,0:T(8,128)(2,1)S(1)} %get-tuple-element.25.refs_2_), channel_id=1, source_target_pairs={{0,4},{4,0},{8,12},{12,8},{1,5},{5,1},{9,13},{13,9},{2,6},{6,2},{1... | collective-permute-start | bytes 1572872 | tf_op jit(solution)/shard_map/ppermute | solution.py:440
  5.2 26.2 %collective-permute-start.2 = (bf16[128,2048]{1,0:T(8,128)(2,1)S(1)}, bf16[128,2048]{1,0:T(8,128)(2,1)S(1)}, u32[]{:S(2)}, u32[]{:S(2)}) collective-permute-start(bf16[128,2048]{1,0:T(8,128)(2,1)S(1)} %bitcast.26), channel_id=1, source_target_pairs={{0,8},{4,12},{8,0},{12,4},{1,9},{5,13},{9,1},{13,5},{2,10},{6,14},... | collective-permute-start | bytes 1572872 | tf_op jit(solution)/shard_map/ppermute | solution.py:443
  7.1 0.7 copy-start.14
  17.9 13.4 %collective-permute-start.10 = (bf16[32,2,32,128]{3,2,1,0:T(8,128)(2,1)}, bf16[32,2,32,128]{3,2,1,0:T(8,128)(2,1)}, u32[]{:S(2)}, u32[]{:S(2)}) collective-permute-start(bf16[32,2,32,128]{3,2,1,0:T(8,128)(2,1)} %collective-permute-done.8.refs_3_), channel_id=1, source_target_pairs={{0,4},{4,0},{8,12},{12,8},{1,5},{5,1},{9,13},{13,9},{2,6},{6,2},{1... | collective-permute-start | bytes 1572872 | tf_op jit(solution)/shard_map/ppermute | solution.py:440
  18.6 1.3 %collective-permute-start.1 = (s32[34]{0:T(128)S(1)}, s32[34]{0:T(128)S(1)}, u32[]{:S(2)}, u32[]{:S(2)}) collective-permute-start(s32[34]{0:T(128)S(1)} %get-tuple-element.27), channel_id=1, source_target_pairs={{0,4},{4,0},{8,12},{12,8},{1,5},{5,1},{9,13},{13,9},{2,6},{6,2},{1... | collective-permute-start | bytes 416 | tf_op jit(solution)/shard_map/ppermute | solution.py:440
  19.9 1.3 %collective-permute-start.6 = (bf16[2,128,256]{2,1,0:T(8,128)(2,1)S(1)}, bf16[2,128,256]{2,1,0:T(8,128)(2,1)S(1)}, u32[]{:S(2)}, u32[]{:S(2)}) collective-permute-start(bf16[2,128,256]{2,1,0:T(8,128)(2,1)S(1)} %bitcast.33), channel_id=1, source_target_pairs={{0,4},{4,0},{8,12},{12,8},{1,5},{5,1},{9,13},{13,9},{2,6},{6,2},{1... | collective-permute-start | bytes 393224 | tf_op jit(solution)/shard_map/ppermute | solution.py:440
  21.3 10.1 %copy-start.13 = (bf16[2,128,256]{2,1,0:T(8,128)(2,1)}, bf16[2,128,256]{2,1,0:T(8,128)(2,1)S(1)}, u32[]{:S(2)}) copy-start(bf16[2,128,256]{2,1,0:T(8,128)(2,1)S(1)} %collective-permute-done.6.refs_7_) | copy-start | bytes 393220
  21.3 21.7 %collective-permute-start.4 = (bf16[32,2,32,128]{3,2,1,0:T(8,128)(2,1)S(1)}, bf16[32,2,32,128]{3,2,1,0:T(8,128)(2,1)}, u32[]{:S(2)}, u32[]{:S(2)}) collective-permute-start(bf16[32,2,32,128]{3,2,1,0:T(8,128)(2,1)S(1)} %get-tuple-element.26.refs_2_), channel_id=1, source_target_pairs={{0,4},{4,0},{8,12},{12,8},{1,5},{5,1},{9,13},{13,9},{2,6},{6,2},{1... | collective-permute-start | bytes 1572872 | tf_op jit(solution)/shard_map/ppermute | solution.py:440
  28.2 13.1 %copy-start.10 = (bf16[32,2,32,128]{3,2,1,0:T(8,128)(2,1)}, bf16[32,2,32,128]{3,2,1,0:T(8,128)(2,1)S(1)}, u32[]{:S(2)}) copy-start(bf16[32,2,32,128]{3,2,1,0:T(8,128)(2,1)S(1)} %collective-permute-done.3.refs_3_) | copy-start | bytes 1572868
  28.2 14.7 %collective-permute-start.5 = (bf16[32,2,32,128]{3,2,1,0:T(8,128)(2,1)S(1)}, bf16[32,2,32,128]{3,2,1,0:T(8,128)(2,1)}, u32[]{:S(2)}, u32[]{:S(2)}) collective-permute-start(bf16[32,2,32,128]{3,2,1,0:T(8,128)(2,1)S(1)} %collective-permute-done.3.refs_3_), channel_id=1, source_target_pairs={{0,4},{4,0},{8,12},{12,8},{1,5},{5,1},{9,13},{13,9},{2,6},{6,2},{1... | collective-permute-start | bytes 1572872 | tf_op jit(solution)/shard_map/ppermute | solution.py:440
  29.6 34.6 %collective-permute-start = (bf16[32,16,256]{2,1,0:T(8,128)(2,1)S(1)}, bf16[32,16,256]{2,1,0:T(8,128)(2,1)S(1)}, u32[]{:S(2)}, u32[]{:S(2)}) collective-permute-start(bf16[32,16,256]{2,1,0:T(8,128)(2,1)S(1)} %copy-done.5), channel_id=1, source_target_pairs={{0,16},{16,0},{1,17},{17,1},{2,18},{18,2},{3,19},{19,3},{4,20},{20... | collective-permute-start | bytes 786440 | tf_op jit(solution)/shard_map/ppermute | solution.py:454
  31.3 0.8 %copy-start.11 = (bf16[128,2048]{1,0:T(8,128)(2,1)}, bf16[128,2048]{1,0:T(8,128)(2,1)S(1)}, u32[]{:S(2)}) copy-start(bf16[128,2048]{1,0:T(8,128)(2,1)S(1)} %collective-permute-done.2.refs_1_) | copy-start | bytes 1572868
  41.4 26.6 %collective-permute-start.11 = (bf16[1056,128]{1,0:T(8,128)(2,1)}, bf16[1056,128]{1,0:T(8,128)(2,1)S(1)}, u32[]{:S(2)}, u32[]{:S(2)}) collective-permute-start(bf16[1056,128]{1,0:T(8,128)(2,1)} %get-tuple-element.24), channel_id=1, source_target_pairs={{0,8},{4,12},{8,0},{12,4},{1,9},{5,13},{9,1},{13,5},{2,10},{6,14},... | collective-permute-start | bytes 811016 | tf_op jit(solution)/shard_map/ppermute | solution.py:443
  52.4 15.6 %collective-permute-start.7 = (bf16[1056,128]{1,0:T(8,128)(2,1)}, bf16[1056,128]{1,0:T(8,128)(2,1)S(1)}, u32[]{:S(2)}, u32[]{:S(2)}) collective-permute-start(bf16[1056,128]{1,0:T(8,128)(2,1)} %get-tuple-element.21), channel_id=1, source_target_pairs={{0,8},{4,12},{8,0},{12,4},{1,9},{5,13},{9,1},{13,5},{2,10},{6,14},... | collective-permute-start | bytes 811016 | tf_op jit(solution)/shard_map/ppermute | solution.py:443
  53.0 0.7 copy-start.7
  54.3 0.7 copy-start.8
  64.2 0.7 %copy-start.6 = (bf16[32,16,256]{2,1,0:T(8,128)(2,1)}, bf16[32,16,256]{2,1,0:T(8,128)(2,1)S(1)}, u32[]{:S(2)}) copy-start(bf16[32,16,256]{2,1,0:T(8,128)(2,1)S(1)} %collective-permute-done.refs_1_) | copy-start | bytes 786436
  68.0 0.7 copy-start.3
  68.0 0.8 %copy-start.4 = (bf16[1056,128]{1,0:T(8,128)(2,1)}, bf16[1056,128]{1,0:T(8,128)(2,1)S(1)}, u32[]{:S(2)}) copy-start(bf16[1056,128]{1,0:T(8,128)(2,1)S(1)} %collective-permute-done.7.refs_2_) | copy-start | bytes 811012

commit v2 on v1

v2 whole, which is shorter than its diff:
```python
import functools

import jax
import jax.numpy as jnp
from jax import lax
from jax.experimental import pallas as pl
from jax.experimental.pallas import tpu as pltpu
from jax.sharding import PartitionSpec as P

Q_HEADS = 64
KV_HEADS = 8
HEAD_DIM = 128
PER_GROUP = Q_HEADS // KV_HEADS
BLK = 128
HIDDEN = -1e30
TO_POWER = (HEAD_DIM**-0.5) * 1.4426950408889634
STAT_ROWS = 32

whole = pl.BlockSpec(memory_space=pltpu.VMEM)
scalar = pl.BlockSpec(memory_space=pltpu.SMEM)
outside = pl.BlockSpec(memory_space=pl.ANY)
distant = pl.BlockSpec(memory_space=pltpu.HBM)


def params(mib):
    return pltpu.CompilerParams(vmem_limit_bytes=mib * 2**20)


def locate(kinds, owner_ref, pages):
    if kinds == 1:
        return 0, 0
    myself = lax.axis_index("pool")
    kind = jnp.where(owner_ref[0, myself * pages] == myself, 0, 1).astype(jnp.int32)
    return kind, jnp.where(kind == 0, myself, 1 - myself) * pages


def as_column(row_ref, start, count):
    row = jnp.broadcast_to(row_ref[...], (count, row_ref.shape[1]))
    across = lax.broadcasted_iota(jnp.int32, row.shape, 1)
    down = lax.broadcasted_iota(jnp.int32, row.shape, 0)
    return jnp.sum(jnp.where(across == down + start, row, 0.0), axis=1, keepdims=True)


def mixer_kernel(valid_ref, x_ref, b_ref, c_ref, dt_ref, rate_ref, gain_ref, y_ref, s_ref, run_ref):
    heads, chans, total = x_ref.shape
    start = pl.program_id(0) * heads
    states = b_ref.shape[1]
    rows = heads * chans
    place = lax.broadcasted_iota(jnp.int32, (heads, total), 1)
    steps = jnp.where(place < valid_ref[0], dt_ref[...], 0.0)
    falls = -as_column(rate_ref, start, heads) * steps
    gains = as_column(gain_ref, start, heads)
    first = lax.broadcasted_iota(jnp.int32, (BLK, BLK), 0)
    second = lax.broadcasted_iota(jnp.int32, (BLK, BLK), 1)
    upper = first <= second
    ones_upper = jnp.where(upper, 1.0, 0.0).astype(jnp.float32)
    turned = b_ref[0].T
    state = jnp.zeros((rows, states), jnp.float32)
    base = jnp.zeros((heads, 1), jnp.float32)
    for blk in range(total // BLK):
        span = slice(blk * BLK, (blk + 1) * BLK)
        run = jnp.dot(
            falls[:, span],
            ones_upper,
            precision=lax.Precision.HIGHEST,
            preferred_element_type=jnp.float32,
        )
        run_col = run.T
        last = run[:, BLK - 1 :]
        pairs = jnp.dot(turned[span], c_ref[0, :, span], preferred_element_type=jnp.float32)
        pairs = jnp.where(upper, pairs, 0.0)
        x_blk = x_ref[:, :, span].astype(jnp.float32)
        stepped = (x_blk * steps[:, None, span]).astype(jnp.bfloat16)
        inside = []
        for head in range(heads):
            gap = jnp.minimum(run[head : head + 1, :] - run_col[:, head : head + 1], 0.0)
            mixing = (jnp.exp(gap) * pairs).astype(jnp.bfloat16)
            inside.append(jnp.dot(stepped[head], mixing, preferred_element_type=jnp.float32))
        result = jnp.stack(inside) + gains[:, :, None] * x_blk
        if blk:
            read = jnp.dot(
                state.astype(jnp.bfloat16), c_ref[0, :, span], preferred_element_type=jnp.float32
            )
            result = result + jnp.exp(run)[:, None, :] * read.reshape(heads, chans, BLK)
        y_ref[:, :, span] = result
        weights = jnp.exp(last - run) * steps[:, span]
        weighted = (x_blk * weights[:, None, :]).astype(jnp.bfloat16).reshape(rows, BLK)
        added = jnp.dot(weighted, turned[span], preferred_element_type=jnp.float32)
        kept = jnp.broadcast_to(jnp.exp(last)[:, :, None], (heads, chans, 1)).reshape(rows, 1)
        state = kept * state + added
        run_ref[:, span] = base + run
        base = base + last
    s_ref[...] = state.reshape(heads, chans, states)


def mixer_from_zero(valid, x, b, c, dt, rates, gains):
    heads, chans, total = x.shape
    groups, states, _ = b.shape
    per = heads // groups
    return pl.pallas_call(
        mixer_kernel,
        grid=(groups,),
        in_specs=[
            scalar,
            pl.BlockSpec((per, chans, total), lambda g: (g, 0, 0)),
            pl.BlockSpec((1, states, total), lambda g: (g, 0, 0)),
            pl.BlockSpec((1, states, total), lambda g: (g, 0, 0)),
            pl.BlockSpec((per, total), lambda g: (g, 0)),
            pl.BlockSpec((1, heads), lambda g: (0, 0)),
            pl.BlockSpec((1, heads), lambda g: (0, 0)),
        ],
        out_specs=[
            pl.BlockSpec((per, chans, total), lambda g: (g, 0, 0)),
            pl.BlockSpec((per, chans, states), lambda g: (g, 0, 0)),
            pl.BlockSpec((per, total), lambda g: (g, 0)),
        ],
        out_shape=[
            jax.ShapeDtypeStruct((heads, chans, total), jnp.float32),
            jax.ShapeDtypeStruct((heads, chans, states), jnp.float32),
            jax.ShapeDtypeStruct((heads, total), jnp.float32),
        ],
        compiler_params=params(16),
        cost_estimate=pl.CostEstimate(flops=1, bytes_accessed=1, transcendentals=0),
        name="mixer_from_zero",
    )(valid, x, b, c, dt, rates[None], gains[None])


def saved_kernel(kinds, valid_ref, owner_ref, place_ref, *refs):
    refs = refs[1:]
    slabs = refs[:kinds]
    y_ref, s_ref, run_ref, c_ref, out_ref, final_ref, done_ref, start, mixed, final, sems = refs[
        kinds:
    ]
    done_ref[...] = jnp.zeros(done_ref.shape, jnp.float32)
    heads, chans, total = y_ref.shape
    groups, states, _ = c_ref.shape
    per = heads // groups
    copies = []
    chosen, source = locate(kinds, owner_ref, heads)
    for kind in range(kinds):

        @pl.when(chosen == kind)
        def _():
            for slot in range(heads):
                start[place_ref[0, source + slot]] = slabs[kind][slot]

    live = lax.broadcasted_iota(jnp.int32, (1, 1, total), 2) < valid_ref[0]
    for group in range(groups):
        mine = slice(group * per, (group + 1) * per)
        saved = start[mine]
        fade = jnp.exp(run_ref[mine, :])
        read = jnp.dot(
            saved.reshape(per * chans, states), c_ref[group], preferred_element_type=jnp.float32
        ).reshape(per, chans, total)
        result = y_ref[mine] + fade[:, None, :] * read
        mixed[mine] = jnp.where(live, result, 0.0).astype(jnp.bfloat16)
        kept = fade[:, None, total - 1 :]
        final[mine] = s_ref[mine] + kept * saved.astype(jnp.float32)
        span = pl.ds(group * per, per)
        for held, target in ((mixed, out_ref), (final, final_ref)):
            copies.append(
                pltpu.make_async_copy(held.at[span], target.at[span], sems.at[len(copies)])
            )
            copies[-1].start()
    for copy in copies:
        copy.wait()


def add_saved(after, valid, rows, slabs, y, s, run, c):
    heads, chans, total = y.shape
    groups, states, _ = c.shape
    return pl.pallas_call(
        functools.partial(saved_kernel, len(slabs)),
        in_specs=[scalar] * 3 + [outside] + [whole] * (len(slabs) + 4),
        out_specs=[distant, distant, whole],
        out_shape=[
            jax.ShapeDtypeStruct((heads, chans, total), jnp.bfloat16),
            jax.ShapeDtypeStruct((heads, chans, states), jnp.float32),
            jax.ShapeDtypeStruct((8, 128), jnp.float32),
        ],
        scratch_shapes=[
            pltpu.VMEM((heads, chans, states), jnp.bfloat16),
            pltpu.VMEM((heads, chans, total), jnp.bfloat16),
            pltpu.VMEM((heads, chans, states), jnp.float32),
            pltpu.SemaphoreType.DMA((2 * groups,)),
        ],
        compiler_params=params(12),
        cost_estimate=pl.CostEstimate(flops=1, bytes_accessed=1, transcendentals=0),
        name="add_saved",
    )(valid, *rows, after, *slabs, y, s, run, c)


def attend_kernel(counts, head, sides, seen_ref, *refs):
    rows_refs, refs = (refs[0:2], refs[2:4]), refs[4:]
    refs = refs[1:]
    q_refs, turn_refs, refs = refs[: len(sides)], refs[len(sides) : len(sides) + 2], refs[len(sides) + 2 :]
    kinds = len(counts)
    kv_refs = ([], [])
    for side in range(2):
        for count in counts:
            kv_refs[side].append(refs[:count])
            refs = refs[count:]
    out_refs = {}
    for asked in sides:
        out_refs[asked], refs = refs[0], refs[1:]
        if asked == 0:
            l_ref, refs = refs[0], refs[1:]
    queries, keys, turn_keys, turn_raw, values, sems = refs
    pages, page = kv_refs[0][0][0].shape[0], kv_refs[0][0][0].shape[-2]
    rows = q_refs[0].shape[0]
    history = pages * page
    width = PER_GROUP * HEAD_DIM
    segment = lax.axis_index("ctx")
    numbers = (segment, segment ^ 1)
    found = [locate(kinds, rows_refs[side][0], pages) for side in range(2)]
    columns = pl.ds(head * HEAD_DIM, HEAD_DIM)
    copies = [
        pltpu.make_async_copy(q_ref.at[:, pl.ds(head * width, width)], queries.at[i], sems.at[i])
        for i, q_ref in enumerate(q_refs)
    ]
    for side in range(2):
        copies.append(
            pltpu.make_async_copy(
                turn_refs[side].at[:, :, columns], turn_raw.at[side], sems.at[2 + side]
            )
        )

    def page_copies(side, kind):
        sources = kv_refs[side][kind]
        if len(sources) == 1:
            sources = [sources[0].at[:, half] for half in range(2)]
        wide = sources[0].shape[2] > HEAD_DIM
        lanes = columns if wide else pl.ds(0, HEAD_DIM)
        target = pl.ds(side * pages, pages)
        return [
            pltpu.make_async_copy(
                sources[half].at[:, :, lanes],
                place.at[target, :, pl.ds(0, HEAD_DIM)],
                sems.at[4 + 2 * half + side],
            )
            for half, place in enumerate((keys, values))
        ]

    for side in range(2):
        for kind in range(kinds):

            @pl.when(found[side][0] == kind)
            def _():
                for copy in page_copies(side, kind):
                    copy.start()

    for copy in copies:
        copy.start()
    in_page = lax.broadcasted_iota(jnp.int32, (page, HEAD_DIM), 0)
    seen = seen_ref[0]
    for side in range(2):
        start = numbers[side] * history
        for number in range(pages):
            left = seen - start - rows_refs[side][1][0, found[side][1] + number] * page
            keys[side * pages + number, :, HEAD_DIM:] = jnp.where(
                in_page < left, 0.0, HIDDEN
            ).astype(jnp.bfloat16)
    values[:, :, HEAD_DIM:] = jnp.ones(
        (values.shape[0], page, HEAD_DIM), jnp.bfloat16
    )
    first = lax.broadcasted_iota(jnp.int32, (rows, rows), 0)
    second = lax.broadcasted_iota(jnp.int32, (rows, rows), 1)
    eye = jnp.where(first == second, 1.0, 0.0).astype(jnp.bfloat16)
    for i, asked in enumerate(sides):
        asking = segment ^ (2 * asked)
        for side in range(2):
            ahead = first + numbers[side] * rows
            turn_keys[i, pl.ds(side * rows, rows), HEAD_DIM:] = jnp.where(
                ahead <= second + asking * rows, 0.0, HIDDEN
            ).astype(jnp.bfloat16)
    for copy in copies:
        copy.wait()
    turn_pages = rows // page
    for side in range(2):
        for i in range(len(sides)):
            turn_keys[i, pl.ds(side * rows, rows), pl.ds(0, HEAD_DIM)] = turn_raw[side, 0]
        values[
            pl.ds(2 * pages + side * turn_pages, turn_pages), :, pl.ds(0, HEAD_DIM)
        ] = turn_raw[side, 1].reshape(turn_pages, page, HEAD_DIM)
    for side in range(2):
        for copy in page_copies(side, 0):
            copy.wait()
    depth = 2 * HEAD_DIM
    all_keys = 2 * history
    lane = lax.broadcasted_iota(jnp.int32, (rows, HEAD_DIM), 1)
    across = (((1,), (1,)), ((), ()))
    at_once = 2
    for which, asked in enumerate(sides):
        out_ref = out_refs[asked]
        stats = jnp.zeros((rows, HEAD_DIM), jnp.float32)
        for batch in range(PER_GROUP // at_once):
            asks = jnp.concatenate(
                [
                    jnp.concatenate(
                        [
                            queries[which, :, pl.ds((batch * at_once + i) * HEAD_DIM, HEAD_DIM)],
                            eye,
                        ],
                        axis=1,
                    )
                    for i in range(at_once)
                ],
                axis=0,
            )
            scores = jnp.concatenate(
                [
                    lax.dot_general(
                        asks,
                        keys[...].reshape(all_keys, depth),
                        across,
                        preferred_element_type=jnp.float32,
                    ),
                    lax.dot_general(
                        asks, turn_keys[which], across, preferred_element_type=jnp.float32
                    ),
                ],
                axis=1,
            )
            peak = jnp.max(scores, axis=1, keepdims=True)
            weights = jnp.exp2((scores - peak) * TO_POWER).astype(jnp.bfloat16)
            summed = jnp.dot(
                weights,
                values[...].reshape(all_keys + 2 * rows, depth),
                preferred_element_type=jnp.float32,
            )
            totals = summed[:, HEAD_DIM:]
            mixed = (summed[:, :HEAD_DIM] / totals).astype(jnp.bfloat16)
            level = peak * TO_POWER + jnp.log2(totals)
            span = pl.ds(batch * at_once * rows, at_once * rows)
            out_ref[span] = mixed
            for i in range(at_once):
                stats = jnp.where(
                    lane == batch * at_once + i, level[i * rows : (i + 1) * rows], stats
                )
        stats = stats.T[:PER_GROUP]
        if asked:
            high = stats.astype(jnp.bfloat16).astype(jnp.float32)
            middle = (stats - high).astype(jnp.bfloat16).astype(jnp.float32)
            low = stats - high - middle
            out_ref[pl.ds(PER_GROUP * rows, STAT_ROWS)] = jnp.concatenate(
                [high, middle, low, jnp.zeros_like(low)], axis=0
            ).astype(jnp.bfloat16)
        else:
            l_ref[...] = stats


def attend(head, sides, seen, tables, after, queries, own_kv, partner_kv, turns):
    rows = queries[0].shape[0]
    pages, page = own_kv[0][0].shape[0], own_kv[0][0].shape[-2]
    counts = tuple(len(choice) for choice in own_kv)
    flat = [array for choice in (*own_kv, *partner_kv) for array in choice]
    all_rows = PER_GROUP * rows
    shapes = []
    for asked in sides:
        extra = STAT_ROWS if asked else 0
        shapes.append(jax.ShapeDtypeStruct((all_rows + extra, HEAD_DIM), jnp.bfloat16))
        if not asked:
            shapes.append(jax.ShapeDtypeStruct((PER_GROUP, rows), jnp.float32))
    asks = [queries[asked] for asked in sides]
    return pl.pallas_call(
        functools.partial(attend_kernel, counts, head, sides),
        in_specs=[scalar] * 5 + [outside] * (3 + len(sides) + len(flat)),
        out_specs=[whole] * len(shapes),
        out_shape=shapes,
        scratch_shapes=[
            pltpu.VMEM((len(sides), rows, PER_GROUP * HEAD_DIM), jnp.bfloat16),
            pltpu.VMEM((2 * pages, page, 2 * HEAD_DIM), jnp.bfloat16),
            pltpu.VMEM((len(sides), 2 * rows, 2 * HEAD_DIM), jnp.bfloat16),
            pltpu.VMEM((2, 2, rows, HEAD_DIM), jnp.bfloat16),
            pltpu.VMEM((2 * pages + 2 * rows // page, page, 2 * HEAD_DIM), jnp.bfloat16),
            pltpu.SemaphoreType.DMA((8,)),
        ],
        compiler_params=params(24),
        cost_estimate=pl.CostEstimate(flops=1, bytes_accessed=1, transcendentals=0),
        name=f"attend_{head}_{len(sides)}_{sides[0]}",
    )(seen, *tables, after, *asks, *turns, *flat)


def merge_kernel(heads, valid_ref, *refs):
    refs = refs[1:]
    out_ref, held, sem = refs[-3:]
    rows = out_ref.shape[0]
    width = PER_GROUP * HEAD_DIM
    place = lax.axis_index("ctx") * rows + lax.broadcasted_iota(jnp.int32, (rows, HEAD_DIM), 0)
    live = place < valid_ref[0]
    copies = []
    for head in range(heads):
        o_ref, l_ref, got_ref = refs[3 * head : 3 * head + 3]
        parts = got_ref[pl.ds(PER_GROUP * rows, STAT_ROWS)].astype(jnp.float32)
        level = parts[:PER_GROUP] + parts[PER_GROUP : 2 * PER_GROUP]
        level = level + parts[2 * PER_GROUP : 3 * PER_GROUP]
        share = 1.0 / (1.0 + jnp.exp2(level - l_ref[...]))
        share = jnp.concatenate(
            [share, jnp.zeros((rows - PER_GROUP, rows), jnp.float32)], axis=0
        ).T
        for member in range(PER_GROUP):
            span = pl.ds(member * rows, rows)
            here = o_ref[span].astype(jnp.float32)
            there = got_ref[span].astype(jnp.float32)
            result = there + share[:, member : member + 1] * (here - there)
            held[:, pl.ds((head * PER_GROUP + member) * HEAD_DIM, HEAD_DIM)] = jnp.where(
                live, result, 0.0
            ).astype(jnp.bfloat16)
        lanes = pl.ds(head * width, width)
        copies.append(pltpu.make_async_copy(held.at[:, lanes], out_ref.at[:, lanes], sem.at[head]))
        copies[-1].start()
    for copy in copies:
        copy.wait()


def merge(after, valid, parts, rows):
    heads = len(parts)
    flat = [array for part in parts for array in part]
    shape = jax.ShapeDtypeStruct((rows, heads * PER_GROUP * HEAD_DIM), jnp.bfloat16)
    return pl.pallas_call(
        functools.partial(merge_kernel, heads),
        in_specs=[scalar, outside] + [whole] * len(flat),
        out_specs=distant,
        out_shape=shape,
        scratch_shapes=[
            pltpu.VMEM(shape.shape, shape.dtype),
            pltpu.SemaphoreType.DMA((heads,)),
        ],
        compiler_params=params(8),
        name="merge",
    )(valid, after, *flat)


def route_blocks(kv_local, state_local, owner_row, index_row):
    parties = lax.axis_size("pool")
    myself = lax.axis_index("pool")
    pages = kv_local.shape[0]
    capacity = max(1, 2 * pages // parties)
    sessions = jnp.arange(parties, dtype=jnp.int32)
    table = (
        (owner_row[:, None] == sessions[None, :]).astype(jnp.int32).reshape(parties, pages, parties)
    )
    before = jnp.cumsum(table, axis=1) - table
    ranks = jnp.sum(before * table, axis=2)
    owners = owner_row.reshape(parties, pages)
    my_owner = lax.dynamic_index_in_dim(owners, myself, 0, keepdims=False)
    device_rank = lax.dynamic_index_in_dim(ranks, myself, 0, keepdims=False)

    def spread(array):
        empty = jnp.zeros((parties, capacity) + array.shape[1:], array.dtype)
        sent = empty.at[my_owner, device_rank].set(array)
        return lax.all_to_all(sent, "pool", split_axis=0, concat_axis=0, tiled=True)

    got_kv, got_state = spread(kv_local), spread(state_local)
    flat_place = (sessions[:, None] * capacity + ranks).reshape(-1)
    target = jnp.where(owner_row == myself, index_row, pages)
    where_from = jnp.zeros((pages,), jnp.int32).at[target].set(flat_place, mode="drop")
    return (
        got_kv.reshape((parties * capacity,) + kv_local.shape[1:])[where_from],
        got_state.reshape((parties * capacity,) + state_local.shape[1:])[where_from],
    )


def local(
    kv_pool,
    state_pool,
    block_owner,
    block_index,
    history_len,
    turn_len,
    mixer_in,
    input_proj,
    output_proj,
    step_size,
    decay_rate,
    bypass_factor,
    queries,
    turn_kv,
):
    parties = lax.axis_size("pool")
    segments = lax.axis_size("ctx")
    kv = kv_pool[0]
    pages = kv.shape[0]
    rows = queries.shape[1]
    heads = kv.shape[-1] // HEAD_DIM
    partner = [(i, i ^ 1) for i in range(segments)]
    opposite = [(i, i ^ 2) for i in range(segments)]

    def to_partner(array):
        return lax.ppermute(array, "ctx", partner)

    def to_opposite(array):
        return lax.ppermute(array, "ctx", opposite)

    if parties == 2:
        swap = [(0, 1), (1, 0)]
        moved, rest = [], kv
        for head in range(heads):
            columns = slice(head * HEAD_DIM, (head + 1) * HEAD_DIM)
            if head == 0:
                cut = (rest[:, 0, :, columns], rest[:, 1, :, columns])
            else:
                cut = (rest[..., columns],)
            cut, rest = lax.optimization_barrier((cut, rest))
            moved.append(tuple(lax.ppermute(piece, "pool", swap) for piece in cut))
        padded = jnp.concatenate([state_pool, state_pool[: pages // 8]], axis=0)
        slab = lax.ppermute(padded, "pool", swap)
        table = (block_owner, block_index)
    else:
        table = (block_owner, jnp.arange(pages, dtype=jnp.int32)[None])
        routed, slab = route_blocks(kv, state_pool, block_owner[0], block_index[0])
        moved = [(routed[..., h * HEAD_DIM : (h + 1) * HEAD_DIM],) for h in range(heads)]
    asks = (queries[0], to_opposite(queries[0]))

    early = [tuple(to_partner(row) for row in table), to_partner(turn_kv[0])]
    if parties == 2:
        early.append(to_partner(kv))
    steps, (table_beside, turn_beside, *kv_beside) = lax.optimization_barrier((step_size[0], early))
    turns = (turn_kv[0], turn_beside)
    tables = table + table_beside
    y, s, run = mixer_from_zero(
        turn_len, mixer_in[0], input_proj[0], output_proj[0], steps, decay_rate, bypass_factor
    )
    parts = []
    after = run
    for head in range(heads):
        came, after = lax.optimization_barrier((moved[head], after))
        own_kv, partner_kv = (came,), (tuple(to_partner(piece) for piece in came),)
        if parties == 2:
            own_kv, partner_kv = ((kv,),) + own_kv, (tuple(kv_beside),) + partner_kv
        ask = functools.partial(
            attend,
            head,
            seen=history_len,
            tables=tables,
            queries=asks,
            own_kv=own_kv,
            partner_kv=partner_kv,
            turns=turns,
        )
        if head + 1 < heads:
            sent, o, after = ask(sides=(1, 0), after=after)
        else:
            (sent,) = ask(sides=(1,), after=after)
            o, after = ask(sides=(0,), after=sent)
        parts.append((o, after, to_opposite(sent)))
    slab, after = lax.optimization_barrier((slab, after))
    slabs = (state_pool, slab) if parties == 2 else (slab,)
    mixed, final, after = add_saved(after, turn_len, table, slabs, y, s, run, output_proj[0])
    attended = merge(after, turn_len, parts, rows)
    return (mixed[None], final[None], attended[None])


def solution(mesh):
    return jax.shard_map(
        local,
        mesh=mesh,
        in_specs=(
            P("ctx", "pool", None, None, "head"),
            P("pool", "ctx", "head"),
            P("ctx", None),
            P("ctx", None),
            P("pool"),
            P("pool"),
            P("pool", "head", "ctx", None),
            P("pool", "head", None, None),
            P("pool", "head", None, None),
            P("pool", "head", None),
            P("head"),
            P("head"),
            P("pool", "ctx", "head"),
            P("pool", None, "ctx", "head"),
        ),
        out_specs=(
            P("pool", "head", "ctx", None),
            P("pool", "head", "ctx", None),
            P("pool", "ctx", "head"),
        ),
        check_vma=False,
    )
```

time: 71.6 us -> 47.7 us (0.67)
  waiting for transfers between devices: 16.8 us -> 1.46 us
  Pallas kernels: 32.6 us -> 26.9 us
  local copies, waits for them, and re-layouts: 8.36 us -> 4.47 us
  starting transfers between devices: 10 us -> 12.2 us
    ppermute x3 -> x4, waiting for transfers between devices: 14.9 us -> 0.33 us  [the longest x3 0.33 us: local(): moved.append(tuple((lax.ppermute(piece, 'pool', swap) for piece in cut)))]
    pallas_call x3 -> x4, Pallas kernels: 21.1 us -> 18.4 us  [the longest x3 17.2 us: attend(): pl.pallas_call(functools.partial(attend_kernel, counts, head, sides), in_...]
    ppermute x3 -> x4, starting transfers between devices: 4.85 us -> 6.91 us  [the longest x3 5.1 us: local(): moved.append(tuple((lax.ppermute(piece, 'pool', swap) for piece in cut)))]
    pallas_call x1, Pallas kernels: 8.49 us -> 6.62 us  [mixer_from_zero(): pl.pallas_call(mixer_kernel, grid=(groups,), in_specs=[scalar, pl.BlockSp...]
    unnamed x30 -> x24, local copies, waits for them, and re-layouts: 4.29 us -> 2.56 us
    broadcast_in_dim x2 -> x0, local copies, waits for them, and re-layouts: 1.38 us -> none  [the longest x1 0.69 us: mixer_from_zero(): rates[:, None]]
    pallas_call x1, Pallas kernels: 3.06 us -> 1.86 us  [add_saved(): pl.pallas_call(functools.partial(saved_kernel, len(slabs)), in_specs=[sca...]
    ppermute x6 -> x7, waiting for transfers between devices: 1.87 us -> 0.74 us  [to_partner(): return lax.ppermute(array, 'ctx', partner)]
  transfers between devices with their start and end apart: 12 -> 14, of which waited for: 4 -> 4; matrix products, arithmetic and copies ran while one was open for 5% -> 3% of each run, Pallas kernels for 42% -> 54%
where the time goes in v2:
time: 47.7 us; the launch traced here: 47.4 us
  Pallas kernels  26.9 us (56%)
  starting transfers between devices  12.2 us (26%)
  local copies, waits for them, and re-layouts  4.47 us (9%)
  between operations  2.31 us (5%)
  waiting for transfers between devices  1.46 us (3%)
    pallas_call x3, Pallas kernels, attend(): pl.pallas_call(functools.partial(attend_kernel, counts, head, sides), in_...  17.2 us
    pallas_call x1, Pallas kernels, mixer_from_zero(): pl.pallas_call(mixer_kernel, grid=(groups,), in_specs=[scalar, pl.BlockSp...  6.62 us
    ppermute x3, starting transfers between devices, local(): moved.append(tuple((lax.ppermute(piece, 'pool', swap) for piece in cut)))  5.1 us
    ppermute x3, starting transfers between devices, to_opposite(): return lax.ppermute(array, 'ctx', opposite)  3.58 us
    unnamed x24, local copies, waits for them, and re-layouts  2.56 us
    pallas_call x1, Pallas kernels, add_saved(): pl.pallas_call(functools.partial(saved_kernel, len(slabs)), in_specs=[sca...  1.86 us
    ppermute x1, starting transfers between devices, local(): slab = lax.ppermute(padded, 'pool', swap)  1.81 us
    ppermute x7, starting transfers between devices, to_partner(): return lax.ppermute(array, 'ctx', partner)  1.68 us
  transfers between devices with their start and end apart: 14, of which 4 were waited for; matrix products, arithmetic and copies ran while one was open for 3% of the time, Pallas kernels for 54%

profile of v2, /device:TPU:0, one launch (start us, length us, event | category | flops | bytes accessed | tf_op | source)
XLA Modules:
  0.0 47.4 jit_solution(260170791154091155)
XLA Ops:
  0.6 0.5 %collective-permute-start.4 = (bf16[32,2,32,256]{3,2,1,0:T(8,128)(2,1)}, bf16[32,2,32,256]{3,2,1,0:T(8,128)(2,1)S(1)}, u32[]{:S(2)}, u32[]{:S(2)}) collective-permute-start(bf16[32,2,32,256]{3,2,1,0:T(8,128)(2,1)} %bitcast.16), channel_id=1, source_target_pairs={{0,4},{4,0},{8,12},{12,8},{1,5},{5,1},{9,13},{13,9},{2,6},{6,2},{1... | collective-permute-start | bytes 3145736 | tf_op jit(solution)/shard_map/ppermute | solution.py:490
  1.2 0.1 collective-permute-start.3
  1.2 0.4 collective-permute-start.1
  1.7 0.1 collective-permute-start.2
  1.7 1.1 %slice_bitcast_fusion = (bf16[32,32,128]{2,1,0:T(8,128)(2,1)S(1)}, bf16[32,32,128]{2,1,0:T(8,128)(2,1)S(1)}) fusion(bf16[32,2,32,256]{3,2,1,0:T(8,128)(2,1)} %bitcast.17), kind=kLoop, calls=%fused_computation.1 | loop fusion | bytes 1048576 | tf_op jit(solution)/shard_map/squeeze | solution.py:501
  2.8 3.0 %collective-permute-start.6 = (bf16[32,32,128]{2,1,0:T(8,128)(2,1)S(1)}, bf16[32,32,128]{2,1,0:T(8,128)(2,1)S(1)}, u32[]{:S(2)}, u32[]{:S(2)}) collective-permute-start(bf16[32,32,128]{2,1,0:T(8,128)(2,1)S(1)} %get-tuple-element.34), channel_id=1, source_target_pairs={{0,16},{16,0},{1,17},{17,1},{2,18},{18,2},{3,19},{19,3},{4,20},{20... | collective-permute-start | bytes 786440 | tf_op jit(solution)/shard_map/ppermute | solution.py:505
  5.8 0.0 collective-permute-done.1.refs_2_
  5.8 0.9 %collective-permute-start.7 = (bf16[32,32,128]{2,1,0:T(8,128)(2,1)S(1)}, bf16[32,32,128]{2,1,0:T(8,128)(2,1)S(1)}, u32[]{:S(2)}, u32[]{:S(2)}) collective-permute-start(bf16[32,32,128]{2,1,0:T(8,128)(2,1)S(1)} %get-tuple-element.35), channel_id=1, source_target_pairs={{0,16},{16,0},{1,17},{17,1},{2,18},{18,2},{3,19},{19,3},{4,20},{20... | collective-permute-start | bytes 786440 | tf_op jit(solution)/shard_map/ppermute | solution.py:505
  6.7 0.0 collective-permute-done.2.refs_3_
  6.7 1.5 %collective-permute-start.8 = (bf16[128,2048]{1,0:T(8,128)(2,1)}, bf16[128,2048]{1,0:T(8,128)(2,1)S(1)}, u32[]{:S(2)}, u32[]{:S(2)}) collective-permute-start(bf16[128,2048]{1,0:T(8,128)(2,1)} %bitcast.24), channel_id=1, source_target_pairs={{0,8},{4,12},{8,0},{12,4},{1,9},{5,13},{9,1},{13,5},{2,10},{6,14},... | collective-permute-start | bytes 1572872 | tf_op jit(solution)/shard_map/ppermute | solution.py:493
  8.2 0.0 copy-done
  8.2 0.1 slice.15
  8.3 0.0 collective-permute-done.3.refs_8_.refs_7_
  8.4 1.2 %collective-permute-start.5 = (bf16[32,2,32,128]{3,2,1,0:T(8,128)(2,1)S(1)}, bf16[32,2,32,128]{3,2,1,0:T(8,128)(2,1)S(1)}, u32[]{:S(2)}, u32[]{:S(2)}) collective-permute-start(bf16[32,2,32,128]{3,2,1,0:T(8,128)(2,1)S(1)} %slice.15), channel_id=1, source_target_pairs={{0,16},{16,0},{1,17},{17,1},{2,18},{18,2},{3,19},{19,3},{4,20},{20... | collective-permute-start | bytes 1572872 | tf_op jit(solution)/shard_map/ppermute | solution.py:505
  10.2 0.0 collective-permute-done.4.refs_12_.refs_10_
  10.2 0.0 copy-start.10
  10.2 0.0 copy-start.11
  10.3 0.6 %copy-done.10 = f32[32]{0:T(128)S(1)} copy-done((f32[32]{0:T(128)S(1)}, f32[32]{0:T(128)}, u32[]{:S(2)}) %copy-start.10) | copy-done | bytes 152
  10.9 0.0 copy-done.11
  10.9 1.0 %copy-done.6 = bf16[1,2,256,512]{3,2,1,0:T(8,128)(2,1)S(1)} copy-done((bf16[1,2,256,512]{3,2,1,0:T(8,128)(2,1)S(1)}, bf16[1,2,256,512]{3,2,1,0:T(8,128)(2,1)}, u32[]{:S(2)}) %copy-start.6) | copy-done | bytes 524312
  11.9 0.8 %copy-done.7 = f32[1,32,512]{2,1,0:T(8,128)S(1)} copy-done((f32[1,32,512]{2,1,0:T(8,128)S(1)}, f32[1,32,512]{2,1,0:T(8,128)}, u32[]{:S(2)}) %copy-start.7) | copy-done | bytes 65560
  12.8 6.6 %mixer_from_zero.1 = (f32[32,16,512]{2,1,0:T(8,128)S(1)}, f32[32,16,256]{2,1,0:T(8,128)S(1)}, f32[32,512]{1,0:T(8,128)S(1)}) custom-call(s32[1]{0:T(128)S(6)} %copy.18.valid_ref, bf16[32,16,512]{2,1,0:T(8,128)(2,1)S(1)} %bitcast.31, bf16[2,256,512]{2,1,0:T(8,128)(2,1)S(1)} %bitcast.32, bf16[2,256,512]{2,1,0:T(8,128)(2,1)S(1)} %bitcast.22, ...), custom_call_target="tpu_custom_call" | custom-call | flops 1 | bytes 1 | tf_op jit(solution)/shard_map/mixer_from_zero/pallas_call | solution.py:100
  19.4 0.0 collective-permute-done.6.refs_10_
  19.4 0.0 collective-permute-done.7.refs_11_
  19.4 0.0 copy-start.8
  19.4 0.0 copy-start.9
  19.4 0.1 collective-permute-start.10
  19.5 0.5 %collective-permute-start.9 = (bf16[32,32,128]{2,1,0:T(8,128)(2,1)S(1)}, bf16[32,32,128]{2,1,0:T(8,128)(2,1)S(1)}, u32[]{:S(2)}, u32[]{:S(2)}) collective-permute-start(bf16[32,32,128]{2,1,0:T(8,128)(2,1)S(1)} %collective-permute-done.6.refs_10_), channel_id=1, source_target_pairs={{0,4},{4,0},{8,12},{12,8},{1,5},{5,1},{9,13},{13,9},{2,6},{6,2},{1... | collective-permute-start | bytes 786440 | tf_op jit(solution)/shard_map/ppermute | solution.py:490
  20.7 0.0 copy-start.3
  20.7 0.0 collective-permute-done.8.refs_5_
  20.7 0.4 collective-permute-done.10.refs_14_
  21.0 0.4 collective-permute-done.9.refs_13_
  21.4 0.0 copy-done.9
  21.4 7.5 %attend_0_2_1.1 = (bf16[1056,128]{1,0:T(8,128)(2,1)S(1)}, bf16[1024,128]{1,0:T(8,128)(2,1)S(1)}, f32[8,128]{1,0:T(8,128)S(1)}) custom-call(s32[1]{0:T(128)S(6)} %copy.17.seen_ref, s32[1,64]{1,0:T(1,128)S(1)} %copy-done.8, s32[1,64]{1,0:T(1,128)S(1)} %copy-done.9, s32[1,64]{1,0:T(1,128)S(1)} %collective-permute-done.1.refs_2_, ...), custom_call_target="tpu_custom_call" | custom-call | flops 1 | bytes 1 | tf_op jit(solution)/shard_map/attend_0_2_1/pallas_call | solution.py:365
  28.9 0.3 collective-permute-done.5.refs_9_
  29.2 0.0 collective-permute-start.11
  29.2 0.7 %slice-done = bf16[4,16,256]{2,1,0:T(8,128)(2,1)S(1)} async-done(((bf16[32,16,256]{2,1,0:T(8,128)(2,1)}), bf16[4,16,256]{2,1,0:T(8,128)(2,1)S(1)}, s32[]{:S(2)}) %slice-start) | async-done | bytes 32792 | tf_op jit(solution)/shard_map/slice | solution.py:506
  30.0 1.8 %collective-permute-start = (bf16[36,16,256]{2,1,0:T(8,128)(2,1)S(1)}, bf16[36,16,256]{2,1,0:T(8,128)(2,1)S(1)}, u32[]{:S(2)}, u32[]{:S(2)}) collective-permute-start(bf16[36,16,256]{2,1,0:T(8,128)(2,1)S(1)} %pad_maximum_fusion), channel_id=1, source_target_pairs={{0,16},{16,0},{1,17},{17,1},{2,18},{18,2},{3,19},{19,3},{4,20},{20... | collective-permute-start | bytes 884744 | tf_op jit(solution)/shard_map/ppermute | solution.py:507
  31.8 1.5 %collective-permute-start.12 = (bf16[1056,128]{1,0:T(8,128)(2,1)S(1)}, bf16[1056,128]{1,0:T(8,128)(2,1)S(1)}, u32[]{:S(2)}, u32[]{:S(2)}) collective-permute-start(bf16[1056,128]{1,0:T(8,128)(2,1)S(1)} %get-tuple-element.55), channel_id=1, source_target_pairs={{0,8},{4,12},{8,0},{12,4},{1,9},{5,13},{9,1},{13,5},{2,10},{6,14},... | collective-permute-start | bytes 811016 | tf_op jit(solution)/shard_map/ppermute | solution.py:493
  33.3 0.0 collective-permute-done.11.refs_11_
  33.3 5.0 %attend_1_1_1.1.refs_4_ = bf16[1056,128]{1,0:T(8,128)(2,1)S(1)} custom-call(s32[1]{0:T(128)S(6)} %copy.17.seen_ref, s32[1,64]{1,0:T(1,128)S(1)} %copy-done.8, s32[1,64]{1,0:T(1,128)S(1)} %copy-done.9, s32[1,64]{1,0:T(1,128)S(1)} %collective-permute-done.1.refs_2_, s32[1,64]{1,0:T(1,128)S(1)} %collective-permute-done.2.refs_3_, ...), custom_call_target="tpu_custom_call" | custom-call | flops 1 | bytes 1 | tf_op jit(solution)/shard_map/attend_1_1_1/pallas_call | solution.py:365
  38.3 0.6 %collective-permute-start.13 = (bf16[1056,128]{1,0:T(8,128)(2,1)S(1)}, bf16[1056,128]{1,0:T(8,128)(2,1)S(1)}, u32[]{:S(2)}, u32[]{:S(2)}) collective-permute-start(bf16[1056,128]{1,0:T(8,128)(2,1)S(1)} %attend_1_1_1.1.refs_4_), channel_id=1, source_target_pairs={{0,8},{4,12},{8,0},{12,4},{1,9},{5,13},{9,1},{13,5},{2,10},{6,14},... | collective-permute-start | bytes 811016 | tf_op jit(solution)/shard_map/ppermute | solution.py:493
  38.9 4.8 %attend_1_1_0.1 = (bf16[1024,128]{1,0:T(8,128)(2,1)S(1)}, f32[8,128]{1,0:T(8,128)S(1)}) custom-call(s32[1]{0:T(128)S(6)} %copy.17.seen_ref, s32[1,64]{1,0:T(1,128)S(1)} %copy-done.8, s32[1,64]{1,0:T(1,128)S(1)} %copy-done.9, s32[1,64]{1,0:T(1,128)S(1)} %collective-permute-done.1.refs_2_, s32[1,64]{1,0:T(1,128)S(1)} %collective-permute-done.2.refs_3_, ...), custom_call_target="tpu_custom_call" | custom-call | flops 1 | bytes 1 | tf_op jit(solution)/shard_map/attend_1_1_0/pallas_call | solution.py:365
  43.7 0.0 collective-permute-done.refs_2_
  43.7 1.9 %add_saved.1 = (bf16[32,16,512]{2,1,0:T(8,128)(2,1)}, f32[32,16,256]{2,1,0:T(8,128)}, f32[8,128]{1,0:T(8,128)S(1)}) custom-call(s32[1]{0:T(128)S(6)} %copy.18.valid_ref, s32[1,64]{1,0:T(1,128)S(1)} %copy-done.8, s32[1,64]{1,0:T(1,128)S(1)} %copy-done.9, f32[8,128]{1,0:T(8,128)S(1)} %get-tuple-element.47.refs_0_.refs_5_, bf16[32,16,256]{2,1,0:T(8,128)(2,1)S(1)} %copy-done.3, ...), custom_call_target="tpu_custom_call" | custom-call | flops 1 | bytes 1 | tf_op jit(solution)/shard_map/add_saved/pallas_call | solution.py:172
  45.5 0.0 collective-permute-done.12.refs_3_
  45.6 0.4 collective-permute-done.13.refs_6_
  45.9 1.2 %merge.1 = bf16[128,2048]{1,0:T(8,128)(2,1)} custom-call(s32[1]{0:T(128)S(6)} %copy.18.valid_ref, f32[8,128]{1,0:T(8,128)S(1)} %get-tuple-element.53.refs_0_, bf16[1024,128]{1,0:T(8,128)(2,1)S(1)} %get-tuple-element.54.refs_1_, f32[8,128]{1,0:T(8,128)S(1)} %get-tuple-element.44.refs_4_.refs_2_, bf16[1056,128]{1,0:T(8,128)(2,1)S(1)} %collective-permute-done.12.refs_3_, ...), custom_call_target="tpu_custom_call" | custom-call | tf_op jit(solution)/shard_map/merge/pallas_call | solution.py:420
  (15 shorter events, 0.1 us)
Async XLA Ops:
  0.6 7.6 %copy-start = (bf16[1,32,2,32,256]{4,3,2,1,0:T(8,128)(2,1)S(1)}, bf16[1,32,2,32,256]{4,3,2,1,0:T(8,128)(2,1)}, u32[]{:S(2)}) copy-start(bf16[1,32,2,32,256]{4,3,2,1,0:T(8,128)(2,1)} %param.14) | copy-start | bytes 3145732
  0.6 9.6 %collective-permute-start.4 = (bf16[32,2,32,256]{3,2,1,0:T(8,128)(2,1)}, bf16[32,2,32,256]{3,2,1,0:T(8,128)(2,1)S(1)}, u32[]{:S(2)}, u32[]{:S(2)}) collective-permute-start(bf16[32,2,32,256]{3,2,1,0:T(8,128)(2,1)} %bitcast.16), channel_id=1, source_target_pairs={{0,4},{4,0},{8,12},{12,8},{1,5},{5,1},{9,13},{13,9},{2,6},{6,2},{1... | collective-permute-start | bytes 3145736 | tf_op jit(solution)/shard_map/ppermute | solution.py:490
  1.2 7.2 %collective-permute-start.3 = (bf16[2,128,256]{2,1,0:T(8,128)(2,1)}, bf16[2,128,256]{2,1,0:T(8,128)(2,1)S(1)}, u32[]{:S(2)}, u32[]{:S(2)}) collective-permute-start(bf16[2,128,256]{2,1,0:T(8,128)(2,1)} %bitcast.27), channel_id=1, source_target_pairs={{0,4},{4,0},{8,12},{12,8},{1,5},{5,1},{9,13},{13,9},{2,6},{6,2},{1... | collective-permute-start | bytes 393224 | tf_op jit(solution)/shard_map/ppermute | solution.py:490
  1.2 4.6 %collective-permute-start.1 = (s32[1,64]{1,0:T(1,128)}, s32[1,64]{1,0:T(1,128)S(1)}, u32[]{:S(2)}, u32[]{:S(2)}) collective-permute-start(s32[1,64]{1,0:T(1,128)} %owner_ref.1), channel_id=1, source_target_pairs={{0,4},{4,0},{8,12},{12,8},{1,5},{5,1},{9,13},{13,9},{2,6},{6,2},{1... | collective-permute-start | bytes 776 | tf_op jit(solution)/shard_map/ppermute | solution.py:490
  1.7 5.1 %collective-permute-start.2 = (s32[1,64]{1,0:T(1,128)}, s32[1,64]{1,0:T(1,128)S(1)}, u32[]{:S(2)}, u32[]{:S(2)}) collective-permute-start(s32[1,64]{1,0:T(1,128)} %place_ref.1), channel_id=1, source_target_pairs={{0,4},{4,0},{8,12},{12,8},{1,5},{5,1},{9,13},{13,9},{2,6},{6,2},{1... | collective-permute-start | bytes 776 | tf_op jit(solution)/shard_map/ppermute | solution.py:490
  2.8 16.6 %collective-permute-start.6 = (bf16[32,32,128]{2,1,0:T(8,128)(2,1)S(1)}, bf16[32,32,128]{2,1,0:T(8,128)(2,1)S(1)}, u32[]{:S(2)}, u32[]{:S(2)}) collective-permute-start(bf16[32,32,128]{2,1,0:T(8,128)(2,1)S(1)} %get-tuple-element.34), channel_id=1, source_target_pairs={{0,16},{16,0},{1,17},{17,1},{2,18},{18,2},{3,19},{19,3},{4,20},{20... | collective-permute-start | bytes 786440 | tf_op jit(solution)/shard_map/ppermute | solution.py:505
  5.8 13.6 %collective-permute-start.7 = (bf16[32,32,128]{2,1,0:T(8,128)(2,1)S(1)}, bf16[32,32,128]{2,1,0:T(8,128)(2,1)S(1)}, u32[]{:S(2)}, u32[]{:S(2)}) collective-permute-start(bf16[32,32,128]{2,1,0:T(8,128)(2,1)S(1)} %get-tuple-element.35), channel_id=1, source_target_pairs={{0,16},{16,0},{1,17},{17,1},{2,18},{18,2},{3,19},{19,3},{4,20},{20... | collective-permute-start | bytes 786440 | tf_op jit(solution)/shard_map/ppermute | solution.py:505
  6.7 3.5 %copy-start.1 = (bf16[1,2,256,512]{3,2,1,0:T(8,128)(2,1)S(1)}, bf16[1,2,256,512]{3,2,1,0:T(8,128)(2,1)}, u32[]{:S(2)}) copy-start(bf16[1,2,256,512]{3,2,1,0:T(8,128)(2,1)} %param.22) | copy-start | bytes 1572868
  6.7 3.5 %copy-start.5 = (bf16[1,32,16,512]{3,2,1,0:T(8,128)(2,1)S(1)}, bf16[1,32,16,512]{3,2,1,0:T(8,128)(2,1)}, u32[]{:S(2)}) copy-start(bf16[1,32,16,512]{3,2,1,0:T(8,128)(2,1)} %param.20) | copy-start | bytes 1572868
  6.7 14.0 %collective-permute-start.8 = (bf16[128,2048]{1,0:T(8,128)(2,1)}, bf16[128,2048]{1,0:T(8,128)(2,1)S(1)}, u32[]{:S(2)}, u32[]{:S(2)}) collective-permute-start(bf16[128,2048]{1,0:T(8,128)(2,1)} %bitcast.24), channel_id=1, source_target_pairs={{0,8},{4,12},{8,0},{12,4},{1,9},{5,13},{9,1},{13,5},{2,10},{6,14},... | collective-permute-start | bytes 1572872 | tf_op jit(solution)/shard_map/ppermute | solution.py:493
  8.4 20.9 %collective-permute-start.5 = (bf16[32,2,32,128]{3,2,1,0:T(8,128)(2,1)S(1)}, bf16[32,2,32,128]{3,2,1,0:T(8,128)(2,1)S(1)}, u32[]{:S(2)}, u32[]{:S(2)}) collective-permute-start(bf16[32,2,32,128]{3,2,1,0:T(8,128)(2,1)S(1)} %slice.15), channel_id=1, source_target_pairs={{0,16},{16,0},{1,17},{17,1},{2,18},{18,2},{3,19},{19,3},{4,20},{20... | collective-permute-start | bytes 1572872 | tf_op jit(solution)/shard_map/ppermute | solution.py:505
  10.2 0.7 %copy-start.10 = (f32[32]{0:T(128)S(1)}, f32[32]{0:T(128)}, u32[]{:S(2)}) copy-start(f32[32]{0:T(128)} %param.24) | copy-start | bytes 388
  10.2 0.7 %copy-start.11 = (f32[32]{0:T(128)S(1)}, f32[32]{0:T(128)}, u32[]{:S(2)}) copy-start(f32[32]{0:T(128)} %param.25) | copy-start | bytes 388
  10.9 1.0 %copy-start.6 = (bf16[1,2,256,512]{3,2,1,0:T(8,128)(2,1)S(1)}, bf16[1,2,256,512]{3,2,1,0:T(8,128)(2,1)}, u32[]{:S(2)}) copy-start(bf16[1,2,256,512]{3,2,1,0:T(8,128)(2,1)} %param.21) | copy-start | bytes 1572868
  11.9 0.8 %copy-start.7 = (f32[1,32,512]{2,1,0:T(8,128)S(1)}, f32[1,32,512]{2,1,0:T(8,128)}, u32[]{:S(2)}) copy-start(f32[1,32,512]{2,1,0:T(8,128)} %param.23) | copy-start | bytes 196612
  12.8 8.7 %copy-start.2 = (bf16[1,128,2048]{2,1,0:T(8,128)(2,1)S(1)}, bf16[1,128,2048]{2,1,0:T(8,128)(2,1)}, u32[]{:S(2)}) copy-start(bf16[1,128,2048]{2,1,0:T(8,128)(2,1)} %param.26) | copy-start | bytes 1572868
  12.8 8.7 %copy-start.4 = (bf16[1,2,128,256]{3,2,1,0:T(8,128)(2,1)S(1)}, bf16[1,2,128,256]{3,2,1,0:T(8,128)(2,1)}, u32[]{:S(2)}) copy-start(bf16[1,2,128,256]{3,2,1,0:T(8,128)(2,1)} %param.27) | copy-start | bytes 393220
  19.4 2.0 %copy-start.8 = (s32[1,64]{1,0:T(1,128)S(1)}, s32[1,64]{1,0:T(1,128)}, u32[]{:S(2)}) copy-start(s32[1,64]{1,0:T(1,128)} %owner_ref.1) | copy-start | bytes 772
  19.4 2.0 %copy-start.9 = (s32[1,64]{1,0:T(1,128)S(1)}, s32[1,64]{1,0:T(1,128)}, u32[]{:S(2)}) copy-start(s32[1,64]{1,0:T(1,128)} %place_ref.1) | copy-start | bytes 772
  19.4 1.6 %collective-permute-start.10 = (bf16[32,32,128]{2,1,0:T(8,128)(2,1)S(1)}, bf16[32,32,128]{2,1,0:T(8,128)(2,1)S(1)}, u32[]{:S(2)}, u32[]{:S(2)}) collective-permute-start(bf16[32,32,128]{2,1,0:T(8,128)(2,1)S(1)} %collective-permute-done.7.refs_11_), channel_id=1, source_target_pairs={{0,4},{4,0},{8,12},{12,8},{1,5},{5,1},{9,13},{13,9},{2,6},{6,2},{1... | collective-permute-start | bytes 786440 | tf_op jit(solution)/shard_map/ppermute | solution.py:490
  19.5 1.9 %collective-permute-start.9 = (bf16[32,32,128]{2,1,0:T(8,128)(2,1)S(1)}, bf16[32,32,128]{2,1,0:T(8,128)(2,1)S(1)}, u32[]{:S(2)}, u32[]{:S(2)}) collective-permute-start(bf16[32,32,128]{2,1,0:T(8,128)(2,1)S(1)} %collective-permute-done.6.refs_10_), channel_id=1, source_target_pairs={{0,4},{4,0},{8,12},{12,8},{1,5},{5,1},{9,13},{13,9},{2,6},{6,2},{1... | collective-permute-start | bytes 786440 | tf_op jit(solution)/shard_map/ppermute | solution.py:490
  20.7 8.6 %copy-start.3 = (bf16[32,16,256]{2,1,0:T(8,128)(2,1)S(1)}, bf16[32,16,256]{2,1,0:T(8,128)(2,1)}, u32[]{:S(2)}) copy-start(bf16[32,16,256]{2,1,0:T(8,128)(2,1)} %refs_1_.7) | copy-start | bytes 786436
  29.2 0.8 %slice-start = ((bf16[32,16,256]{2,1,0:T(8,128)(2,1)}), bf16[4,16,256]{2,1,0:T(8,128)(2,1)S(1)}, s32[]{:S(2)}) async-start(bf16[32,16,256]{2,1,0:T(8,128)(2,1)} %refs_1_.7), calls=%async_computation | async-start | bytes 65536 | tf_op jit(solution)/shard_map/slice | solution.py:506
  29.2 4.1 %collective-permute-start.11 = (bf16[32,2,32,128]{3,2,1,0:T(8,128)(2,1)S(1)}, bf16[32,2,32,128]{3,2,1,0:T(8,128)(2,1)S(1)}, u32[]{:S(2)}, u32[]{:S(2)}) collective-permute-start(bf16[32,2,32,128]{3,2,1,0:T(8,128)(2,1)S(1)} %collective-permute-done.5.refs_9_), channel_id=1, source_target_pairs={{0,4},{4,0},{8,12},{12,8},{1,5},{5,1},{9,13},{13,9},{2,6},{6,2},{1... | collective-permute-start | bytes 1572872 | tf_op jit(solution)/shard_map/ppermute | solution.py:490
  30.0 13.7 %collective-permute-start = (bf16[36,16,256]{2,1,0:T(8,128)(2,1)S(1)}, bf16[36,16,256]{2,1,0:T(8,128)(2,1)S(1)}, u32[]{:S(2)}, u32[]{:S(2)}) collective-permute-start(bf16[36,16,256]{2,1,0:T(8,128)(2,1)S(1)} %pad_maximum_fusion), channel_id=1, source_target_pairs={{0,16},{16,0},{1,17},{17,1},{2,18},{18,2},{3,19},{19,3},{4,20},{20... | collective-permute-start | bytes 884744 | tf_op jit(solution)/shard_map/ppermute | solution.py:507
  31.8 13.7 %collective-permute-start.12 = (bf16[1056,128]{1,0:T(8,128)(2,1)S(1)}, bf16[1056,128]{1,0:T(8,128)(2,1)S(1)}, u32[]{:S(2)}, u32[]{:S(2)}) collective-permute-start(bf16[1056,128]{1,0:T(8,128)(2,1)S(1)} %get-tuple-element.55), channel_id=1, source_target_pairs={{0,8},{4,12},{8,0},{12,4},{1,9},{5,13},{9,1},{13,5},{2,10},{6,14},... | collective-permute-start | bytes 811016 | tf_op jit(solution)/shard_map/ppermute | solution.py:493
  38.3 7.7 %collective-permute-start.13 = (bf16[1056,128]{1,0:T(8,128)(2,1)S(1)}, bf16[1056,128]{1,0:T(8,128)(2,1)S(1)}, u32[]{:S(2)}, u32[]{:S(2)}) collective-permute-start(bf16[1056,128]{1,0:T(8,128)(2,1)S(1)} %attend_1_1_1.1.refs_4_), channel_id=1, source_target_pairs={{0,8},{4,12},{8,0},{12,4},{1,9},{5,13},{9,1},{13,5},{2,10},{6,14},... | collective-permute-start | bytes 811016 | tf_op jit(solution)/shard_map/ppermute | solution.py:493

commit v3 on v2

--- a/solution.py
+++ b/solution.py
@@ -15,6 +15,9 @@
 HIDDEN = -1e30
 TO_POWER = (HEAD_DIM**-0.5) * 1.4426950408889634
 STAT_ROWS = 32
+SPARE_ROWS = 48
+CHUNK = 768
+OWNER = 65536
 
 whole = pl.BlockSpec(memory_space=pltpu.VMEM)
 scalar = pl.BlockSpec(memory_space=pltpu.SMEM)
@@ -26,11 +29,11 @@
     return pltpu.CompilerParams(vmem_limit_bytes=mib * 2**20)
 
 
-def locate(kinds, owner_ref, pages):
+def locate(kinds, table_ref, pages):
     if kinds == 1:
         return 0, 0
     myself = lax.axis_index("pool")
-    kind = jnp.where(owner_ref[0, myself * pages] == myself, 0, 1).astype(jnp.int32)
+    kind = jnp.where(table_ref[0, myself * pages] // OWNER == myself, 0, 1).astype(jnp.int32)
     return kind, jnp.where(kind == 0, myself, 1 - myself) * pages
 
 
@@ -125,7 +128,7 @@
     )(valid, x, b, c, dt, rates[None], gains[None])
 
 
-def saved_kernel(kinds, valid_ref, owner_ref, place_ref, *refs):
+def saved_kernel(kinds, valid_ref, chosen_ref, *refs):
     refs = refs[1:]
     slabs = refs[:kinds]
     y_ref, s_ref, run_ref, c_ref, out_ref, final_ref, done_ref, start, mixed, final, sems = refs[
@@ -136,27 +139,28 @@
     groups, states, _ = c_ref.shape
     per = heads // groups
     copies = []
-    chosen, source = locate(kinds, owner_ref, heads)
+    chosen = jnp.max(chosen_ref[0])
     for kind in range(kinds):
 
         @pl.when(chosen == kind)
         def _():
-            for slot in range(heads):
-                start[place_ref[0, source + slot]] = slabs[kind][slot]
+            start[...] = slabs[kind][:heads]
 
     live = lax.broadcasted_iota(jnp.int32, (1, 1, total), 2) < valid_ref[0]
-    for group in range(groups):
-        mine = slice(group * per, (group + 1) * per)
+    some = per // 2
+    for part in range(2 * groups):
+        group = part // 2
+        mine = slice(part * some, (part + 1) * some)
         saved = start[mine]
         fade = jnp.exp(run_ref[mine, :])
         read = jnp.dot(
-            saved.reshape(per * chans, states), c_ref[group], preferred_element_type=jnp.float32
-        ).reshape(per, chans, total)
+            saved.reshape(some * chans, states), c_ref[group], preferred_element_type=jnp.float32
+        ).reshape(some, chans, total)
         result = y_ref[mine] + fade[:, None, :] * read
         mixed[mine] = jnp.where(live, result, 0.0).astype(jnp.bfloat16)
         kept = fade[:, None, total - 1 :]
         final[mine] = s_ref[mine] + kept * saved.astype(jnp.float32)
-        span = pl.ds(group * per, per)
+        span = pl.ds(part * some, some)
         for held, target in ((mixed, out_ref), (final, final_ref)):
             copies.append(
                 pltpu.make_async_copy(held.at[span], target.at[span], sems.at[len(copies)])
@@ -166,12 +170,12 @@
         copy.wait()
 
 
-def add_saved(after, valid, rows, slabs, y, s, run, c):
+def add_saved(after, valid, chosen, slabs, y, s, run, c):
     heads, chans, total = y.shape
     groups, states, _ = c.shape
     return pl.pallas_call(
         functools.partial(saved_kernel, len(slabs)),
-        in_specs=[scalar] * 3 + [outside] + [whole] * (len(slabs) + 4),
+        in_specs=[scalar, whole, outside] + [whole] * (len(slabs) + 4),
         out_specs=[distant, distant, whole],
         out_shape=[
             jax.ShapeDtypeStruct((heads, chans, total), jnp.bfloat16),
@@ -182,18 +186,23 @@
             pltpu.VMEM((heads, chans, states), jnp.bfloat16),
             pltpu.VMEM((heads, chans, total), jnp.bfloat16),
             pltpu.VMEM((heads, chans, states), jnp.float32),
-            pltpu.SemaphoreType.DMA((2 * groups,)),
+            pltpu.SemaphoreType.DMA((4 * groups,)),
         ],
         compiler_params=params(12),
         cost_estimate=pl.CostEstimate(flops=1, bytes_accessed=1, transcendentals=0),
         name="add_saved",
-    )(valid, *rows, after, *slabs, y, s, run, c)
-
-
-def attend_kernel(counts, head, sides, seen_ref, *refs):
-    rows_refs, refs = (refs[0:2], refs[2:4]), refs[4:]
+    )(valid, chosen, after, *slabs, y, s, run, c)
+
+
+def attend_kernel(counts, head, sides, padding, *refs):
+    if head == 0:
+        seen_ref, table_refs, refs = refs[0], refs[1:3], refs[3:]
+    else:
+        hidden_ref, chosen_ref, refs = refs[0], refs[1], refs[2:]
     refs = refs[1:]
     q_refs, turn_refs, refs = refs[: len(sides)], refs[len(sides) : len(sides) + 2], refs[len(sides) + 2 :]
+    if padding:
+        state_ref, refs = refs[0], refs[1:]
     kinds = len(counts)
     kv_refs = ([], [])
     for side in range(2):
@@ -205,61 +214,59 @@
         out_refs[asked], refs = refs[0], refs[1:]
         if asked == 0:
             l_ref, refs = refs[0], refs[1:]
-    queries, keys, turn_keys, turn_raw, values, sems = refs
-    pages, page = kv_refs[0][0][0].shape[0], kv_refs[0][0][0].shape[-2]
+    if padding:
+        padded_ref, refs = refs[0], refs[1:]
+        mine = lax.axis_index("pool") * state_ref.shape[0]
+        for slot in range(state_ref.shape[0]):
+            padded_ref[table_refs[0][0, mine + slot] % OWNER] = state_ref[slot]
+        padded_ref[-padding:] = state_ref[:padding]
+    if head == 0:
+        hidden_ref, chosen_ref, refs = refs[0], refs[1], refs[2:]
+    keys, turn_keys, values = refs
+    pages, page = keys.shape[0] // 2, keys.shape[1]
     rows = q_refs[0].shape[0]
     history = pages * page
     width = PER_GROUP * HEAD_DIM
     segment = lax.axis_index("ctx")
     numbers = (segment, segment ^ 1)
-    found = [locate(kinds, rows_refs[side][0], pages) for side in range(2)]
-    columns = pl.ds(head * HEAD_DIM, HEAD_DIM)
-    copies = [
-        pltpu.make_async_copy(q_ref.at[:, pl.ds(head * width, width)], queries.at[i], sems.at[i])
-        for i, q_ref in enumerate(q_refs)
-    ]
-    for side in range(2):
-        copies.append(
-            pltpu.make_async_copy(
-                turn_refs[side].at[:, :, columns], turn_raw.at[side], sems.at[2 + side]
-            )
-        )
-
-    def page_copies(side, kind):
+    columns = slice(head * HEAD_DIM, (head + 1) * HEAD_DIM)
+    if head == 0:
+        found = [locate(kinds, table_refs[side], pages) for side in range(2)]
+        chosen = [kind for kind, _ in found]
+        for side in range(2):
+            chosen_ref[side] = jnp.full(chosen_ref.shape[1:], chosen[side], jnp.int32)
+    else:
+        chosen = [jnp.max(chosen_ref[side]) for side in range(2)]
+
+    def take_pages(side, kind):
         sources = kv_refs[side][kind]
-        if len(sources) == 1:
-            sources = [sources[0].at[:, half] for half in range(2)]
-        wide = sources[0].shape[2] > HEAD_DIM
-        lanes = columns if wide else pl.ds(0, HEAD_DIM)
-        target = pl.ds(side * pages, pages)
-        return [
-            pltpu.make_async_copy(
-                sources[half].at[:, :, lanes],
-                place.at[target, :, pl.ds(0, HEAD_DIM)],
-                sems.at[4 + 2 * half + side],
-            )
-            for half, place in enumerate((keys, values))
-        ]
+        lanes = columns if sources[0].shape[-1] > HEAD_DIM else slice(0, HEAD_DIM)
+        target = slice(side * pages, (side + 1) * pages)
+        for half, place in enumerate((keys, values)):
+            if len(sources) == 1:
+                taken = sources[0][:pages, half, :, lanes]
+            else:
+                taken = sources[half][:pages, :, lanes]
+            place[target, :, :HEAD_DIM] = taken
 
     for side in range(2):
         for kind in range(kinds):
 
-            @pl.when(found[side][0] == kind)
+            @pl.when(chosen[side] == kind)
             def _():
-                for copy in page_copies(side, kind):
-                    copy.start()
-
-    for copy in copies:
-        copy.start()
-    in_page = lax.broadcasted_iota(jnp.int32, (page, HEAD_DIM), 0)
-    seen = seen_ref[0]
-    for side in range(2):
-        start = numbers[side] * history
-        for number in range(pages):
-            left = seen - start - rows_refs[side][1][0, found[side][1] + number] * page
-            keys[side * pages + number, :, HEAD_DIM:] = jnp.where(
-                in_page < left, 0.0, HIDDEN
-            ).astype(jnp.bfloat16)
+                take_pages(side, kind)
+
+    if head == 0:
+        in_page = lax.broadcasted_iota(jnp.int32, (page, HEAD_DIM), 0)
+        seen = seen_ref[0]
+        for side in range(2):
+            start = numbers[side] * history
+            for number in range(pages):
+                left = seen - start - (table_refs[side][0, found[side][1] + number] % OWNER) * page
+                hidden_ref[side * pages + number] = jnp.where(in_page < left, 0.0, HIDDEN).astype(
+                    jnp.bfloat16
+                )
+    keys[:, :, HEAD_DIM:] = hidden_ref[...]
     values[:, :, HEAD_DIM:] = jnp.ones(
         (values.shape[0], page, HEAD_DIM), jnp.bfloat16
     )
@@ -273,18 +280,13 @@
             turn_keys[i, pl.ds(side * rows, rows), HEAD_DIM:] = jnp.where(
                 ahead <= second + asking * rows, 0.0, HIDDEN
             ).astype(jnp.bfloat16)
-    for copy in copies:
-        copy.wait()
     turn_pages = rows // page
     for side in range(2):
         for i in range(len(sides)):
-            turn_keys[i, pl.ds(side * rows, rows), pl.ds(0, HEAD_DIM)] = turn_raw[side, 0]
+            turn_keys[i, pl.ds(side * rows, rows), pl.ds(0, HEAD_DIM)] = turn_refs[side][0, :, columns]
         values[
             pl.ds(2 * pages + side * turn_pages, turn_pages), :, pl.ds(0, HEAD_DIM)
-        ] = turn_raw[side, 1].reshape(turn_pages, page, HEAD_DIM)
-    for side in range(2):
-        for copy in page_copies(side, 0):
-            copy.wait()
+        ] = turn_refs[side][1, :, columns].reshape(turn_pages, page, HEAD_DIM)
     depth = 2 * HEAD_DIM
     all_keys = 2 * history
     lane = lax.broadcasted_iota(jnp.int32, (rows, HEAD_DIM), 1)
@@ -298,7 +300,7 @@
                 [
                     jnp.concatenate(
                         [
-                            queries[which, :, pl.ds((batch * at_once + i) * HEAD_DIM, HEAD_DIM)],
+                            q_refs[which][:, pl.ds(head * width + (batch * at_once + i) * HEAD_DIM, HEAD_DIM)],
                             eye,
                         ],
                         axis=1,
@@ -307,27 +309,33 @@
                 ],
                 axis=0,
             )
-            scores = jnp.concatenate(
-                [
-                    lax.dot_general(
-                        asks,
-                        keys[...].reshape(all_keys, depth),
-                        across,
-                        preferred_element_type=jnp.float32,
-                    ),
-                    lax.dot_general(
+            peak = summed = None
+            for low in range(0, all_keys, CHUNK):
+                high = min(low + CHUNK, all_keys)
+                scores = lax.dot_general(
+                    asks,
+                    keys[...].reshape(all_keys, depth)[low:high],
+                    across,
+                    preferred_element_type=jnp.float32,
+                )
+                if high == all_keys:
+                    new = lax.dot_general(
                         asks, turn_keys[which], across, preferred_element_type=jnp.float32
-                    ),
-                ],
-                axis=1,
-            )
-            peak = jnp.max(scores, axis=1, keepdims=True)
-            weights = jnp.exp2((scores - peak) * TO_POWER).astype(jnp.bfloat16)
-            summed = jnp.dot(
-                weights,
-                values[...].reshape(all_keys + 2 * rows, depth),
-                preferred_element_type=jnp.float32,
-            )
+                    )
+                    scores = jnp.concatenate([scores, new], axis=1)
+                    high = high + 2 * rows
+                top = jnp.max(scores, axis=1, keepdims=True)
+                if peak is not None:
+                    top = jnp.maximum(top, peak)
+                weights = jnp.exp2((scores - top) * TO_POWER).astype(jnp.bfloat16)
+                added = jnp.dot(
+                    weights,
+                    values[...].reshape(all_keys + 2 * rows, depth)[low:high],
+                    preferred_element_type=jnp.float32,
+                )
+                if peak is not None:
+                    added = added + summed * jnp.exp2((peak - top) * TO_POWER)
+                peak, summed = top, added
             totals = summed[:, HEAD_DIM:]
             mixed = (summed[:, :HEAD_DIM] / totals).astype(jnp.bfloat16)
             level = peak * TO_POWER + jnp.log2(totals)
@@ -342,6 +350,11 @@
             high = stats.astype(jnp.bfloat16).astype(jnp.float32)
             middle = (stats - high).astype(jnp.bfloat16).astype(jnp.float32)
             low = stats - high - middle
+            spare = out_ref.shape[0] - PER_GROUP * rows - STAT_ROWS
+            if spare:
+                out_ref[pl.ds(PER_GROUP * rows + STAT_ROWS, spare)] = jnp.zeros(
+                    (spare, HEAD_DIM), jnp.bfloat16
+                )
             out_ref[pl.ds(PER_GROUP * rows, STAT_ROWS)] = jnp.concatenate(
                 [high, middle, low, jnp.zeros_like(low)], axis=0
             ).astype(jnp.bfloat16)
@@ -349,86 +362,93 @@
             l_ref[...] = stats
 
 
-def attend(head, sides, seen, tables, after, queries, own_kv, partner_kv, turns):
+def attend(head, sides, pages, marks, after, queries, own_kv, partner_kv, turns, states=None):
     rows = queries[0].shape[0]
-    pages, page = own_kv[0][0].shape[0], own_kv[0][0].shape[-2]
+    page = own_kv[0][0].shape[-2]
     counts = tuple(len(choice) for choice in own_kv)
     flat = [array for choice in (*own_kv, *partner_kv) for array in choice]
     all_rows = PER_GROUP * rows
     shapes = []
     for asked in sides:
-        extra = STAT_ROWS if asked else 0
+        extra = STAT_ROWS + (SPARE_ROWS if len(sides) == 2 else 0) if asked else 0
         shapes.append(jax.ShapeDtypeStruct((all_rows + extra, HEAD_DIM), jnp.bfloat16))
         if not asked:
             shapes.append(jax.ShapeDtypeStruct((PER_GROUP, rows), jnp.float32))
     asks = [queries[asked] for asked in sides]
+    padding = 0
+    if states is not None:
+        padding = 2
+        flat = [states] + flat
+        shapes.append(
+            jax.ShapeDtypeStruct((states.shape[0] + padding,) + states.shape[1:], states.dtype)
+        )
+    if head == 0:
+        shapes.append(jax.ShapeDtypeStruct((2 * pages, page, HEAD_DIM), jnp.bfloat16))
+        shapes.append(jax.ShapeDtypeStruct((2, 8, 128), jnp.int32))
     return pl.pallas_call(
-        functools.partial(attend_kernel, counts, head, sides),
-        in_specs=[scalar] * 5 + [outside] * (3 + len(sides) + len(flat)),
+        functools.partial(attend_kernel, counts, head, sides, padding),
+        in_specs=([scalar] * 3 if head == 0 else [whole] * 2) + [outside] + [whole] * (2 + len(sides) + len(flat)),
         out_specs=[whole] * len(shapes),
         out_shape=shapes,
         scratch_shapes=[
-            pltpu.VMEM((len(sides), rows, PER_GROUP * HEAD_DIM), jnp.bfloat16),
             pltpu.VMEM((2 * pages, page, 2 * HEAD_DIM), jnp.bfloat16),
             pltpu.VMEM((len(sides), 2 * rows, 2 * HEAD_DIM), jnp.bfloat16),
-            pltpu.VMEM((2, 2, rows, HEAD_DIM), jnp.bfloat16),
             pltpu.VMEM((2 * pages + 2 * rows // page, page, 2 * HEAD_DIM), jnp.bfloat16),
-            pltpu.SemaphoreType.DMA((8,)),
         ],
         compiler_params=params(24),
         cost_estimate=pl.CostEstimate(flops=1, bytes_accessed=1, transcendentals=0),
         name=f"attend_{head}_{len(sides)}_{sides[0]}",
-    )(seen, *tables, after, *asks, *turns, *flat)
-
-
-def merge_kernel(heads, valid_ref, *refs):
-    refs = refs[1:]
+    )(*marks, after, *asks, *turns, *flat)
+
+
+def merge_kernel(head, valid_ref, after_ref, o_ref, l_ref, got_ref, *refs):
     out_ref, held, sem = refs[-3:]
-    rows = out_ref.shape[0]
-    width = PER_GROUP * HEAD_DIM
+    rows, width = held.shape
     place = lax.axis_index("ctx") * rows + lax.broadcasted_iota(jnp.int32, (rows, HEAD_DIM), 0)
     live = place < valid_ref[0]
+    parts = got_ref[pl.ds(PER_GROUP * rows, STAT_ROWS)].astype(jnp.float32)
+    level = parts[:PER_GROUP] + parts[PER_GROUP : 2 * PER_GROUP]
+    level = level + parts[2 * PER_GROUP : 3 * PER_GROUP]
+    share = 1.0 / (1.0 + jnp.exp2(level - l_ref[...]))
+    share = jnp.concatenate([share, jnp.zeros((rows - PER_GROUP, rows), jnp.float32)], axis=0).T
     copies = []
-    for head in range(heads):
-        o_ref, l_ref, got_ref = refs[3 * head : 3 * head + 3]
-        parts = got_ref[pl.ds(PER_GROUP * rows, STAT_ROWS)].astype(jnp.float32)
-        level = parts[:PER_GROUP] + parts[PER_GROUP : 2 * PER_GROUP]
-        level = level + parts[2 * PER_GROUP : 3 * PER_GROUP]
-        share = 1.0 / (1.0 + jnp.exp2(level - l_ref[...]))
-        share = jnp.concatenate(
-            [share, jnp.zeros((rows - PER_GROUP, rows), jnp.float32)], axis=0
-        ).T
-        for member in range(PER_GROUP):
-            span = pl.ds(member * rows, rows)
-            here = o_ref[span].astype(jnp.float32)
-            there = got_ref[span].astype(jnp.float32)
-            result = there + share[:, member : member + 1] * (here - there)
-            held[:, pl.ds((head * PER_GROUP + member) * HEAD_DIM, HEAD_DIM)] = jnp.where(
-                live, result, 0.0
-            ).astype(jnp.bfloat16)
-        lanes = pl.ds(head * width, width)
-        copies.append(pltpu.make_async_copy(held.at[:, lanes], out_ref.at[:, lanes], sem.at[head]))
-        copies[-1].start()
+    for member in range(PER_GROUP):
+        span = pl.ds(member * rows, rows)
+        here = o_ref[span].astype(jnp.float32)
+        there = got_ref[span].astype(jnp.float32)
+        result = there + share[:, member : member + 1] * (here - there)
+        lanes = pl.ds(member * HEAD_DIM, HEAD_DIM)
+        held[:, lanes] = jnp.where(live, result, 0.0).astype(jnp.bfloat16)
+        if member % 4 == 3:
+            first = (member - 3) * HEAD_DIM
+            copies.append(
+                pltpu.make_async_copy(
+                    held.at[:, pl.ds(first, 4 * HEAD_DIM)],
+                    out_ref.at[:, pl.ds(head * width + first, 4 * HEAD_DIM)],
+                    sem.at[member // 4],
+                )
+            )
+            copies[-1].start()
     for copy in copies:
         copy.wait()
 
 
-def merge(after, valid, parts, rows):
-    heads = len(parts)
-    flat = [array for part in parts for array in part]
-    shape = jax.ShapeDtypeStruct((rows, heads * PER_GROUP * HEAD_DIM), jnp.bfloat16)
+def merge(head, heads, after, valid, part, rows, before=None):
+    width = PER_GROUP * HEAD_DIM
+    extra = [] if before is None else [before]
     return pl.pallas_call(
-        functools.partial(merge_kernel, heads),
-        in_specs=[scalar, outside] + [whole] * len(flat),
+        functools.partial(merge_kernel, head),
+        in_specs=[scalar, outside] + [whole] * len(part) + [distant] * len(extra),
         out_specs=distant,
-        out_shape=shape,
+        out_shape=jax.ShapeDtypeStruct((rows, heads * width), jnp.bfloat16),
+        input_output_aliases={2 + len(part): 0} if extra else {},
         scratch_shapes=[
-            pltpu.VMEM(shape.shape, shape.dtype),
-            pltpu.SemaphoreType.DMA((heads,)),
+            pltpu.VMEM((rows, width), jnp.bfloat16),
+            pltpu.SemaphoreType.DMA((PER_GROUP // 4,)),
         ],
         compiler_params=params(8),
-        name="merge",
-    )(valid, after, *flat)
+        name=f"merge_{head}",
+    )(valid, after, *part, *extra)
 
 
 def route_blocks(kv_local, state_local, owner_row, index_row):
@@ -494,60 +514,64 @@
 
     if parties == 2:
         swap = [(0, 1), (1, 0)]
-        moved, rest = [], kv
+        moved, pieces, rest = [], [], kv
         for head in range(heads):
             columns = slice(head * HEAD_DIM, (head + 1) * HEAD_DIM)
-            if head == 0:
-                cut = (rest[:, 0, :, columns], rest[:, 1, :, columns])
-            else:
-                cut = (rest[..., columns],)
+            cut = rest[..., columns]
+            if head:
+                cut = jnp.concatenate([cut, cut[:1]], axis=0)
+            cut = (cut,)
             cut, rest = lax.optimization_barrier((cut, rest))
+            pieces.append(cut)
             moved.append(tuple(lax.ppermute(piece, "pool", swap) for piece in cut))
-        padded = jnp.concatenate([state_pool, state_pool[: pages // 8]], axis=0)
-        slab = lax.ppermute(padded, "pool", swap)
-        table = (block_owner, block_index)
+        table = block_owner * OWNER + block_index
     else:
-        table = (block_owner, jnp.arange(pages, dtype=jnp.int32)[None])
+        table = jnp.arange(pages, dtype=jnp.int32)[None]
         routed, slab = route_blocks(kv, state_pool, block_owner[0], block_index[0])
         moved = [(routed[..., h * HEAD_DIM : (h + 1) * HEAD_DIM],) for h in range(heads)]
     asks = (queries[0], to_opposite(queries[0]))
 
-    early = [tuple(to_partner(row) for row in table), to_partner(turn_kv[0])]
-    if parties == 2:
-        early.append(to_partner(kv))
-    steps, (table_beside, turn_beside, *kv_beside) = lax.optimization_barrier((step_size[0], early))
-    turns = (turn_kv[0], turn_beside)
-    tables = table + table_beside
+    turns = (turn_kv[0], to_partner(turn_kv[0]))
+    tables = (table, to_partner(table))
     y, s, run = mixer_from_zero(
-        turn_len, mixer_in[0], input_proj[0], output_proj[0], steps, decay_rate, bypass_factor
+        turn_len, mixer_in[0], input_proj[0], output_proj[0], step_size[0], decay_rate, bypass_factor
     )
     parts = []
     after = run
+    marks = (history_len, *tables)
     for head in range(heads):
         came, after = lax.optimization_barrier((moved[head], after))
         own_kv, partner_kv = (came,), (tuple(to_partner(piece) for piece in came),)
         if parties == 2:
-            own_kv, partner_kv = ((kv,),) + own_kv, (tuple(kv_beside),) + partner_kv
+            beside = tuple(to_partner(piece) for piece in pieces[head])
+            own_kv, partner_kv = (pieces[head],) + own_kv, (beside,) + partner_kv
         ask = functools.partial(
             attend,
             head,
-            seen=history_len,
-            tables=tables,
+            pages=pages,
+            marks=marks,
             queries=asks,
             own_kv=own_kv,
             partner_kv=partner_kv,
             turns=turns,
         )
         if head + 1 < heads:
-            sent, o, after = ask(sides=(1, 0), after=after)
+            states = state_pool if parties == 2 and head == 0 else None
+            sent, o, after, *padded, hidden, chosen = ask(sides=(1, 0), after=after, states=states)
+            marks = (hidden, chosen)
+            if padded:
+                ordered = padded[0]
+                slab = lax.ppermute(ordered, "pool", swap)
         else:
             (sent,) = ask(sides=(1,), after=after)
             o, after = ask(sides=(0,), after=sent)
         parts.append((o, after, to_opposite(sent)))
     slab, after = lax.optimization_barrier((slab, after))
-    slabs = (state_pool, slab) if parties == 2 else (slab,)
-    mixed, final, after = add_saved(after, turn_len, table, slabs, y, s, run, output_proj[0])
-    attended = merge(after, turn_len, parts, rows)
+    slabs = (ordered, slab) if parties == 2 else (slab,)
+    mixed, final, after = add_saved(after, turn_len, chosen, slabs, y, s, run, output_proj[0])
+    attended = None
+    for head in range(heads):
+        attended = merge(head, heads, after, turn_len, parts[head], rows, attended)
     return (mixed[None], final[None], attended[None])
 
 

time: 47.7 us -> 45.5 us (0.954)
  waiting for transfers between devices: 1.46 us -> 5.16 us
  starting transfers between devices: 12.2 us -> 9.98 us
  Pallas kernels: 26.9 us -> 25.1 us
  local copies, waits for them, and re-layouts: 4.47 us -> 2.76 us
    ppermute x3 -> x2, starting transfers between devices: 5.1 us -> 3.23 us  [local(): moved.append(tuple((lax.ppermute(piece, 'pool', swap) for piece in cut)))]
    ppermute x3 -> x2, waiting for transfers between devices: 0.33 us -> 2.14 us  [local(): moved.append(tuple((lax.ppermute(piece, 'pool', swap) for piece in cut)))]
    pallas_call x4 -> x5, Pallas kernels: 18.4 us -> 17 us  [the longest x3 14.9 us: attend(): pl.pallas_call(functools.partial(attend_kernel, counts, head, sides, padd...]
    ppermute x7 -> x6, waiting for transfers between devices: 0.74 us -> 1.89 us  [to_partner(): return lax.ppermute(array, 'ctx', partner)]
    squeeze x1 -> x0, local copies, waits for them, and re-layouts: 1.07 us -> none  [local(): cut = (rest[:, 0, :, columns], rest[:, 1, :, columns])]
    unnamed x24, local copies, waits for them, and re-layouts: 2.56 us -> 1.49 us
    ppermute x3, waiting for transfers between devices: 0.39 us -> 1.12 us  [to_opposite(): return lax.ppermute(array, 'ctx', opposite)]
    ppermute x7 -> x6, starting transfers between devices: 1.68 us -> 1.14 us  [to_partner(): return lax.ppermute(array, 'ctx', partner)]
  transfers between devices with their start and end apart: 14 -> 12, of which waited for: 4 -> 5; matrix products, arithmetic and copies ran while one was open for 3% -> 0% of each run, Pallas kernels for 54% -> 53%
where the time goes in v3:
time: 45.5 us; the launch traced here: 45.3 us
  Pallas kernels  25.1 us (55%)
  starting transfers between devices  9.98 us (22%)
  waiting for transfers between devices  5.16 us (11%)
  local copies, waits for them, and re-layouts  2.76 us (6%)
  between operations  2.29 us (5%)
    pallas_call x3, Pallas kernels, attend(): pl.pallas_call(functools.partial(attend_kernel, counts, head, sides, padd...  14.9 us
    pallas_call x1, Pallas kernels, mixer_from_zero(): pl.pallas_call(mixer_kernel, grid=(groups,), in_specs=[scalar, pl.BlockSp...  6.63 us
    ppermute x3, starting transfers between devices, to_opposite(): return lax.ppermute(array, 'ctx', opposite)  4.09 us
    ppermute x2, starting transfers between devices, local(): moved.append(tuple((lax.ppermute(piece, 'pool', swap) for piece in cut)))  3.23 us
    ppermute x2, waiting for transfers between devices, local(): moved.append(tuple((lax.ppermute(piece, 'pool', swap) for piece in cut)))  2.14 us
    pallas_call x2, Pallas kernels, merge(): pl.pallas_call(functools.partial(merge_kernel, head), in_specs=[scalar, o...  2.07 us
    ppermute x6, waiting for transfers between devices, to_partner(): return lax.ppermute(array, 'ctx', partner)  1.89 us
    ppermute x1, starting transfers between devices, local(): slab = lax.ppermute(ordered, 'pool', swap)  1.52 us
  transfers between devices with their start and end apart: 12, of which 5 were waited for; matrix products, arithmetic and copies ran while one was open for 0% of the time, Pallas kernels for 53%

profile of v3, /device:TPU:0, one launch (start us, length us, event | category | flops | bytes accessed | tf_op | source)
XLA Modules:
  0.0 45.3 jit_solution(12949234869525504316)
XLA Ops:
  0.6 0.0 copy-start.9
  0.6 1.2 %slice.13.refs_9_ = bf16[32,2,32,128]{3,2,1,0:T(8,128)(2,1)S(1)} slice(bf16[32,2,32,256]{3,2,1,0:T(8,128)(2,1)} %bitcast.27), slice={[0:32], [0:2], [0:32], [0:128]} | slice | bytes 1048576 | tf_op jit(solution)/shard_map/slice | solution.py:520
  1.8 3.0 %collective-permute-start.1 = (bf16[32,2,32,128]{3,2,1,0:T(8,128)(2,1)S(1)}, bf16[32,2,32,128]{3,2,1,0:T(8,128)(2,1)S(1)}, u32[]{:S(2)}, u32[]{:S(2)}) collective-permute-start(bf16[32,2,32,128]{3,2,1,0:T(8,128)(2,1)S(1)} %slice.13.refs_9_), channel_id=1, source_target_pairs={{0,16},{16,0},{1,17},{17,1},{2,18},{18,2},{3,19},{19,3},{4,20},{20... | collective-permute-start | bytes 1572872 | tf_op jit(solution)/shard_map/ppermute | solution.py:526
  4.8 0.0 copy-done.9
  4.8 0.1 slice.11
  5.0 0.0 copy-start.6
  5.0 0.0 copy-start
  5.0 0.0 copy-start.1
  5.0 0.1 pad_maximum_fusion.refs_6_
  5.1 0.2 collective-permute-start.7
  5.3 0.0 collective-permute-start.4
  5.3 0.8 %copy-done = bf16[1,128,2048]{2,1,0:T(8,128)(2,1)S(1)} copy-done((bf16[1,128,2048]{2,1,0:T(8,128)(2,1)S(1)}, bf16[1,128,2048]{2,1,0:T(8,128)(2,1)}, u32[]{:S(2)}) %copy-start) | copy-done | bytes 524312
  6.1 1.5 %collective-permute-start.2 = (bf16[128,2048]{1,0:T(8,128)(2,1)S(1)}, bf16[128,2048]{1,0:T(8,128)(2,1)S(1)}, u32[]{:S(2)}, u32[]{:S(2)}) collective-permute-start(bf16[128,2048]{1,0:T(8,128)(2,1)S(1)} %bitcast.12), channel_id=1, source_target_pairs={{0,8},{4,12},{8,0},{12,4},{1,9},{5,13},{9,1},{13,5},{2,10},{6,14},... | collective-permute-start | bytes 1572872 | tf_op jit(solution)/shard_map/ppermute | solution.py:513
  8.2 0.0 copy-start.7
  8.3 0.0 copy-start.8
  8.3 0.6 %copy-done.7 = f32[32]{0:T(128)S(1)} copy-done((f32[32]{0:T(128)S(1)}, f32[32]{0:T(128)}, u32[]{:S(2)}) %copy-start.7) | copy-done | bytes 152
  8.9 0.0 copy-done.8
  8.9 6.6 %mixer_from_zero.1 = (f32[32,16,512]{2,1,0:T(8,128)S(1)}, f32[32,16,256]{2,1,0:T(8,128)S(1)}, f32[32,512]{1,0:T(8,128)S(1)}) custom-call(s32[1]{0:T(128)S(6)} %copy.20.valid_ref, bf16[32,16,512]{2,1,0:T(8,128)(2,1)S(1)} %bitcast.21, bf16[2,256,512]{2,1,0:T(8,128)(2,1)S(1)} %bitcast.22, bf16[2,256,512]{2,1,0:T(8,128)(2,1)S(1)} %bitcast.15, ...), custom_call_target="tpu_custom_call" | custom-call | flops 1 | bytes 1 | tf_op jit(solution)/shard_map/mixer_from_zero/pallas_call | solution.py:103
  15.6 0.0 copy-start.10
  15.6 0.0 copy-start.11
  15.6 2.0 %collective-permute-done.1.refs_10_ = bf16[32,2,32,128]{3,2,1,0:T(8,128)(2,1)S(1)} collective-permute-done((bf16[32,2,32,128]{3,2,1,0:T(8,128)(2,1)S(1)}, bf16[32,2,32,128]{3,2,1,0:T(8,128)(2,1)S(1)}, u32[]{:S(2)}, u32[]{:S(2)}) %collective-permute-start.1) | collective-permute-done | bytes 524320 | tf_op jit(solution)/shard_map/ppermute | solution.py:526
  17.6 0.0 collective-permute-start.5
  17.6 0.0 copy-done.11
  17.6 0.6 %collective-permute-start = (s32[1,64]{1,0:T(1,128)S(1)}, s32[1,64]{1,0:T(1,128)S(1)}, u32[]{:S(2)}, u32[]{:S(2)}) collective-permute-start(s32[1,64]{1,0:T(1,128)S(1)} %multiply_add_fusion.refs_1_), channel_id=1, source_target_pairs={{0,4},{4,0},{8,12},{12,8},{1,5},{5,1},{9,13},{13,9},{2,6},{6,2},{1... | collective-permute-start | bytes 776 | tf_op jit(solution)/shard_map/ppermute | solution.py:510
  18.2 1.3 %collective-permute-done.refs_2_ = s32[1,64]{1,0:T(1,128)S(1)} collective-permute-done((s32[1,64]{1,0:T(1,128)S(1)}, s32[1,64]{1,0:T(1,128)S(1)}, u32[]{:S(2)}, u32[]{:S(2)}) %collective-permute-start) | collective-permute-done | bytes 288 | tf_op jit(solution)/shard_map/ppermute | solution.py:510
  19.5 0.1 collective-permute-start.3
  20.3 0.6 %collective-permute-done.3.refs_7_.refs_5_ = bf16[2,128,256]{2,1,0:T(8,128)(2,1)S(1)} collective-permute-done((bf16[2,128,256]{2,1,0:T(8,128)(2,1)S(1)}, bf16[2,128,256]{2,1,0:T(8,128)(2,1)S(1)}, u32[]{:S(2)}, u32[]{:S(2)}) %collective-permute-start.3) | collective-permute-done | bytes 131104 | tf_op jit(solution)/shard_map/ppermute | solution.py:510
  20.9 0.1 collective-permute-start.8
  21.0 0.0 collective-permute-done.4.refs_11_
  21.0 0.0 collective-permute-done.2.refs_4_.refs_3_
  21.0 0.0 collective-permute-done.5.refs_12_
  21.0 0.0 copy-done.5
  21.0 7.2 %attend_0_2_1.1 = (bf16[1104,128]{1,0:T(8,128)(2,1)S(1)}, bf16[1024,128]{1,0:T(8,128)(2,1)S(1)}, f32[8,128]{1,0:T(8,128)S(1)}, bf16[34,16,256]{2,1,0:T(8,128)(2,...) custom-call(s32[1]{0:T(128)S(6)} %copy.19.refs_0_, s32[1,64]{1,0:T(1,128)S(1)} %multiply_add_fusion.refs_1_, ...), custom_call_target="tpu_custom_call" | custom-call | flops 1 | bytes 1 | tf_op jit(solution)/shard_map/attend_0_2_1/pallas_call | solution.py:388
  28.2 0.1 collective-permute-done.7.refs_7_
  28.3 0.3 collective-permute-start.9
  28.6 2.0 %collective-permute-start.11 = (bf16[1104,128]{1,0:T(8,128)(2,1)S(1)}, bf16[1104,128]{1,0:T(8,128)(2,1)S(1)}, u32[]{:S(2)}, u32[]{:S(2)}) collective-permute-start(bf16[1104,128]{1,0:T(8,128)(2,1)S(1)} %get-tuple-element.48), channel_id=1, source_target_pairs={{0,8},{4,12},{8,0},{12,4},{1,9},{5,13},{9,1},{13,5},{2,10},{6,14},... | collective-permute-start | bytes 847880 | tf_op jit(solution)/shard_map/ppermute | solution.py:513
  30.7 1.5 %collective-permute-start.6 = (bf16[34,16,256]{2,1,0:T(8,128)(2,1)S(1)}, bf16[34,16,256]{2,1,0:T(8,128)(2,1)S(1)}, u32[]{:S(2)}, u32[]{:S(2)}) collective-permute-start(bf16[34,16,256]{2,1,0:T(8,128)(2,1)S(1)} %get-tuple-element.31.refs_1_), channel_id=1, source_target_pairs={{0,16},{16,0},{1,17},{17,1},{2,18},{18,2},{3,19},{19,3},{4,20},{20... | collective-permute-start | bytes 835592 | tf_op jit(solution)/shard_map/ppermute | solution.py:564
  32.2 0.0 collective-permute-done.8.refs_8_
  32.2 0.0 collective-permute-done.9.refs_9_
  32.2 4.0 %attend_1_1_1.1.refs_2_ = bf16[1056,128]{1,0:T(8,128)(2,1)S(1)} custom-call(bf16[64,32,128]{2,1,0:T(8,128)(2,1)S(1)} %get-tuple-element.32.refs_0_, s32[2,8,128]{2,1,0:T(8,128)S(1)} %get-tuple-element.30.refs_1_.chosen_ref, f32[8,128]{1,0:T(8,128)S(1)} %get-tuple-element.36.refs_2_.l_ref, bf16[128,2048]{1,0:T(8,128)(2,1)S(1)} %collective-permute-done.2.refs_4_.refs_3_, ...), custom_call_target="tpu_custom_call" | custom-call | flops 1 | bytes 1 | tf_op jit(solution)/shard_map/attend_1_1_1/pallas_call | solution.py:388
  36.1 0.6 %collective-permute-start.10 = (bf16[1056,128]{1,0:T(8,128)(2,1)S(1)}, bf16[1056,128]{1,0:T(8,128)(2,1)S(1)}, u32[]{:S(2)}, u32[]{:S(2)}) collective-permute-start(bf16[1056,128]{1,0:T(8,128)(2,1)S(1)} %attend_1_1_1.1.refs_2_), channel_id=1, source_target_pairs={{0,8},{4,12},{8,0},{12,4},{1,9},{5,13},{9,1},{13,5},{2,10},{6,14},... | collective-permute-start | bytes 811016 | tf_op jit(solution)/shard_map/ppermute | solution.py:513
  36.7 3.8 %attend_1_1_0.1 = (bf16[1024,128]{1,0:T(8,128)(2,1)S(1)}, f32[8,128]{1,0:T(8,128)S(1)}) custom-call(bf16[64,32,128]{2,1,0:T(8,128)(2,1)S(1)} %get-tuple-element.32.refs_0_, s32[2,8,128]{2,1,0:T(8,128)S(1)} %get-tuple-element.30.refs_1_.chosen_ref, bf16[1056,128]{1,0:T(8,128)(2,1)S(1)} %attend_1_1_1.1.refs_2_, bf16[128,2048]{1,0:T(8,128)(2,1)S(1)} %bitcast.14, ...), custom_call_target="tpu_custom_call" | custom-call | flops 1 | bytes 1 | tf_op jit(solution)/shard_map/attend_1_1_0/pallas_call | solution.py:388
  40.5 0.0 collective-permute-done.6.refs_2_
  40.5 1.5 %add_saved.1 = (bf16[32,16,512]{2,1,0:T(8,128)(2,1)}, f32[32,16,256]{2,1,0:T(8,128)}, f32[8,128]{1,0:T(8,128)S(1)}) custom-call(s32[1]{0:T(128)S(6)} %copy.20.valid_ref, s32[2,8,128]{2,1,0:T(8,128)S(1)} %get-tuple-element.30.refs_1_.chosen_ref, f32[8,128]{1,0:T(8,128)S(1)} %get-tuple-element.39.refs_0_.l_ref, ...), custom_call_target="tpu_custom_call" | custom-call | flops 1 | bytes 1 | tf_op jit(solution)/shard_map/add_saved/pallas_call | solution.py:176
  42.0 0.0 collective-permute-done.11.got_ref
  42.0 1.0 %merge_0.1.refs_0_ = bf16[128,2048]{1,0:T(8,128)(2,1)} custom-call(s32[1]{0:T(128)S(6)} %copy.20.valid_ref, f32[8,128]{1,0:T(8,128)S(1)} %get-tuple-element.45.after_ref, bf16[1024,128]{1,0:T(8,128)(2,1)S(1)} %get-tuple-element.47.o_ref, f32[8,128]{1,0:T(8,128)S(1)} %get-tuple-element.36.refs_2_.l_ref, bf16[1104,128]{1,0:T(8,128)(2,1)S(1)} %collective-permute-done.11.got_ref), custom_call_target="tpu_custom_call" | custom-call | tf_op jit(solution)/shard_map/merge_0/pallas_call | solution.py:439
  43.0 1.1 %collective-permute-done.10.got_ref = bf16[1056,128]{1,0:T(8,128)(2,1)S(1)} collective-permute-done((bf16[1056,128]{1,0:T(8,128)(2,1)S(1)}, bf16[1056,128]{1,0:T(8,128)(2,1)S(1)}, u32[]{:S(2)}, u32[]{:S(2)}) %collective-permute-start.10) | collective-permute-done | bytes 270368 | tf_op jit(solution)/shard_map/ppermute | solution.py:513
  44.2 1.0 %merge_1.1 = bf16[128,2048]{1,0:T(8,128)(2,1)} custom-call(s32[1]{0:T(128)S(6)} %copy.20.valid_ref, f32[8,128]{1,0:T(8,128)S(1)} %get-tuple-element.45.after_ref, bf16[1024,128]{1,0:T(8,128)(2,1)S(1)} %get-tuple-element.46.o_ref, f32[8,128]{1,0:T(8,128)S(1)} %get-tuple-element.39.refs_0_.l_ref, ...), custom_call_target="tpu_custom_call", output_to_operand_aliasing={{}: (5, {})} | custom-call | tf_op jit(solution)/shard_map/merge_1/pallas_call | solution.py:439
  (12 shorter events, 0.0 us)
Async XLA Ops:
  0.6 4.2 %copy-start.9 = (bf16[1,32,2,32,256]{4,3,2,1,0:T(8,128)(2,1)S(1)}, bf16[1,32,2,32,256]{4,3,2,1,0:T(8,128)(2,1)}, u32[]{:S(2)}) copy-start(bf16[1,32,2,32,256]{4,3,2,1,0:T(8,128)(2,1)} %param.14) | copy-start | bytes 3145732
  1.8 15.8 %collective-permute-start.1 = (bf16[32,2,32,128]{3,2,1,0:T(8,128)(2,1)S(1)}, bf16[32,2,32,128]{3,2,1,0:T(8,128)(2,1)S(1)}, u32[]{:S(2)}, u32[]{:S(2)}) collective-permute-start(bf16[32,2,32,128]{3,2,1,0:T(8,128)(2,1)S(1)} %slice.13.refs_9_), channel_id=1, source_target_pairs={{0,16},{16,0},{1,17},{17,1},{2,18},{18,2},{3,19},{19,3},{4,20},{20... | collective-permute-start | bytes 1572872 | tf_op jit(solution)/shard_map/ppermute | solution.py:526
  4.8 3.4 %copy-start.3 = (bf16[1,32,16,512]{3,2,1,0:T(8,128)(2,1)S(1)}, bf16[1,32,16,512]{3,2,1,0:T(8,128)(2,1)}, u32[]{:S(2)}) copy-start(bf16[1,32,16,512]{3,2,1,0:T(8,128)(2,1)} %param.20) | copy-start | bytes 1572868
  4.8 3.4 %copy-start.4 = (bf16[1,2,256,512]{3,2,1,0:T(8,128)(2,1)S(1)}, bf16[1,2,256,512]{3,2,1,0:T(8,128)(2,1)}, u32[]{:S(2)}) copy-start(bf16[1,2,256,512]{3,2,1,0:T(8,128)(2,1)} %param.21) | copy-start | bytes 1572868
  5.0 3.3 %copy-start.6 = (f32[1,32,512]{2,1,0:T(8,128)S(1)}, f32[1,32,512]{2,1,0:T(8,128)}, u32[]{:S(2)}) copy-start(f32[1,32,512]{2,1,0:T(8,128)} %param.23) | copy-start | bytes 196612
  5.0 1.1 %copy-start = (bf16[1,128,2048]{2,1,0:T(8,128)(2,1)S(1)}, bf16[1,128,2048]{2,1,0:T(8,128)(2,1)}, u32[]{:S(2)}) copy-start(bf16[1,128,2048]{2,1,0:T(8,128)(2,1)} %param.26) | copy-start | bytes 1572868
  5.0 3.3 %copy-start.1 = (bf16[1,2,256,512]{3,2,1,0:T(8,128)(2,1)S(1)}, bf16[1,2,256,512]{3,2,1,0:T(8,128)(2,1)}, u32[]{:S(2)}) copy-start(bf16[1,2,256,512]{3,2,1,0:T(8,128)(2,1)} %param.22) | copy-start | bytes 1572868
  5.1 23.3 %collective-permute-start.7 = (bf16[33,2,32,128]{3,2,1,0:T(8,128)(2,1)S(1)}, bf16[33,2,32,128]{3,2,1,0:T(8,128)(2,1)S(1)}, u32[]{:S(2)}, u32[]{:S(2)}) collective-permute-start(bf16[33,2,32,128]{3,2,1,0:T(8,128)(2,1)S(1)} %pad_maximum_fusion.refs_6_), channel_id=1, source_target_pairs={{0,16},{16,0},{1,17},{17,1},{2,18},{18,2},{3,19},{19,3},{4,20},{20... | collective-permute-start | bytes 1622024 | tf_op jit(solution)/shard_map/ppermute | solution.py:526
  5.3 15.7 %collective-permute-start.4 = (bf16[32,2,32,128]{3,2,1,0:T(8,128)(2,1)S(1)}, bf16[32,2,32,128]{3,2,1,0:T(8,128)(2,1)S(1)}, u32[]{:S(2)}, u32[]{:S(2)}) collective-permute-start(bf16[32,2,32,128]{3,2,1,0:T(8,128)(2,1)S(1)} %slice.13.refs_9_), channel_id=1, source_target_pairs={{0,4},{4,0},{8,12},{12,8},{1,5},{5,1},{9,13},{13,9},{2,6},{6,2},{1... | collective-permute-start | bytes 1572872 | tf_op jit(solution)/shard_map/ppermute | solution.py:510
  6.1 14.9 %collective-permute-start.2 = (bf16[128,2048]{1,0:T(8,128)(2,1)S(1)}, bf16[128,2048]{1,0:T(8,128)(2,1)S(1)}, u32[]{:S(2)}, u32[]{:S(2)}) collective-permute-start(bf16[128,2048]{1,0:T(8,128)(2,1)S(1)} %bitcast.12), channel_id=1, source_target_pairs={{0,8},{4,12},{8,0},{12,4},{1,9},{5,13},{9,1},{13,5},{2,10},{6,14},... | collective-permute-start | bytes 1572872 | tf_op jit(solution)/shard_map/ppermute | solution.py:513
  8.2 0.7 %copy-start.7 = (f32[32]{0:T(128)S(1)}, f32[32]{0:T(128)}, u32[]{:S(2)}) copy-start(f32[32]{0:T(128)} %param.24) | copy-start | bytes 388
  8.3 0.7 %copy-start.8 = (f32[32]{0:T(128)S(1)}, f32[32]{0:T(128)}, u32[]{:S(2)}) copy-start(f32[32]{0:T(128)} %param.25) | copy-start | bytes 388
  8.9 10.6 %copy-start.2 = (bf16[1,2,128,256]{3,2,1,0:T(8,128)(2,1)S(1)}, bf16[1,2,128,256]{3,2,1,0:T(8,128)(2,1)}, u32[]{:S(2)}) copy-start(bf16[1,2,128,256]{3,2,1,0:T(8,128)(2,1)} %param.27) | copy-start | bytes 393220
  8.9 12.1 %copy-start.5 = (bf16[32,16,256]{2,1,0:T(8,128)(2,1)S(1)}, bf16[32,16,256]{2,1,0:T(8,128)(2,1)}, u32[]{:S(2)}) copy-start(bf16[32,16,256]{2,1,0:T(8,128)(2,1)} %refs_8_.1) | copy-start | bytes 786436
  15.6 2.0 %copy-start.10 = (s32[1,64]{1,0:T(1,128)S(1)}, s32[1,64]{1,0:T(1,128)}, u32[]{:S(2)}) copy-start(s32[1,64]{1,0:T(1,128)} %param.17) | copy-start | bytes 772
  15.6 2.0 %copy-start.11 = (s32[1,64]{1,0:T(1,128)S(1)}, s32[1,64]{1,0:T(1,128)}, u32[]{:S(2)}) copy-start(s32[1,64]{1,0:T(1,128)} %param.16) | copy-start | bytes 772
  17.6 3.4 %collective-permute-start.5 = (bf16[32,2,32,128]{3,2,1,0:T(8,128)(2,1)S(1)}, bf16[32,2,32,128]{3,2,1,0:T(8,128)(2,1)S(1)}, u32[]{:S(2)}, u32[]{:S(2)}) collective-permute-start(bf16[32,2,32,128]{3,2,1,0:T(8,128)(2,1)S(1)} %collective-permute-done.1.refs_10_), channel_id=1, source_target_pairs={{0,4},{4,0},{8,12},{12,8},{1,5},{5,1},{9,13},{13,9},{2,6},{6,2},{1... | collective-permute-start | bytes 1572872 | tf_op jit(solution)/shard_map/ppermute | solution.py:510
  17.6 1.9 %collective-permute-start = (s32[1,64]{1,0:T(1,128)S(1)}, s32[1,64]{1,0:T(1,128)S(1)}, u32[]{:S(2)}, u32[]{:S(2)}) collective-permute-start(s32[1,64]{1,0:T(1,128)S(1)} %multiply_add_fusion.refs_1_), channel_id=1, source_target_pairs={{0,4},{4,0},{8,12},{12,8},{1,5},{5,1},{9,13},{13,9},{2,6},{6,2},{1... | collective-permute-start | bytes 776 | tf_op jit(solution)/shard_map/ppermute | solution.py:510
  19.5 1.3 %collective-permute-start.3 = (bf16[2,128,256]{2,1,0:T(8,128)(2,1)S(1)}, bf16[2,128,256]{2,1,0:T(8,128)(2,1)S(1)}, u32[]{:S(2)}, u32[]{:S(2)}) collective-permute-start(bf16[2,128,256]{2,1,0:T(8,128)(2,1)S(1)} %bitcast.17), channel_id=1, source_target_pairs={{0,4},{4,0},{8,12},{12,8},{1,5},{5,1},{9,13},{13,9},{2,6},{6,2},{1... | collective-permute-start | bytes 393224 | tf_op jit(solution)/shard_map/ppermute | solution.py:510
  20.9 11.3 %collective-permute-start.8 = (bf16[33,2,32,128]{3,2,1,0:T(8,128)(2,1)S(1)}, bf16[33,2,32,128]{3,2,1,0:T(8,128)(2,1)S(1)}, u32[]{:S(2)}, u32[]{:S(2)}) collective-permute-start(bf16[33,2,32,128]{3,2,1,0:T(8,128)(2,1)S(1)} %pad_maximum_fusion.refs_6_), channel_id=1, source_target_pairs={{0,4},{4,0},{8,12},{12,8},{1,5},{5,1},{9,13},{13,9},{2,6},{6,2},{1... | collective-permute-start | bytes 1622024 | tf_op jit(solution)/shard_map/ppermute | solution.py:510
  28.3 3.8 %collective-permute-start.9 = (bf16[33,2,32,128]{3,2,1,0:T(8,128)(2,1)S(1)}, bf16[33,2,32,128]{3,2,1,0:T(8,128)(2,1)S(1)}, u32[]{:S(2)}, u32[]{:S(2)}) collective-permute-start(bf16[33,2,32,128]{3,2,1,0:T(8,128)(2,1)S(1)} %collective-permute-done.7.refs_7_), channel_id=1, source_target_pairs={{0,4},{4,0},{8,12},{12,8},{1,5},{5,1},{9,13},{13,9},{2,6},{6,2},{1... | collective-permute-start | bytes 1622024 | tf_op jit(solution)/shard_map/ppermute | solution.py:510
  28.6 13.4 %collective-permute-start.11 = (bf16[1104,128]{1,0:T(8,128)(2,1)S(1)}, bf16[1104,128]{1,0:T(8,128)(2,1)S(1)}, u32[]{:S(2)}, u32[]{:S(2)}) collective-permute-start(bf16[1104,128]{1,0:T(8,128)(2,1)S(1)} %get-tuple-element.48), channel_id=1, source_target_pairs={{0,8},{4,12},{8,0},{12,4},{1,9},{5,13},{9,1},{13,5},{2,10},{6,14},... | collective-permute-start | bytes 847880 | tf_op jit(solution)/shard_map/ppermute | solution.py:513
  30.7 9.8 %collective-permute-start.6 = (bf16[34,16,256]{2,1,0:T(8,128)(2,1)S(1)}, bf16[34,16,256]{2,1,0:T(8,128)(2,1)S(1)}, u32[]{:S(2)}, u32[]{:S(2)}) collective-permute-start(bf16[34,16,256]{2,1,0:T(8,128)(2,1)S(1)} %get-tuple-element.31.refs_1_), channel_id=1, source_target_pairs={{0,16},{16,0},{1,17},{17,1},{2,18},{18,2},{3,19},{19,3},{4,20},{20... | collective-permute-start | bytes 835592 | tf_op jit(solution)/shard_map/ppermute | solution.py:564
  36.1 8.0 %collective-permute-start.10 = (bf16[1056,128]{1,0:T(8,128)(2,1)S(1)}, bf16[1056,128]{1,0:T(8,128)(2,1)S(1)}, u32[]{:S(2)}, u32[]{:S(2)}) collective-permute-start(bf16[1056,128]{1,0:T(8,128)(2,1)S(1)} %attend_1_1_1.1.refs_2_), channel_id=1, source_target_pairs={{0,8},{4,12},{8,0},{12,4},{1,9},{5,13},{9,1},{13,5},{2,10},{6,14},... | collective-permute-start | bytes 811016 | tf_op jit(solution)/shard_map/ppermute | solution.py:513

commit v4 on v3

--- a/solution.py
+++ b/solution.py
@@ -532,9 +532,10 @@
     asks = (queries[0], to_opposite(queries[0]))
 
     turns = (turn_kv[0], to_partner(turn_kv[0]))
-    tables = (table, to_partner(table))
+    steps, table_beside = lax.optimization_barrier((step_size[0], to_partner(table)))
+    tables = (table, table_beside)
     y, s, run = mixer_from_zero(
-        turn_len, mixer_in[0], input_proj[0], output_proj[0], step_size[0], decay_rate, bypass_factor
+        turn_len, mixer_in[0], input_proj[0], output_proj[0], steps, decay_rate, bypass_factor
     )
     parts = []
     after = run

time: 45.5 us -> 45.3 us (level)
  waiting for transfers between devices: 5.16 us -> 5.67 us
    ppermute x3, waiting for transfers between devices: 1.12 us -> 2.14 us  [to_opposite(): return lax.ppermute(array, 'ctx', opposite)]
    ppermute x6, waiting for transfers between devices: 1.89 us -> 0.95 us  [to_partner(): return lax.ppermute(array, 'ctx', partner)]
where the time goes in v4:
time: 45.3 us; the launch traced here: 45.1 us
  Pallas kernels  25.1 us (55%)
  starting transfers between devices  9.66 us (21%)
  waiting for transfers between devices  5.67 us (13%)
  local copies, waits for them, and re-layouts  2.36 us (5%)
  between operations  2.28 us (5%)
    pallas_call x3, Pallas kernels, attend(): pl.pallas_call(functools.partial(attend_kernel, counts, head, sides, padd...  14.9 us
    pallas_call x1, Pallas kernels, mixer_from_zero(): pl.pallas_call(mixer_kernel, grid=(groups,), in_specs=[scalar, pl.BlockSp...  6.62 us
    ppermute x3, starting transfers between devices, to_opposite(): return lax.ppermute(array, 'ctx', opposite)  3.77 us
    ppermute x2, starting transfers between devices, local(): moved.append(tuple((lax.ppermute(piece, 'pool', swap) for piece in cut)))  3.22 us
    ppermute x2, waiting for transfers between devices, local(): moved.append(tuple((lax.ppermute(piece, 'pool', swap) for piece in cut)))  2.58 us
    ppermute x3, waiting for transfers between devices, to_opposite(): return lax.ppermute(array, 'ctx', opposite)  2.14 us
    pallas_call x2, Pallas kernels, merge(): pl.pallas_call(functools.partial(merge_kernel, head), in_specs=[scalar, o...  2.07 us
    ppermute x1, starting transfers between devices, local(): slab = lax.ppermute(ordered, 'pool', swap)  1.52 us
  transfers between devices with their start and end apart: 12, of which 5 were waited for; matrix products, arithmetic and copies ran while one was open for 0% of the time, Pallas kernels for 53%

profile of v4, /device:TPU:0, one launch (start us, length us, event | category | flops | bytes accessed | tf_op | source)
XLA Modules:
  0.0 45.1 jit_solution(10501500043242316441)
XLA Ops:
  0.6 0.0 copy-start.9
  0.6 1.2 %slice.13.refs_9_ = bf16[32,2,32,128]{3,2,1,0:T(8,128)(2,1)S(1)} slice(bf16[32,2,32,256]{3,2,1,0:T(8,128)(2,1)} %bitcast.27), slice={[0:32], [0:2], [0:32], [0:128]} | slice | bytes 1048576 | tf_op jit(solution)/shard_map/slice | solution.py:520
  1.8 3.0 %collective-permute-start.1 = (bf16[32,2,32,128]{3,2,1,0:T(8,128)(2,1)S(1)}, bf16[32,2,32,128]{3,2,1,0:T(8,128)(2,1)S(1)}, u32[]{:S(2)}, u32[]{:S(2)}) collective-permute-start(bf16[32,2,32,128]{3,2,1,0:T(8,128)(2,1)S(1)} %slice.13.refs_9_), channel_id=1, source_target_pairs={{0,16},{16,0},{1,17},{17,1},{2,18},{18,2},{3,19},{19,3},{4,20},{20... | collective-permute-start | bytes 1572872 | tf_op jit(solution)/shard_map/ppermute | solution.py:526
  4.8 0.0 collective-permute-start.4
  4.9 0.1 slice.11
  5.0 0.0 copy-start.10
  5.0 0.0 copy-start.11
  5.0 0.0 copy-start.6
  5.0 0.0 copy-start
  5.0 0.0 copy-start.1
  5.0 0.1 pad_maximum_fusion.refs_6_
  5.1 0.2 collective-permute-start.7
  5.3 0.4 copy-done.10
  5.7 0.0 copy-done.11
  5.7 0.5 %collective-permute-start = (s32[1,64]{1,0:T(1,128)S(1)}, s32[1,64]{1,0:T(1,128)S(1)}, u32[]{:S(2)}, u32[]{:S(2)}) collective-permute-start(s32[1,64]{1,0:T(1,128)S(1)} %multiply_add_fusion.refs_1_), channel_id=1, source_target_pairs={{0,4},{4,0},{8,12},{12,8},{1,5},{5,1},{9,13},{13,9},{2,6},{6,2},{1... | collective-permute-start | bytes 776 | tf_op jit(solution)/shard_map/ppermute | solution.py:510
  6.2 1.5 %collective-permute-start.2 = (bf16[128,2048]{1,0:T(8,128)(2,1)S(1)}, bf16[128,2048]{1,0:T(8,128)(2,1)S(1)}, u32[]{:S(2)}, u32[]{:S(2)}) collective-permute-start(bf16[128,2048]{1,0:T(8,128)(2,1)S(1)} %bitcast.12), channel_id=1, source_target_pairs={{0,8},{4,12},{8,0},{12,4},{1,9},{5,13},{9,1},{13,5},{2,10},{6,14},... | collective-permute-start | bytes 1572872 | tf_op jit(solution)/shard_map/ppermute | solution.py:513
  8.4 0.0 collective-permute-done.refs_2_
  8.4 0.0 copy-start.7
  8.4 0.0 copy-start.8
  8.4 0.0 copy-done.3
  8.4 0.0 copy-done.4
  8.4 0.6 %copy-done.7 = f32[32]{0:T(128)S(1)} copy-done((f32[32]{0:T(128)S(1)}, f32[32]{0:T(128)}, u32[]{:S(2)}) %copy-start.7) | copy-done | bytes 152
  9.0 0.0 copy-done.8
  9.0 6.6 %mixer_from_zero.1 = (f32[32,16,512]{2,1,0:T(8,128)S(1)}, f32[32,16,256]{2,1,0:T(8,128)S(1)}, f32[32,512]{1,0:T(8,128)S(1)}) custom-call(s32[1]{0:T(128)S(6)} %copy.20.valid_ref, bf16[32,16,512]{2,1,0:T(8,128)(2,1)S(1)} %bitcast.21, bf16[2,256,512]{2,1,0:T(8,128)(2,1)S(1)} %bitcast.22, bf16[2,256,512]{2,1,0:T(8,128)(2,1)S(1)} %bitcast.15, ...), custom_call_target="tpu_custom_call" | custom-call | flops 1 | bytes 1 | tf_op jit(solution)/shard_map/mixer_from_zero/pallas_call | solution.py:103
  15.7 1.9 %collective-permute-done.1.refs_10_ = bf16[32,2,32,128]{3,2,1,0:T(8,128)(2,1)S(1)} collective-permute-done((bf16[32,2,32,128]{3,2,1,0:T(8,128)(2,1)S(1)}, bf16[32,2,32,128]{3,2,1,0:T(8,128)(2,1)S(1)}, u32[]{:S(2)}, u32[]{:S(2)}) %collective-permute-start.1) | collective-permute-done | bytes 524320 | tf_op jit(solution)/shard_map/ppermute | solution.py:526
  17.6 0.0 collective-permute-start.5
  17.6 0.5 %collective-permute-start.3 = (bf16[2,128,256]{2,1,0:T(8,128)(2,1)S(1)}, bf16[2,128,256]{2,1,0:T(8,128)(2,1)S(1)}, u32[]{:S(2)}, u32[]{:S(2)}) collective-permute-start(bf16[2,128,256]{2,1,0:T(8,128)(2,1)S(1)} %bitcast.17), channel_id=1, source_target_pairs={{0,4},{4,0},{8,12},{12,8},{1,5},{5,1},{9,13},{13,9},{2,6},{6,2},{1... | collective-permute-start | bytes 393224 | tf_op jit(solution)/shard_map/ppermute | solution.py:510
  18.8 0.9 %collective-permute-done.3.refs_7_.refs_5_ = bf16[2,128,256]{2,1,0:T(8,128)(2,1)S(1)} collective-permute-done((bf16[2,128,256]{2,1,0:T(8,128)(2,1)S(1)}, bf16[2,128,256]{2,1,0:T(8,128)(2,1)S(1)}, u32[]{:S(2)}, u32[]{:S(2)}) %collective-permute-start.3) | collective-permute-done | bytes 131104 | tf_op jit(solution)/shard_map/ppermute | solution.py:510
  19.7 0.1 collective-permute-start.8
  19.8 0.0 collective-permute-done.4.refs_11_
  19.8 0.7 %collective-permute-done.2.refs_4_.refs_3_ = bf16[128,2048]{1,0:T(8,128)(2,1)S(1)} collective-permute-done((bf16[128,2048]{1,0:T(8,128)(2,1)S(1)}, bf16[128,2048]{1,0:T(8,128)(2,1)S(1)}, u32[]{:S(2)}, u32[]{:S(2)}) %collective-permute-start.2) | collective-permute-done | bytes 524320 | tf_op jit(solution)/shard_map/ppermute | solution.py:513
  20.5 0.0 collective-permute-done.5.refs_12_
  20.5 7.2 %attend_0_2_1.1 = (bf16[1104,128]{1,0:T(8,128)(2,1)S(1)}, bf16[1024,128]{1,0:T(8,128)(2,1)S(1)}, f32[8,128]{1,0:T(8,128)S(1)}, bf16[34,16,256]{2,1,0:T(8,128)(2,...) custom-call(s32[1]{0:T(128)S(6)} %copy.19.refs_0_, s32[1,64]{1,0:T(1,128)S(1)} %multiply_add_fusion.refs_1_, ...), custom_call_target="tpu_custom_call" | custom-call | flops 1 | bytes 1 | tf_op jit(solution)/shard_map/attend_0_2_1/pallas_call | solution.py:388
  27.7 0.7 %collective-permute-done.7.refs_7_ = bf16[33,2,32,128]{3,2,1,0:T(8,128)(2,1)S(1)} collective-permute-done((bf16[33,2,32,128]{3,2,1,0:T(8,128)(2,1)S(1)}, bf16[33,2,32,128]{3,2,1,0:T(8,128)(2,1)S(1)}, u32[]{:S(2)}, u32[]{:S(2)}) %collective-permute-start.7) | collective-permute-done | bytes 540704 | tf_op jit(solution)/shard_map/ppermute | solution.py:526
  28.3 0.0 collective-permute-start.9
  28.4 1.7 %collective-permute-start.11 = (bf16[1104,128]{1,0:T(8,128)(2,1)S(1)}, bf16[1104,128]{1,0:T(8,128)(2,1)S(1)}, u32[]{:S(2)}, u32[]{:S(2)}) collective-permute-start(bf16[1104,128]{1,0:T(8,128)(2,1)S(1)} %get-tuple-element.52), channel_id=1, source_target_pairs={{0,8},{4,12},{8,0},{12,4},{1,9},{5,13},{9,1},{13,5},{2,10},{6,14},... | collective-permute-start | bytes 847880 | tf_op jit(solution)/shard_map/ppermute | solution.py:513
  30.1 1.5 %collective-permute-start.6 = (bf16[34,16,256]{2,1,0:T(8,128)(2,1)S(1)}, bf16[34,16,256]{2,1,0:T(8,128)(2,1)S(1)}, u32[]{:S(2)}, u32[]{:S(2)}) collective-permute-start(bf16[34,16,256]{2,1,0:T(8,128)(2,1)S(1)} %get-tuple-element.35.refs_1_), channel_id=1, source_target_pairs={{0,16},{16,0},{1,17},{17,1},{2,18},{18,2},{3,19},{19,3},{4,20},{20... | collective-permute-start | bytes 835592 | tf_op jit(solution)/shard_map/ppermute | solution.py:565
  31.6 0.0 collective-permute-done.8.refs_8_
  31.6 0.0 collective-permute-done.9.refs_9_
  31.6 4.0 %attend_1_1_1.1.refs_2_ = bf16[1056,128]{1,0:T(8,128)(2,1)S(1)} custom-call(bf16[64,32,128]{2,1,0:T(8,128)(2,1)S(1)} %get-tuple-element.36.refs_0_, s32[2,8,128]{2,1,0:T(8,128)S(1)} %get-tuple-element.34.refs_1_.chosen_ref, f32[8,128]{1,0:T(8,128)S(1)} %get-tuple-element.40.refs_2_.l_ref, bf16[128,2048]{1,0:T(8,128)(2,1)S(1)} %collective-permute-done.2.refs_4_.refs_3_, ...), custom_call_target="tpu_custom_call" | custom-call | flops 1 | bytes 1 | tf_op jit(solution)/shard_map/attend_1_1_1/pallas_call | solution.py:388
  35.5 0.6 %collective-permute-start.10 = (bf16[1056,128]{1,0:T(8,128)(2,1)S(1)}, bf16[1056,128]{1,0:T(8,128)(2,1)S(1)}, u32[]{:S(2)}, u32[]{:S(2)}) collective-permute-start(bf16[1056,128]{1,0:T(8,128)(2,1)S(1)} %attend_1_1_1.1.refs_2_), channel_id=1, source_target_pairs={{0,8},{4,12},{8,0},{12,4},{1,9},{5,13},{9,1},{13,5},{2,10},{6,14},... | collective-permute-start | bytes 811016 | tf_op jit(solution)/shard_map/ppermute | solution.py:513
  36.1 3.8 %attend_1_1_0.1 = (bf16[1024,128]{1,0:T(8,128)(2,1)S(1)}, f32[8,128]{1,0:T(8,128)S(1)}) custom-call(bf16[64,32,128]{2,1,0:T(8,128)(2,1)S(1)} %get-tuple-element.36.refs_0_, s32[2,8,128]{2,1,0:T(8,128)S(1)} %get-tuple-element.34.refs_1_.chosen_ref, bf16[1056,128]{1,0:T(8,128)(2,1)S(1)} %attend_1_1_1.1.refs_2_, bf16[128,2048]{1,0:T(8,128)(2,1)S(1)} %bitcast.14, ...), custom_call_target="tpu_custom_call" | custom-call | flops 1 | bytes 1 | tf_op jit(solution)/shard_map/attend_1_1_0/pallas_call | solution.py:388
  39.9 0.0 collective-permute-done.6.refs_2_
  39.9 1.5 %add_saved.1 = (bf16[32,16,512]{2,1,0:T(8,128)(2,1)}, f32[32,16,256]{2,1,0:T(8,128)}, f32[8,128]{1,0:T(8,128)S(1)}) custom-call(s32[1]{0:T(128)S(6)} %copy.20.valid_ref, s32[2,8,128]{2,1,0:T(8,128)S(1)} %get-tuple-element.34.refs_1_.chosen_ref, f32[8,128]{1,0:T(8,128)S(1)} %get-tuple-element.43.refs_0_.l_ref, ...), custom_call_target="tpu_custom_call" | custom-call | flops 1 | bytes 1 | tf_op jit(solution)/shard_map/add_saved/pallas_call | solution.py:176
  41.4 0.0 collective-permute-done.11.got_ref
  41.4 1.0 %merge_0.1.refs_0_ = bf16[128,2048]{1,0:T(8,128)(2,1)} custom-call(s32[1]{0:T(128)S(6)} %copy.20.valid_ref, f32[8,128]{1,0:T(8,128)S(1)} %get-tuple-element.49.after_ref, bf16[1024,128]{1,0:T(8,128)(2,1)S(1)} %get-tuple-element.51.o_ref, f32[8,128]{1,0:T(8,128)S(1)} %get-tuple-element.40.refs_2_.l_ref, bf16[1104,128]{1,0:T(8,128)(2,1)S(1)} %collective-permute-done.11.got_ref), custom_call_target="tpu_custom_call" | custom-call | tf_op jit(solution)/shard_map/merge_0/pallas_call | solution.py:439
  42.4 1.5 %collective-permute-done.10.got_ref = bf16[1056,128]{1,0:T(8,128)(2,1)S(1)} collective-permute-done((bf16[1056,128]{1,0:T(8,128)(2,1)S(1)}, bf16[1056,128]{1,0:T(8,128)(2,1)S(1)}, u32[]{:S(2)}, u32[]{:S(2)}) %collective-permute-start.10) | collective-permute-done | bytes 270368 | tf_op jit(solution)/shard_map/ppermute | solution.py:513
  43.9 1.0 %merge_1.1 = bf16[128,2048]{1,0:T(8,128)(2,1)} custom-call(s32[1]{0:T(128)S(6)} %copy.20.valid_ref, f32[8,128]{1,0:T(8,128)S(1)} %get-tuple-element.49.after_ref, bf16[1024,128]{1,0:T(8,128)(2,1)S(1)} %get-tuple-element.50.o_ref, f32[8,128]{1,0:T(8,128)S(1)} %get-tuple-element.43.refs_0_.l_ref, ...), custom_call_target="tpu_custom_call", output_to_operand_aliasing={{}: (5, {})} | custom-call | tf_op jit(solution)/shard_map/merge_1/pallas_call | solution.py:439
  (12 shorter events, 0.0 us)
Async XLA Ops:
  0.6 4.2 %copy-start.9 = (bf16[1,32,2,32,256]{4,3,2,1,0:T(8,128)(2,1)S(1)}, bf16[1,32,2,32,256]{4,3,2,1,0:T(8,128)(2,1)}, u32[]{:S(2)}) copy-start(bf16[1,32,2,32,256]{4,3,2,1,0:T(8,128)(2,1)} %param.14) | copy-start | bytes 3145732
  1.8 15.8 %collective-permute-start.1 = (bf16[32,2,32,128]{3,2,1,0:T(8,128)(2,1)S(1)}, bf16[32,2,32,128]{3,2,1,0:T(8,128)(2,1)S(1)}, u32[]{:S(2)}, u32[]{:S(2)}) collective-permute-start(bf16[32,2,32,128]{3,2,1,0:T(8,128)(2,1)S(1)} %slice.13.refs_9_), channel_id=1, source_target_pairs={{0,16},{16,0},{1,17},{17,1},{2,18},{18,2},{3,19},{19,3},{4,20},{20... | collective-permute-start | bytes 1572872 | tf_op jit(solution)/shard_map/ppermute | solution.py:526
  4.8 15.0 %collective-permute-start.4 = (bf16[32,2,32,128]{3,2,1,0:T(8,128)(2,1)S(1)}, bf16[32,2,32,128]{3,2,1,0:T(8,128)(2,1)S(1)}, u32[]{:S(2)}, u32[]{:S(2)}) collective-permute-start(bf16[32,2,32,128]{3,2,1,0:T(8,128)(2,1)S(1)} %slice.13.refs_9_), channel_id=1, source_target_pairs={{0,4},{4,0},{8,12},{12,8},{1,5},{5,1},{9,13},{13,9},{2,6},{6,2},{1... | collective-permute-start | bytes 1572872 | tf_op jit(solution)/shard_map/ppermute | solution.py:510
  4.8 3.6 %copy-start.3 = (bf16[1,32,16,512]{3,2,1,0:T(8,128)(2,1)S(1)}, bf16[1,32,16,512]{3,2,1,0:T(8,128)(2,1)}, u32[]{:S(2)}) copy-start(bf16[1,32,16,512]{3,2,1,0:T(8,128)(2,1)} %param.20) | copy-start | bytes 1572868
  4.8 3.6 %copy-start.4 = (bf16[1,2,256,512]{3,2,1,0:T(8,128)(2,1)S(1)}, bf16[1,2,256,512]{3,2,1,0:T(8,128)(2,1)}, u32[]{:S(2)}) copy-start(bf16[1,2,256,512]{3,2,1,0:T(8,128)(2,1)} %param.21) | copy-start | bytes 1572868
  5.0 0.7 %copy-start.10 = (s32[1,64]{1,0:T(1,128)S(1)}, s32[1,64]{1,0:T(1,128)}, u32[]{:S(2)}) copy-start(s32[1,64]{1,0:T(1,128)} %param.17) | copy-start | bytes 772
  5.0 0.7 %copy-start.11 = (s32[1,64]{1,0:T(1,128)S(1)}, s32[1,64]{1,0:T(1,128)}, u32[]{:S(2)}) copy-start(s32[1,64]{1,0:T(1,128)} %param.16) | copy-start | bytes 772
  5.0 3.4 %copy-start.6 = (f32[1,32,512]{2,1,0:T(8,128)S(1)}, f32[1,32,512]{2,1,0:T(8,128)}, u32[]{:S(2)}) copy-start(f32[1,32,512]{2,1,0:T(8,128)} %param.23) | copy-start | bytes 196612
  5.0 1.2 %copy-start = (bf16[1,128,2048]{2,1,0:T(8,128)(2,1)S(1)}, bf16[1,128,2048]{2,1,0:T(8,128)(2,1)}, u32[]{:S(2)}) copy-start(bf16[1,128,2048]{2,1,0:T(8,128)(2,1)} %param.26) | copy-start | bytes 1572868
  5.0 3.4 %copy-start.1 = (bf16[1,2,256,512]{3,2,1,0:T(8,128)(2,1)S(1)}, bf16[1,2,256,512]{3,2,1,0:T(8,128)(2,1)}, u32[]{:S(2)}) copy-start(bf16[1,2,256,512]{3,2,1,0:T(8,128)(2,1)} %param.22) | copy-start | bytes 1572868
  5.1 23.3 %collective-permute-start.7 = (bf16[33,2,32,128]{3,2,1,0:T(8,128)(2,1)S(1)}, bf16[33,2,32,128]{3,2,1,0:T(8,128)(2,1)S(1)}, u32[]{:S(2)}, u32[]{:S(2)}) collective-permute-start(bf16[33,2,32,128]{3,2,1,0:T(8,128)(2,1)S(1)} %pad_maximum_fusion.refs_6_), channel_id=1, source_target_pairs={{0,16},{16,0},{1,17},{17,1},{2,18},{18,2},{3,19},{19,3},{4,20},{20... | collective-permute-start | bytes 1622024 | tf_op jit(solution)/shard_map/ppermute | solution.py:526
  5.7 2.6 %collective-permute-start = (s32[1,64]{1,0:T(1,128)S(1)}, s32[1,64]{1,0:T(1,128)S(1)}, u32[]{:S(2)}, u32[]{:S(2)}) collective-permute-start(s32[1,64]{1,0:T(1,128)S(1)} %multiply_add_fusion.refs_1_), channel_id=1, source_target_pairs={{0,4},{4,0},{8,12},{12,8},{1,5},{5,1},{9,13},{13,9},{2,6},{6,2},{1... | collective-permute-start | bytes 776 | tf_op jit(solution)/shard_map/ppermute | solution.py:510
  6.2 14.3 %collective-permute-start.2 = (bf16[128,2048]{1,0:T(8,128)(2,1)S(1)}, bf16[128,2048]{1,0:T(8,128)(2,1)S(1)}, u32[]{:S(2)}, u32[]{:S(2)}) collective-permute-start(bf16[128,2048]{1,0:T(8,128)(2,1)S(1)} %bitcast.12), channel_id=1, source_target_pairs={{0,8},{4,12},{8,0},{12,4},{1,9},{5,13},{9,1},{13,5},{2,10},{6,14},... | collective-permute-start | bytes 1572872 | tf_op jit(solution)/shard_map/ppermute | solution.py:513
  8.4 0.7 %copy-start.7 = (f32[32]{0:T(128)S(1)}, f32[32]{0:T(128)}, u32[]{:S(2)}) copy-start(f32[32]{0:T(128)} %param.24) | copy-start | bytes 388
  8.4 0.7 %copy-start.8 = (f32[32]{0:T(128)S(1)}, f32[32]{0:T(128)}, u32[]{:S(2)}) copy-start(f32[32]{0:T(128)} %param.25) | copy-start | bytes 388
  9.0 8.6 %copy-start.2 = (bf16[1,2,128,256]{3,2,1,0:T(8,128)(2,1)S(1)}, bf16[1,2,128,256]{3,2,1,0:T(8,128)(2,1)}, u32[]{:S(2)}) copy-start(bf16[1,2,128,256]{3,2,1,0:T(8,128)(2,1)} %param.27) | copy-start | bytes 393220
  9.0 11.5 %copy-start.5 = (bf16[32,16,256]{2,1,0:T(8,128)(2,1)S(1)}, bf16[32,16,256]{2,1,0:T(8,128)(2,1)}, u32[]{:S(2)}) copy-start(bf16[32,16,256]{2,1,0:T(8,128)(2,1)} %refs_8_.1) | copy-start | bytes 786436
  17.6 2.9 %collective-permute-start.5 = (bf16[32,2,32,128]{3,2,1,0:T(8,128)(2,1)S(1)}, bf16[32,2,32,128]{3,2,1,0:T(8,128)(2,1)S(1)}, u32[]{:S(2)}, u32[]{:S(2)}) collective-permute-start(bf16[32,2,32,128]{3,2,1,0:T(8,128)(2,1)S(1)} %collective-permute-done.1.refs_10_), channel_id=1, source_target_pairs={{0,4},{4,0},{8,12},{12,8},{1,5},{5,1},{9,13},{13,9},{2,6},{6,2},{1... | collective-permute-start | bytes 1572872 | tf_op jit(solution)/shard_map/ppermute | solution.py:510
  17.6 2.1 %collective-permute-start.3 = (bf16[2,128,256]{2,1,0:T(8,128)(2,1)S(1)}, bf16[2,128,256]{2,1,0:T(8,128)(2,1)S(1)}, u32[]{:S(2)}, u32[]{:S(2)}) collective-permute-start(bf16[2,128,256]{2,1,0:T(8,128)(2,1)S(1)} %bitcast.17), channel_id=1, source_target_pairs={{0,4},{4,0},{8,12},{12,8},{1,5},{5,1},{9,13},{13,9},{2,6},{6,2},{1... | collective-permute-start | bytes 393224 | tf_op jit(solution)/shard_map/ppermute | solution.py:510
  19.7 11.9 %collective-permute-start.8 = (bf16[33,2,32,128]{3,2,1,0:T(8,128)(2,1)S(1)}, bf16[33,2,32,128]{3,2,1,0:T(8,128)(2,1)S(1)}, u32[]{:S(2)}, u32[]{:S(2)}) collective-permute-start(bf16[33,2,32,128]{3,2,1,0:T(8,128)(2,1)S(1)} %pad_maximum_fusion.refs_6_), channel_id=1, source_target_pairs={{0,4},{4,0},{8,12},{12,8},{1,5},{5,1},{9,13},{13,9},{2,6},{6,2},{1... | collective-permute-start | bytes 1622024 | tf_op jit(solution)/shard_map/ppermute | solution.py:510
  28.3 3.2 %collective-permute-start.9 = (bf16[33,2,32,128]{3,2,1,0:T(8,128)(2,1)S(1)}, bf16[33,2,32,128]{3,2,1,0:T(8,128)(2,1)S(1)}, u32[]{:S(2)}, u32[]{:S(2)}) collective-permute-start(bf16[33,2,32,128]{3,2,1,0:T(8,128)(2,1)S(1)} %collective-permute-done.7.refs_7_), channel_id=1, source_target_pairs={{0,4},{4,0},{8,12},{12,8},{1,5},{5,1},{9,13},{13,9},{2,6},{6,2},{1... | collective-permute-start | bytes 1622024 | tf_op jit(solution)/shard_map/ppermute | solution.py:510
  28.4 13.0 %collective-permute-start.11 = (bf16[1104,128]{1,0:T(8,128)(2,1)S(1)}, bf16[1104,128]{1,0:T(8,128)(2,1)S(1)}, u32[]{:S(2)}, u32[]{:S(2)}) collective-permute-start(bf16[1104,128]{1,0:T(8,128)(2,1)S(1)} %get-tuple-element.52), channel_id=1, source_target_pairs={{0,8},{4,12},{8,0},{12,4},{1,9},{5,13},{9,1},{13,5},{2,10},{6,14},... | collective-permute-start | bytes 847880 | tf_op jit(solution)/shard_map/ppermute | solution.py:513
  30.1 9.8 %collective-permute-start.6 = (bf16[34,16,256]{2,1,0:T(8,128)(2,1)S(1)}, bf16[34,16,256]{2,1,0:T(8,128)(2,1)S(1)}, u32[]{:S(2)}, u32[]{:S(2)}) collective-permute-start(bf16[34,16,256]{2,1,0:T(8,128)(2,1)S(1)} %get-tuple-element.35.refs_1_), channel_id=1, source_target_pairs={{0,16},{16,0},{1,17},{17,1},{2,18},{18,2},{3,19},{19,3},{4,20},{20... | collective-permute-start | bytes 835592 | tf_op jit(solution)/shard_map/ppermute | solution.py:565
  35.5 8.4 %collective-permute-start.10 = (bf16[1056,128]{1,0:T(8,128)(2,1)S(1)}, bf16[1056,128]{1,0:T(8,128)(2,1)S(1)}, u32[]{:S(2)}, u32[]{:S(2)}) collective-permute-start(bf16[1056,128]{1,0:T(8,128)(2,1)S(1)} %attend_1_1_1.1.refs_2_), channel_id=1, source_target_pairs={{0,8},{4,12},{8,0},{12,4},{1,9},{5,13},{9,1},{13,5},{2,10},{6,14},... | collective-permute-start | bytes 811016 | tf_op jit(solution)/shard_map/ppermute | solution.py:513

commit v5 on v3

--- a/solution.py
+++ b/solution.py
@@ -139,7 +139,7 @@
     groups, states, _ = c_ref.shape
     per = heads // groups
     copies = []
-    chosen = jnp.max(chosen_ref[0])
+    chosen = jnp.max(chosen_ref[0].astype(jnp.float32))
     for kind in range(kinds):
 
         @pl.when(chosen == kind)
@@ -234,27 +234,36 @@
         found = [locate(kinds, table_refs[side], pages) for side in range(2)]
         chosen = [kind for kind, _ in found]
         for side in range(2):
-            chosen_ref[side] = jnp.full(chosen_ref.shape[1:], chosen[side], jnp.int32)
+            chosen_ref[side] = jnp.full(chosen_ref.shape[1:], chosen[side], jnp.int32).astype(
+                jnp.bfloat16
+            )
     else:
-        chosen = [jnp.max(chosen_ref[side]) for side in range(2)]
-
-    def take_pages(side, kind):
+        chosen = [0, 0]
+
+    def read_pages(side, kind):
         sources = kv_refs[side][kind]
         lanes = columns if sources[0].shape[-1] > HEAD_DIM else slice(0, HEAD_DIM)
-        target = slice(side * pages, (side + 1) * pages)
-        for half, place in enumerate((keys, values)):
-            if len(sources) == 1:
-                taken = sources[0][:pages, half, :, lanes]
-            else:
-                taken = sources[half][:pages, :, lanes]
-            place[target, :, :HEAD_DIM] = taken
+        if len(sources) == 1:
+            return [sources[0][:pages, half, :, lanes] for half in range(2)]
+        return [sources[half][:pages, :, lanes] for half in range(2)]
+
+    def take_pages(side, kind):
+        for place, taken in zip((keys, values), read_pages(side, kind)):
+            place[side * pages : (side + 1) * pages, :, :HEAD_DIM] = taken
 
     for side in range(2):
-        for kind in range(kinds):
-
-            @pl.when(chosen[side] == kind)
-            def _():
-                take_pages(side, kind)
+        if head and kinds == 2:
+            first_one, other = (read_pages(side, kind) for kind in range(2))
+            target = slice(side * pages, (side + 1) * pages)
+            weight = chosen_ref[side][:1][None]
+            for half, place in enumerate((keys, values)):
+                place[target, :, :HEAD_DIM] = first_one[half] * (1 - weight) + other[half] * weight
+        else:
+            for kind in range(kinds):
+
+                @pl.when(chosen[side] == kind)
+                def _():
+                    take_pages(side, kind)
 
     if head == 0:
         in_page = lax.broadcasted_iota(jnp.int32, (page, HEAD_DIM), 0)
@@ -384,7 +393,7 @@
         )
     if head == 0:
         shapes.append(jax.ShapeDtypeStruct((2 * pages, page, HEAD_DIM), jnp.bfloat16))
-        shapes.append(jax.ShapeDtypeStruct((2, 8, 128), jnp.int32))
+        shapes.append(jax.ShapeDtypeStruct((2, 16, 128), jnp.bfloat16))
     return pl.pallas_call(
         functools.partial(attend_kernel, counts, head, sides, padding),
         in_specs=([scalar] * 3 if head == 0 else [whole] * 2) + [outside] + [whole] * (2 + len(sides) + len(flat)),

time: 45.5 us -> 45.4 us (level)
  transfers between devices with their start and end apart: 12 -> 12, of which waited for: 5 -> 4; matrix products, arithmetic and copies ran while one was open for 0% -> 0% of each run, Pallas kernels for 53% -> 53%
where the time goes in v5:
time: 45.4 us; the launch traced here: 45.2 us
  Pallas kernels  24.9 us (55%)
  starting transfers between devices  10.1 us (22%)
  waiting for transfers between devices  5.06 us (11%)
  local copies, waits for them, and re-layouts  2.76 us (6%)
  between operations  2.31 us (5%)
    pallas_call x3, Pallas kernels, attend(): pl.pallas_call(functools.partial(attend_kernel, counts, head, sides, padd...  14.8 us
    pallas_call x1, Pallas kernels, mixer_from_zero(): pl.pallas_call(mixer_kernel, grid=(groups,), in_specs=[scalar, pl.BlockSp...  6.63 us
    ppermute x3, starting transfers between devices, to_opposite(): return lax.ppermute(array, 'ctx', opposite)  4.09 us
    ppermute x2, starting transfers between devices, local(): moved.append(tuple((lax.ppermute(piece, 'pool', swap) for piece in cut)))  3.23 us
    pallas_call x2, Pallas kernels, merge(): pl.pallas_call(functools.partial(merge_kernel, head), in_specs=[scalar, o...  2.07 us
    ppermute x2, waiting for transfers between devices, local(): moved.append(tuple((lax.ppermute(piece, 'pool', swap) for piece in cut)))  2.02 us
    ppermute x6, waiting for transfers between devices, to_partner(): return lax.ppermute(array, 'ctx', partner)  1.89 us
    ppermute x1, starting transfers between devices, local(): slab = lax.ppermute(ordered, 'pool', swap)  1.52 us
  transfers between devices with their start and end apart: 12, of which 4 were waited for; matrix products, arithmetic and copies ran while one was open for 0% of the time, Pallas kernels for 53%

profile of v5, /device:TPU:0, one launch (start us, length us, event | category | flops | bytes accessed | tf_op | source)
XLA Modules:
  0.0 45.2 jit_solution(3859335023919257517)
XLA Ops:
  0.6 0.0 copy-start.9
  0.6 1.2 %slice.13.refs_9_ = bf16[32,2,32,128]{3,2,1,0:T(8,128)(2,1)S(1)} slice(bf16[32,2,32,256]{3,2,1,0:T(8,128)(2,1)} %bitcast.27), slice={[0:32], [0:2], [0:32], [0:128]} | slice | bytes 1048576 | tf_op jit(solution)/shard_map/slice | solution.py:529
  1.8 3.0 %collective-permute-start.1 = (bf16[32,2,32,128]{3,2,1,0:T(8,128)(2,1)S(1)}, bf16[32,2,32,128]{3,2,1,0:T(8,128)(2,1)S(1)}, u32[]{:S(2)}, u32[]{:S(2)}) collective-permute-start(bf16[32,2,32,128]{3,2,1,0:T(8,128)(2,1)S(1)} %slice.13.refs_9_), channel_id=1, source_target_pairs={{0,16},{16,0},{1,17},{17,1},{2,18},{18,2},{3,19},{19,3},{4,20},{20... | collective-permute-start | bytes 1572872 | tf_op jit(solution)/shard_map/ppermute | solution.py:535
  4.8 0.0 copy-done.9
  4.8 0.1 slice.11
  5.0 0.0 copy-start.6
  5.0 0.0 copy-start
  5.0 0.0 copy-start.1
  5.0 0.1 pad_maximum_fusion.refs_6_
  5.1 0.2 collective-permute-start.7
  5.3 0.0 collective-permute-start.4
  5.3 0.8 %copy-done = bf16[1,128,2048]{2,1,0:T(8,128)(2,1)S(1)} copy-done((bf16[1,128,2048]{2,1,0:T(8,128)(2,1)S(1)}, bf16[1,128,2048]{2,1,0:T(8,128)(2,1)}, u32[]{:S(2)}) %copy-start) | copy-done | bytes 524312
  6.1 1.5 %collective-permute-start.2 = (bf16[128,2048]{1,0:T(8,128)(2,1)S(1)}, bf16[128,2048]{1,0:T(8,128)(2,1)S(1)}, u32[]{:S(2)}, u32[]{:S(2)}) collective-permute-start(bf16[128,2048]{1,0:T(8,128)(2,1)S(1)} %bitcast.12), channel_id=1, source_target_pairs={{0,8},{4,12},{8,0},{12,4},{1,9},{5,13},{9,1},{13,5},{2,10},{6,14},... | collective-permute-start | bytes 1572872 | tf_op jit(solution)/shard_map/ppermute | solution.py:522
  8.2 0.0 copy-start.7
  8.3 0.0 copy-start.8
  8.3 0.0 copy-done.3
  8.3 0.0 copy-done.4
  8.3 0.6 %copy-done.7 = f32[32]{0:T(128)S(1)} copy-done((f32[32]{0:T(128)S(1)}, f32[32]{0:T(128)}, u32[]{:S(2)}) %copy-start.7) | copy-done | bytes 152
  8.9 0.0 copy-done.8
  8.9 6.6 %mixer_from_zero.1 = (f32[32,16,512]{2,1,0:T(8,128)S(1)}, f32[32,16,256]{2,1,0:T(8,128)S(1)}, f32[32,512]{1,0:T(8,128)S(1)}) custom-call(s32[1]{0:T(128)S(6)} %copy.20.valid_ref, bf16[32,16,512]{2,1,0:T(8,128)(2,1)S(1)} %bitcast.21, bf16[2,256,512]{2,1,0:T(8,128)(2,1)S(1)} %bitcast.22, bf16[2,256,512]{2,1,0:T(8,128)(2,1)S(1)} %bitcast.15, ...), custom_call_target="tpu_custom_call" | custom-call | flops 1 | bytes 1 | tf_op jit(solution)/shard_map/mixer_from_zero/pallas_call | solution.py:103
  15.6 0.0 copy-start.10
  15.6 0.0 copy-start.11
  15.6 2.0 %collective-permute-done.1.refs_10_ = bf16[32,2,32,128]{3,2,1,0:T(8,128)(2,1)S(1)} collective-permute-done((bf16[32,2,32,128]{3,2,1,0:T(8,128)(2,1)S(1)}, bf16[32,2,32,128]{3,2,1,0:T(8,128)(2,1)S(1)}, u32[]{:S(2)}, u32[]{:S(2)}) %collective-permute-start.1) | collective-permute-done | bytes 524320 | tf_op jit(solution)/shard_map/ppermute | solution.py:535
  17.6 0.0 collective-permute-start.5
  17.6 0.6 %collective-permute-start = (s32[1,64]{1,0:T(1,128)S(1)}, s32[1,64]{1,0:T(1,128)S(1)}, u32[]{:S(2)}, u32[]{:S(2)}) collective-permute-start(s32[1,64]{1,0:T(1,128)S(1)} %multiply_add_fusion.refs_1_), channel_id=1, source_target_pairs={{0,4},{4,0},{8,12},{12,8},{1,5},{5,1},{9,13},{13,9},{2,6},{6,2},{1... | collective-permute-start | bytes 776 | tf_op jit(solution)/shard_map/ppermute | solution.py:519
  18.2 1.3 %collective-permute-done.refs_2_ = s32[1,64]{1,0:T(1,128)S(1)} collective-permute-done((s32[1,64]{1,0:T(1,128)S(1)}, s32[1,64]{1,0:T(1,128)S(1)}, u32[]{:S(2)}, u32[]{:S(2)}) %collective-permute-start) | collective-permute-done | bytes 288 | tf_op jit(solution)/shard_map/ppermute | solution.py:519
  19.5 0.1 collective-permute-start.3
  20.3 0.6 %collective-permute-done.3.refs_7_.refs_5_ = bf16[2,128,256]{2,1,0:T(8,128)(2,1)S(1)} collective-permute-done((bf16[2,128,256]{2,1,0:T(8,128)(2,1)S(1)}, bf16[2,128,256]{2,1,0:T(8,128)(2,1)S(1)}, u32[]{:S(2)}, u32[]{:S(2)}) %collective-permute-start.3) | collective-permute-done | bytes 131104 | tf_op jit(solution)/shard_map/ppermute | solution.py:519
  20.9 0.1 collective-permute-start.8
  21.0 0.0 collective-permute-done.4.refs_11_
  21.0 0.0 collective-permute-done.2.refs_4_.refs_3_
  21.0 0.0 collective-permute-done.5.refs_12_
  21.0 7.4 %attend_0_2_1.1 = (bf16[1104,128]{1,0:T(8,128)(2,1)S(1)}, bf16[1024,128]{1,0:T(8,128)(2,1)S(1)}, f32[8,128]{1,0:T(8,128)S(1)}, bf16[34,16,256]{2,1,0:T(8,128)(2,...) custom-call(s32[1]{0:T(128)S(6)} %copy.19.refs_0_, s32[1,64]{1,0:T(1,128)S(1)} %multiply_add_fusion.refs_1_, ...), custom_call_target="tpu_custom_call" | custom-call | flops 1 | bytes 1 | tf_op jit(solution)/shard_map/attend_0_2_1/pallas_call | solution.py:397
  28.4 0.0 collective-permute-done.7.refs_7_
  28.4 0.4 collective-permute-start.9
  28.8 2.0 %collective-permute-start.11 = (bf16[1104,128]{1,0:T(8,128)(2,1)S(1)}, bf16[1104,128]{1,0:T(8,128)(2,1)S(1)}, u32[]{:S(2)}, u32[]{:S(2)}) collective-permute-start(bf16[1104,128]{1,0:T(8,128)(2,1)S(1)} %get-tuple-element.48), channel_id=1, source_target_pairs={{0,8},{4,12},{8,0},{12,4},{1,9},{5,13},{9,1},{13,5},{2,10},{6,14},... | collective-permute-start | bytes 847880 | tf_op jit(solution)/shard_map/ppermute | solution.py:522
  30.8 1.5 %collective-permute-start.6 = (bf16[34,16,256]{2,1,0:T(8,128)(2,1)S(1)}, bf16[34,16,256]{2,1,0:T(8,128)(2,1)S(1)}, u32[]{:S(2)}, u32[]{:S(2)}) collective-permute-start(bf16[34,16,256]{2,1,0:T(8,128)(2,1)S(1)} %get-tuple-element.31.refs_1_), channel_id=1, source_target_pairs={{0,16},{16,0},{1,17},{17,1},{2,18},{18,2},{3,19},{19,3},{4,20},{20... | collective-permute-start | bytes 835592 | tf_op jit(solution)/shard_map/ppermute | solution.py:573
  32.4 0.0 collective-permute-done.8.refs_8_
  32.4 0.0 collective-permute-done.9.refs_9_
  32.4 3.6 %attend_1_1_1.1.refs_2_ = bf16[1056,128]{1,0:T(8,128)(2,1)S(1)} custom-call(bf16[64,32,128]{2,1,0:T(8,128)(2,1)S(1)} %get-tuple-element.32.refs_0_, bf16[2,16,128]{2,1,0:T(8,128)(2,1)S(1)} %get-tuple-element.30.refs_1_.chosen_ref, f32[8,128]{1,0:T(8,128)S(1)} %get-tuple-element.36.refs_2_.l_ref, ...), custom_call_target="tpu_custom_call" | custom-call | flops 1 | bytes 1 | tf_op jit(solution)/shard_map/attend_1_1_1/pallas_call | solution.py:397
  36.0 0.6 %collective-permute-start.10 = (bf16[1056,128]{1,0:T(8,128)(2,1)S(1)}, bf16[1056,128]{1,0:T(8,128)(2,1)S(1)}, u32[]{:S(2)}, u32[]{:S(2)}) collective-permute-start(bf16[1056,128]{1,0:T(8,128)(2,1)S(1)} %attend_1_1_1.1.refs_2_), channel_id=1, source_target_pairs={{0,8},{4,12},{8,0},{12,4},{1,9},{5,13},{9,1},{13,5},{2,10},{6,14},... | collective-permute-start | bytes 811016 | tf_op jit(solution)/shard_map/ppermute | solution.py:522
  36.5 3.8 %attend_1_1_0.1 = (bf16[1024,128]{1,0:T(8,128)(2,1)S(1)}, f32[8,128]{1,0:T(8,128)S(1)}) custom-call(bf16[64,32,128]{2,1,0:T(8,128)(2,1)S(1)} %get-tuple-element.32.refs_0_, bf16[2,16,128]{2,1,0:T(8,128)(2,1)S(1)} %get-tuple-element.30.refs_1_.chosen_ref, bf16[1056,128]{1,0:T(8,128)(2,1)S(1)} %attend_1_1_1.1.refs_2_, bf16[128,2048]{1,0:T(8,128)(2,1)S(1)} %bitcast.14, ...), custom_call_target="tpu_custom_call" | custom-call | flops 1 | bytes 1 | tf_op jit(solution)/shard_map/attend_1_1_0/pallas_call | solution.py:397
  40.4 0.0 collective-permute-done.6.refs_2_
  40.4 1.4 %add_saved.1 = (bf16[32,16,512]{2,1,0:T(8,128)(2,1)}, f32[32,16,256]{2,1,0:T(8,128)}, f32[8,128]{1,0:T(8,128)S(1)}) custom-call(s32[1]{0:T(128)S(6)} %copy.20.valid_ref, bf16[2,16,128]{2,1,0:T(8,128)(2,1)S(1)} %get-tuple-element.30.refs_1_.chosen_ref, f32[8,128]{1,0:T(8,128)S(1)} %get-tuple-element.39.refs_0_.l_ref, ...), custom_call_target="tpu_custom_call" | custom-call | flops 1 | bytes 1 | tf_op jit(solution)/shard_map/add_saved/pallas_call | solution.py:176
  41.8 0.0 collective-permute-done.11.got_ref
  41.8 1.0 %merge_0.1.refs_0_ = bf16[128,2048]{1,0:T(8,128)(2,1)} custom-call(s32[1]{0:T(128)S(6)} %copy.20.valid_ref, f32[8,128]{1,0:T(8,128)S(1)} %get-tuple-element.45.after_ref, bf16[1024,128]{1,0:T(8,128)(2,1)S(1)} %get-tuple-element.47.o_ref, f32[8,128]{1,0:T(8,128)S(1)} %get-tuple-element.36.refs_2_.l_ref, bf16[1104,128]{1,0:T(8,128)(2,1)S(1)} %collective-permute-done.11.got_ref), custom_call_target="tpu_custom_call" | custom-call | tf_op jit(solution)/shard_map/merge_0/pallas_call | solution.py:448
  42.8 1.1 %collective-permute-done.10.got_ref = bf16[1056,128]{1,0:T(8,128)(2,1)S(1)} collective-permute-done((bf16[1056,128]{1,0:T(8,128)(2,1)S(1)}, bf16[1056,128]{1,0:T(8,128)(2,1)S(1)}, u32[]{:S(2)}, u32[]{:S(2)}) %collective-permute-start.10) | collective-permute-done | bytes 270368 | tf_op jit(solution)/shard_map/ppermute | solution.py:522
  44.0 1.0 %merge_1.1 = bf16[128,2048]{1,0:T(8,128)(2,1)} custom-call(s32[1]{0:T(128)S(6)} %copy.20.valid_ref, f32[8,128]{1,0:T(8,128)S(1)} %get-tuple-element.45.after_ref, bf16[1024,128]{1,0:T(8,128)(2,1)S(1)} %get-tuple-element.46.o_ref, f32[8,128]{1,0:T(8,128)S(1)} %get-tuple-element.39.refs_0_.l_ref, ...), custom_call_target="tpu_custom_call", output_to_operand_aliasing={{}: (5, {})} | custom-call | tf_op jit(solution)/shard_map/merge_1/pallas_call | solution.py:448
  (12 shorter events, 0.0 us)
Async XLA Ops:
  0.6 4.2 %copy-start.9 = (bf16[1,32,2,32,256]{4,3,2,1,0:T(8,128)(2,1)S(1)}, bf16[1,32,2,32,256]{4,3,2,1,0:T(8,128)(2,1)}, u32[]{:S(2)}) copy-start(bf16[1,32,2,32,256]{4,3,2,1,0:T(8,128)(2,1)} %param.14) | copy-start | bytes 3145732
  1.8 15.8 %collective-permute-start.1 = (bf16[32,2,32,128]{3,2,1,0:T(8,128)(2,1)S(1)}, bf16[32,2,32,128]{3,2,1,0:T(8,128)(2,1)S(1)}, u32[]{:S(2)}, u32[]{:S(2)}) collective-permute-start(bf16[32,2,32,128]{3,2,1,0:T(8,128)(2,1)S(1)} %slice.13.refs_9_), channel_id=1, source_target_pairs={{0,16},{16,0},{1,17},{17,1},{2,18},{18,2},{3,19},{19,3},{4,20},{20... | collective-permute-start | bytes 1572872 | tf_op jit(solution)/shard_map/ppermute | solution.py:535
  4.8 3.4 %copy-start.3 = (bf16[1,32,16,512]{3,2,1,0:T(8,128)(2,1)S(1)}, bf16[1,32,16,512]{3,2,1,0:T(8,128)(2,1)}, u32[]{:S(2)}) copy-start(bf16[1,32,16,512]{3,2,1,0:T(8,128)(2,1)} %param.20) | copy-start | bytes 1572868
  4.8 3.4 %copy-start.4 = (bf16[1,2,256,512]{3,2,1,0:T(8,128)(2,1)S(1)}, bf16[1,2,256,512]{3,2,1,0:T(8,128)(2,1)}, u32[]{:S(2)}) copy-start(bf16[1,2,256,512]{3,2,1,0:T(8,128)(2,1)} %param.21) | copy-start | bytes 1572868
  5.0 3.3 %copy-start.6 = (f32[1,32,512]{2,1,0:T(8,128)S(1)}, f32[1,32,512]{2,1,0:T(8,128)}, u32[]{:S(2)}) copy-start(f32[1,32,512]{2,1,0:T(8,128)} %param.23) | copy-start | bytes 196612
  5.0 1.1 %copy-start = (bf16[1,128,2048]{2,1,0:T(8,128)(2,1)S(1)}, bf16[1,128,2048]{2,1,0:T(8,128)(2,1)}, u32[]{:S(2)}) copy-start(bf16[1,128,2048]{2,1,0:T(8,128)(2,1)} %param.26) | copy-start | bytes 1572868
  5.0 3.3 %copy-start.1 = (bf16[1,2,256,512]{3,2,1,0:T(8,128)(2,1)S(1)}, bf16[1,2,256,512]{3,2,1,0:T(8,128)(2,1)}, u32[]{:S(2)}) copy-start(bf16[1,2,256,512]{3,2,1,0:T(8,128)(2,1)} %param.22) | copy-start | bytes 1572868
  5.1 23.3 %collective-permute-start.7 = (bf16[33,2,32,128]{3,2,1,0:T(8,128)(2,1)S(1)}, bf16[33,2,32,128]{3,2,1,0:T(8,128)(2,1)S(1)}, u32[]{:S(2)}, u32[]{:S(2)}) collective-permute-start(bf16[33,2,32,128]{3,2,1,0:T(8,128)(2,1)S(1)} %pad_maximum_fusion.refs_6_), channel_id=1, source_target_pairs={{0,16},{16,0},{1,17},{17,1},{2,18},{18,2},{3,19},{19,3},{4,20},{20... | collective-permute-start | bytes 1622024 | tf_op jit(solution)/shard_map/ppermute | solution.py:535
  5.3 15.7 %collective-permute-start.4 = (bf16[32,2,32,128]{3,2,1,0:T(8,128)(2,1)S(1)}, bf16[32,2,32,128]{3,2,1,0:T(8,128)(2,1)S(1)}, u32[]{:S(2)}, u32[]{:S(2)}) collective-permute-start(bf16[32,2,32,128]{3,2,1,0:T(8,128)(2,1)S(1)} %slice.13.refs_9_), channel_id=1, source_target_pairs={{0,4},{4,0},{8,12},{12,8},{1,5},{5,1},{9,13},{13,9},{2,6},{6,2},{1... | collective-permute-start | bytes 1572872 | tf_op jit(solution)/shard_map/ppermute | solution.py:519
  6.1 14.9 %collective-permute-start.2 = (bf16[128,2048]{1,0:T(8,128)(2,1)S(1)}, bf16[128,2048]{1,0:T(8,128)(2,1)S(1)}, u32[]{:S(2)}, u32[]{:S(2)}) collective-permute-start(bf16[128,2048]{1,0:T(8,128)(2,1)S(1)} %bitcast.12), channel_id=1, source_target_pairs={{0,8},{4,12},{8,0},{12,4},{1,9},{5,13},{9,1},{13,5},{2,10},{6,14},... | collective-permute-start | bytes 1572872 | tf_op jit(solution)/shard_map/ppermute | solution.py:522
  8.2 0.7 %copy-start.7 = (f32[32]{0:T(128)S(1)}, f32[32]{0:T(128)}, u32[]{:S(2)}) copy-start(f32[32]{0:T(128)} %param.24) | copy-start | bytes 388
  8.3 0.7 %copy-start.8 = (f32[32]{0:T(128)S(1)}, f32[32]{0:T(128)}, u32[]{:S(2)}) copy-start(f32[32]{0:T(128)} %param.25) | copy-start | bytes 388
  8.9 10.6 %copy-start.2 = (bf16[1,2,128,256]{3,2,1,0:T(8,128)(2,1)S(1)}, bf16[1,2,128,256]{3,2,1,0:T(8,128)(2,1)}, u32[]{:S(2)}) copy-start(bf16[1,2,128,256]{3,2,1,0:T(8,128)(2,1)} %param.27) | copy-start | bytes 393220
  8.9 12.1 %copy-start.5 = (bf16[32,16,256]{2,1,0:T(8,128)(2,1)S(1)}, bf16[32,16,256]{2,1,0:T(8,128)(2,1)}, u32[]{:S(2)}) copy-start(bf16[32,16,256]{2,1,0:T(8,128)(2,1)} %refs_8_.1) | copy-start | bytes 786436
  15.6 2.0 %copy-start.10 = (s32[1,64]{1,0:T(1,128)S(1)}, s32[1,64]{1,0:T(1,128)}, u32[]{:S(2)}) copy-start(s32[1,64]{1,0:T(1,128)} %param.17) | copy-start | bytes 772
  15.6 2.0 %copy-start.11 = (s32[1,64]{1,0:T(1,128)S(1)}, s32[1,64]{1,0:T(1,128)}, u32[]{:S(2)}) copy-start(s32[1,64]{1,0:T(1,128)} %param.16) | copy-start | bytes 772
  17.6 3.4 %collective-permute-start.5 = (bf16[32,2,32,128]{3,2,1,0:T(8,128)(2,1)S(1)}, bf16[32,2,32,128]{3,2,1,0:T(8,128)(2,1)S(1)}, u32[]{:S(2)}, u32[]{:S(2)}) collective-permute-start(bf16[32,2,32,128]{3,2,1,0:T(8,128)(2,1)S(1)} %collective-permute-done.1.refs_10_), channel_id=1, source_target_pairs={{0,4},{4,0},{8,12},{12,8},{1,5},{5,1},{9,13},{13,9},{2,6},{6,2},{1... | collective-permute-start | bytes 1572872 | tf_op jit(solution)/shard_map/ppermute | solution.py:519
  17.6 1.9 %collective-permute-start = (s32[1,64]{1,0:T(1,128)S(1)}, s32[1,64]{1,0:T(1,128)S(1)}, u32[]{:S(2)}, u32[]{:S(2)}) collective-permute-start(s32[1,64]{1,0:T(1,128)S(1)} %multiply_add_fusion.refs_1_), channel_id=1, source_target_pairs={{0,4},{4,0},{8,12},{12,8},{1,5},{5,1},{9,13},{13,9},{2,6},{6,2},{1... | collective-permute-start | bytes 776 | tf_op jit(solution)/shard_map/ppermute | solution.py:519
  19.5 1.3 %collective-permute-start.3 = (bf16[2,128,256]{2,1,0:T(8,128)(2,1)S(1)}, bf16[2,128,256]{2,1,0:T(8,128)(2,1)S(1)}, u32[]{:S(2)}, u32[]{:S(2)}) collective-permute-start(bf16[2,128,256]{2,1,0:T(8,128)(2,1)S(1)} %bitcast.17), channel_id=1, source_target_pairs={{0,4},{4,0},{8,12},{12,8},{1,5},{5,1},{9,13},{13,9},{2,6},{6,2},{1... | collective-permute-start | bytes 393224 | tf_op jit(solution)/shard_map/ppermute | solution.py:519
  20.9 11.5 %collective-permute-start.8 = (bf16[33,2,32,128]{3,2,1,0:T(8,128)(2,1)S(1)}, bf16[33,2,32,128]{3,2,1,0:T(8,128)(2,1)S(1)}, u32[]{:S(2)}, u32[]{:S(2)}) collective-permute-start(bf16[33,2,32,128]{3,2,1,0:T(8,128)(2,1)S(1)} %pad_maximum_fusion.refs_6_), channel_id=1, source_target_pairs={{0,4},{4,0},{8,12},{12,8},{1,5},{5,1},{9,13},{13,9},{2,6},{6,2},{1... | collective-permute-start | bytes 1622024 | tf_op jit(solution)/shard_map/ppermute | solution.py:519
  28.4 4.0 %collective-permute-start.9 = (bf16[33,2,32,128]{3,2,1,0:T(8,128)(2,1)S(1)}, bf16[33,2,32,128]{3,2,1,0:T(8,128)(2,1)S(1)}, u32[]{:S(2)}, u32[]{:S(2)}) collective-permute-start(bf16[33,2,32,128]{3,2,1,0:T(8,128)(2,1)S(1)} %collective-permute-done.7.refs_7_), channel_id=1, source_target_pairs={{0,4},{4,0},{8,12},{12,8},{1,5},{5,1},{9,13},{13,9},{2,6},{6,2},{1... | collective-permute-start | bytes 1622024 | tf_op jit(solution)/shard_map/ppermute | solution.py:519
  28.8 13.0 %collective-permute-start.11 = (bf16[1104,128]{1,0:T(8,128)(2,1)S(1)}, bf16[1104,128]{1,0:T(8,128)(2,1)S(1)}, u32[]{:S(2)}, u32[]{:S(2)}) collective-permute-start(bf16[1104,128]{1,0:T(8,128)(2,1)S(1)} %get-tuple-element.48), channel_id=1, source_target_pairs={{0,8},{4,12},{8,0},{12,4},{1,9},{5,13},{9,1},{13,5},{2,10},{6,14},... | collective-permute-start | bytes 847880 | tf_op jit(solution)/shard_map/ppermute | solution.py:522
  30.8 9.5 %collective-permute-start.6 = (bf16[34,16,256]{2,1,0:T(8,128)(2,1)S(1)}, bf16[34,16,256]{2,1,0:T(8,128)(2,1)S(1)}, u32[]{:S(2)}, u32[]{:S(2)}) collective-permute-start(bf16[34,16,256]{2,1,0:T(8,128)(2,1)S(1)} %get-tuple-element.31.refs_1_), channel_id=1, source_target_pairs={{0,16},{16,0},{1,17},{17,1},{2,18},{18,2},{3,19},{19,3},{4,20},{20... | collective-permute-start | bytes 835592 | tf_op jit(solution)/shard_map/ppermute | solution.py:573
  36.0 8.0 %collective-permute-start.10 = (bf16[1056,128]{1,0:T(8,128)(2,1)S(1)}, bf16[1056,128]{1,0:T(8,128)(2,1)S(1)}, u32[]{:S(2)}, u32[]{:S(2)}) collective-permute-start(bf16[1056,128]{1,0:T(8,128)(2,1)S(1)} %attend_1_1_1.1.refs_2_), channel_id=1, source_target_pairs={{0,8},{4,12},{8,0},{12,4},{1,9},{5,13},{9,1},{13,5},{2,10},{6,14},... | collective-permute-start | bytes 811016 | tf_op jit(solution)/shard_map/ppermute | solution.py:522

commit v6 on v5

--- a/solution.py
+++ b/solution.py
@@ -15,7 +15,7 @@
 HIDDEN = -1e30
 TO_POWER = (HEAD_DIM**-0.5) * 1.4426950408889634
 STAT_ROWS = 32
-SPARE_ROWS = 48
+SPARE_ROWS = 16
 CHUNK = 768
 OWNER = 65536
 
@@ -386,7 +386,7 @@
     asks = [queries[asked] for asked in sides]
     padding = 0
     if states is not None:
-        padding = 2
+        padding = 1
         flat = [states] + flat
         shapes.append(
             jax.ShapeDtypeStruct((states.shape[0] + padding,) + states.shape[1:], states.dtype)

time: 45.4 us -> 45.4 us (level)
  no operation moved by 1% of the time
where the time goes in v6:
time: 45.4 us; the launch traced here: 45.2 us
  Pallas kernels  24.9 us (55%)
  starting transfers between devices  10.1 us (22%)
  waiting for transfers between devices  5.07 us (11%)
  local copies, waits for them, and re-layouts  2.76 us (6%)
  between operations  2.3 us (5%)
    pallas_call x3, Pallas kernels, attend(): pl.pallas_call(functools.partial(attend_kernel, counts, head, sides, padd...  14.8 us
    pallas_call x1, Pallas kernels, mixer_from_zero(): pl.pallas_call(mixer_kernel, grid=(groups,), in_specs=[scalar, pl.BlockSp...  6.63 us
    ppermute x3, starting transfers between devices, to_opposite(): return lax.ppermute(array, 'ctx', opposite)  4.09 us
    ppermute x2, starting transfers between devices, local(): moved.append(tuple((lax.ppermute(piece, 'pool', swap) for piece in cut)))  3.23 us
    pallas_call x2, Pallas kernels, merge(): pl.pallas_call(functools.partial(merge_kernel, head), in_specs=[scalar, o...  2.07 us
    ppermute x2, waiting for transfers between devices, local(): moved.append(tuple((lax.ppermute(piece, 'pool', swap) for piece in cut)))  2.03 us
    ppermute x6, waiting for transfers between devices, to_partner(): return lax.ppermute(array, 'ctx', partner)  1.89 us
    ppermute x1, starting transfers between devices, local(): slab = lax.ppermute(ordered, 'pool', swap)  1.52 us
  transfers between devices with their start and end apart: 12, of which 4 were waited for; matrix products, arithmetic and copies ran while one was open for 0% of the time, Pallas kernels for 53%

profile of v6, /device:TPU:0, one launch (start us, length us, event | category | flops | bytes accessed | tf_op | source)
XLA Modules:
  0.0 45.2 jit_solution(7056462452257610212)
XLA Ops:
  0.6 1.2 %slice.13.refs_9_ = bf16[32,2,32,128]{3,2,1,0:T(8,128)(2,1)S(1)} slice(bf16[32,2,32,256]{3,2,1,0:T(8,128)(2,1)} %bitcast.27), slice={[0:32], [0:2], [0:32], [0:128]} | slice | bytes 1048576 | tf_op jit(solution)/shard_map/slice | solution.py:529
  1.8 3.0 %collective-permute-start.1 = (bf16[32,2,32,128]{3,2,1,0:T(8,128)(2,1)S(1)}, bf16[32,2,32,128]{3,2,1,0:T(8,128)(2,1)S(1)}, u32[]{:S(2)}, u32[]{:S(2)}) collective-permute-start(bf16[32,2,32,128]{3,2,1,0:T(8,128)(2,1)S(1)} %slice.13.refs_9_), channel_id=1, source_target_pairs={{0,16},{16,0},{1,17},{17,1},{2,18},{18,2},{3,19},{19,3},{4,20},{20... | collective-permute-start | bytes 1572872 | tf_op jit(solution)/shard_map/ppermute | solution.py:535
  4.8 0.0 copy-done.9
  4.8 0.1 slice.11
  4.9 0.0 copy-start.6
  5.0 0.0 copy-start
  5.0 0.0 copy-start.1
  5.0 0.1 pad_maximum_fusion.refs_6_
  5.1 0.2 collective-permute-start.7
  5.3 0.0 collective-permute-start.4
  5.3 0.8 %copy-done = bf16[1,128,2048]{2,1,0:T(8,128)(2,1)S(1)} copy-done((bf16[1,128,2048]{2,1,0:T(8,128)(2,1)S(1)}, bf16[1,128,2048]{2,1,0:T(8,128)(2,1)}, u32[]{:S(2)}) %copy-start) | copy-done | bytes 524312
  6.1 1.5 %collective-permute-start.2 = (bf16[128,2048]{1,0:T(8,128)(2,1)S(1)}, bf16[128,2048]{1,0:T(8,128)(2,1)S(1)}, u32[]{:S(2)}, u32[]{:S(2)}) collective-permute-start(bf16[128,2048]{1,0:T(8,128)(2,1)S(1)} %bitcast.12), channel_id=1, source_target_pairs={{0,8},{4,12},{8,0},{12,4},{1,9},{5,13},{9,1},{13,5},{2,10},{6,14},... | collective-permute-start | bytes 1572872 | tf_op jit(solution)/shard_map/ppermute | solution.py:522
  8.2 0.0 copy-start.7
  8.2 0.0 copy-start.8
  8.3 0.0 copy-done.3
  8.3 0.0 copy-done.4
  8.3 0.0 copy-done.6
  8.3 0.6 %copy-done.7 = f32[32]{0:T(128)S(1)} copy-done((f32[32]{0:T(128)S(1)}, f32[32]{0:T(128)}, u32[]{:S(2)}) %copy-start.7) | copy-done | bytes 152
  8.9 0.0 copy-done.8
  8.9 6.6 %mixer_from_zero.1 = (f32[32,16,512]{2,1,0:T(8,128)S(1)}, f32[32,16,256]{2,1,0:T(8,128)S(1)}, f32[32,512]{1,0:T(8,128)S(1)}) custom-call(s32[1]{0:T(128)S(6)} %copy.20.valid_ref, bf16[32,16,512]{2,1,0:T(8,128)(2,1)S(1)} %bitcast.21, bf16[2,256,512]{2,1,0:T(8,128)(2,1)S(1)} %bitcast.22, bf16[2,256,512]{2,1,0:T(8,128)(2,1)S(1)} %bitcast.15, ...), custom_call_target="tpu_custom_call" | custom-call | flops 1 | bytes 1 | tf_op jit(solution)/shard_map/mixer_from_zero/pallas_call | solution.py:103
  15.5 0.0 copy-start.10
  15.6 0.0 copy-start.11
  15.6 2.0 %collective-permute-done.1.refs_10_ = bf16[32,2,32,128]{3,2,1,0:T(8,128)(2,1)S(1)} collective-permute-done((bf16[32,2,32,128]{3,2,1,0:T(8,128)(2,1)S(1)}, bf16[32,2,32,128]{3,2,1,0:T(8,128)(2,1)S(1)}, u32[]{:S(2)}, u32[]{:S(2)}) %collective-permute-start.1) | collective-permute-done | bytes 524320 | tf_op jit(solution)/shard_map/ppermute | solution.py:535
  17.6 0.0 collective-permute-start.5
  17.6 0.6 %collective-permute-start = (s32[1,64]{1,0:T(1,128)S(1)}, s32[1,64]{1,0:T(1,128)S(1)}, u32[]{:S(2)}, u32[]{:S(2)}) collective-permute-start(s32[1,64]{1,0:T(1,128)S(1)} %multiply_add_fusion.refs_1_), channel_id=1, source_target_pairs={{0,4},{4,0},{8,12},{12,8},{1,5},{5,1},{9,13},{13,9},{2,6},{6,2},{1... | collective-permute-start | bytes 776 | tf_op jit(solution)/shard_map/ppermute | solution.py:519
  18.2 1.3 %collective-permute-done.refs_2_ = s32[1,64]{1,0:T(1,128)S(1)} collective-permute-done((s32[1,64]{1,0:T(1,128)S(1)}, s32[1,64]{1,0:T(1,128)S(1)}, u32[]{:S(2)}, u32[]{:S(2)}) %collective-permute-start) | collective-permute-done | bytes 288 | tf_op jit(solution)/shard_map/ppermute | solution.py:519
  19.5 0.1 collective-permute-start.3
  20.3 0.6 %collective-permute-done.3.refs_7_.refs_5_ = bf16[2,128,256]{2,1,0:T(8,128)(2,1)S(1)} collective-permute-done((bf16[2,128,256]{2,1,0:T(8,128)(2,1)S(1)}, bf16[2,128,256]{2,1,0:T(8,128)(2,1)S(1)}, u32[]{:S(2)}, u32[]{:S(2)}) %collective-permute-start.3) | collective-permute-done | bytes 131104 | tf_op jit(solution)/shard_map/ppermute | solution.py:519
  20.9 0.1 collective-permute-start.8
  21.0 0.0 collective-permute-done.4.refs_11_
  21.0 0.0 collective-permute-done.2.refs_4_.refs_3_
  21.0 0.0 collective-permute-done.5.refs_12_
  21.0 7.4 %attend_0_2_1.1 = (bf16[1072,128]{1,0:T(8,128)(2,1)S(1)}, bf16[1024,128]{1,0:T(8,128)(2,1)S(1)}, f32[8,128]{1,0:T(8,128)S(1)}, bf16[33,16,256]{2,1,0:T(8,128)(2,...) custom-call(s32[1]{0:T(128)S(6)} %copy.19.refs_0_, s32[1,64]{1,0:T(1,128)S(1)} %multiply_add_fusion.refs_1_, ...), custom_call_target="tpu_custom_call" | custom-call | flops 1 | bytes 1 | tf_op jit(solution)/shard_map/attend_0_2_1/pallas_call | solution.py:397
  28.4 0.0 collective-permute-done.7.refs_7_
  28.4 0.4 collective-permute-start.9
  28.8 2.0 %collective-permute-start.11 = (bf16[1072,128]{1,0:T(8,128)(2,1)S(1)}, bf16[1072,128]{1,0:T(8,128)(2,1)S(1)}, u32[]{:S(2)}, u32[]{:S(2)}) collective-permute-start(bf16[1072,128]{1,0:T(8,128)(2,1)S(1)} %get-tuple-element.48), channel_id=1, source_target_pairs={{0,8},{4,12},{8,0},{12,4},{1,9},{5,13},{9,1},{13,5},{2,10},{6,14},... | collective-permute-start | bytes 823304 | tf_op jit(solution)/shard_map/ppermute | solution.py:522
  30.8 1.5 %collective-permute-start.6 = (bf16[33,16,256]{2,1,0:T(8,128)(2,1)S(1)}, bf16[33,16,256]{2,1,0:T(8,128)(2,1)S(1)}, u32[]{:S(2)}, u32[]{:S(2)}) collective-permute-start(bf16[33,16,256]{2,1,0:T(8,128)(2,1)S(1)} %get-tuple-element.31.refs_1_), channel_id=1, source_target_pairs={{0,16},{16,0},{1,17},{17,1},{2,18},{18,2},{3,19},{19,3},{4,20},{20... | collective-permute-start | bytes 811016 | tf_op jit(solution)/shard_map/ppermute | solution.py:573
  32.4 0.0 collective-permute-done.8.refs_8_
  32.4 0.0 collective-permute-done.9.refs_9_
  32.4 3.6 %attend_1_1_1.1.refs_2_ = bf16[1056,128]{1,0:T(8,128)(2,1)S(1)} custom-call(bf16[64,32,128]{2,1,0:T(8,128)(2,1)S(1)} %get-tuple-element.32.refs_0_, bf16[2,16,128]{2,1,0:T(8,128)(2,1)S(1)} %get-tuple-element.30.refs_1_.chosen_ref, f32[8,128]{1,0:T(8,128)S(1)} %get-tuple-element.36.refs_2_.l_ref, ...), custom_call_target="tpu_custom_call" | custom-call | flops 1 | bytes 1 | tf_op jit(solution)/shard_map/attend_1_1_1/pallas_call | solution.py:397
  36.0 0.6 %collective-permute-start.10 = (bf16[1056,128]{1,0:T(8,128)(2,1)S(1)}, bf16[1056,128]{1,0:T(8,128)(2,1)S(1)}, u32[]{:S(2)}, u32[]{:S(2)}) collective-permute-start(bf16[1056,128]{1,0:T(8,128)(2,1)S(1)} %attend_1_1_1.1.refs_2_), channel_id=1, source_target_pairs={{0,8},{4,12},{8,0},{12,4},{1,9},{5,13},{9,1},{13,5},{2,10},{6,14},... | collective-permute-start | bytes 811016 | tf_op jit(solution)/shard_map/ppermute | solution.py:522
  36.5 3.8 %attend_1_1_0.1 = (bf16[1024,128]{1,0:T(8,128)(2,1)S(1)}, f32[8,128]{1,0:T(8,128)S(1)}) custom-call(bf16[64,32,128]{2,1,0:T(8,128)(2,1)S(1)} %get-tuple-element.32.refs_0_, bf16[2,16,128]{2,1,0:T(8,128)(2,1)S(1)} %get-tuple-element.30.refs_1_.chosen_ref, bf16[1056,128]{1,0:T(8,128)(2,1)S(1)} %attend_1_1_1.1.refs_2_, bf16[128,2048]{1,0:T(8,128)(2,1)S(1)} %bitcast.14, ...), custom_call_target="tpu_custom_call" | custom-call | flops 1 | bytes 1 | tf_op jit(solution)/shard_map/attend_1_1_0/pallas_call | solution.py:397
  40.4 0.0 collective-permute-done.6.refs_2_
  40.4 1.4 %add_saved.1 = (bf16[32,16,512]{2,1,0:T(8,128)(2,1)}, f32[32,16,256]{2,1,0:T(8,128)}, f32[8,128]{1,0:T(8,128)S(1)}) custom-call(s32[1]{0:T(128)S(6)} %copy.20.valid_ref, bf16[2,16,128]{2,1,0:T(8,128)(2,1)S(1)} %get-tuple-element.30.refs_1_.chosen_ref, f32[8,128]{1,0:T(8,128)S(1)} %get-tuple-element.39.refs_0_.l_ref, ...), custom_call_target="tpu_custom_call" | custom-call | flops 1 | bytes 1 | tf_op jit(solution)/shard_map/add_saved/pallas_call | solution.py:176
  41.8 0.0 collective-permute-done.11.got_ref
  41.8 1.0 %merge_0.1.refs_0_ = bf16[128,2048]{1,0:T(8,128)(2,1)} custom-call(s32[1]{0:T(128)S(6)} %copy.20.valid_ref, f32[8,128]{1,0:T(8,128)S(1)} %get-tuple-element.45.after_ref, bf16[1024,128]{1,0:T(8,128)(2,1)S(1)} %get-tuple-element.47.o_ref, f32[8,128]{1,0:T(8,128)S(1)} %get-tuple-element.36.refs_2_.l_ref, bf16[1072,128]{1,0:T(8,128)(2,1)S(1)} %collective-permute-done.11.got_ref), custom_call_target="tpu_custom_call" | custom-call | tf_op jit(solution)/shard_map/merge_0/pallas_call | solution.py:448
  42.8 1.1 %collective-permute-done.10.got_ref = bf16[1056,128]{1,0:T(8,128)(2,1)S(1)} collective-permute-done((bf16[1056,128]{1,0:T(8,128)(2,1)S(1)}, bf16[1056,128]{1,0:T(8,128)(2,1)S(1)}, u32[]{:S(2)}, u32[]{:S(2)}) %collective-permute-start.10) | collective-permute-done | bytes 270368 | tf_op jit(solution)/shard_map/ppermute | solution.py:522
  44.0 1.0 %merge_1.1 = bf16[128,2048]{1,0:T(8,128)(2,1)} custom-call(s32[1]{0:T(128)S(6)} %copy.20.valid_ref, f32[8,128]{1,0:T(8,128)S(1)} %get-tuple-element.45.after_ref, bf16[1024,128]{1,0:T(8,128)(2,1)S(1)} %get-tuple-element.46.o_ref, f32[8,128]{1,0:T(8,128)S(1)} %get-tuple-element.39.refs_0_.l_ref, ...), custom_call_target="tpu_custom_call", output_to_operand_aliasing={{}: (5, {})} | custom-call | tf_op jit(solution)/shard_map/merge_1/pallas_call | solution.py:448
  (12 shorter events, 0.0 us)
Async XLA Ops:
  0.6 4.2 %copy-start.9 = (bf16[1,32,2,32,256]{4,3,2,1,0:T(8,128)(2,1)S(1)}, bf16[1,32,2,32,256]{4,3,2,1,0:T(8,128)(2,1)}, u32[]{:S(2)}) copy-start(bf16[1,32,2,32,256]{4,3,2,1,0:T(8,128)(2,1)} %param.14) | copy-start | bytes 3145732
  1.8 15.8 %collective-permute-start.1 = (bf16[32,2,32,128]{3,2,1,0:T(8,128)(2,1)S(1)}, bf16[32,2,32,128]{3,2,1,0:T(8,128)(2,1)S(1)}, u32[]{:S(2)}, u32[]{:S(2)}) collective-permute-start(bf16[32,2,32,128]{3,2,1,0:T(8,128)(2,1)S(1)} %slice.13.refs_9_), channel_id=1, source_target_pairs={{0,16},{16,0},{1,17},{17,1},{2,18},{18,2},{3,19},{19,3},{4,20},{20... | collective-permute-start | bytes 1572872 | tf_op jit(solution)/shard_map/ppermute | solution.py:535
  4.8 3.4 %copy-start.3 = (bf16[1,32,16,512]{3,2,1,0:T(8,128)(2,1)S(1)}, bf16[1,32,16,512]{3,2,1,0:T(8,128)(2,1)}, u32[]{:S(2)}) copy-start(bf16[1,32,16,512]{3,2,1,0:T(8,128)(2,1)} %param.20) | copy-start | bytes 1572868
  4.8 3.4 %copy-start.4 = (bf16[1,2,256,512]{3,2,1,0:T(8,128)(2,1)S(1)}, bf16[1,2,256,512]{3,2,1,0:T(8,128)(2,1)}, u32[]{:S(2)}) copy-start(bf16[1,2,256,512]{3,2,1,0:T(8,128)(2,1)} %param.21) | copy-start | bytes 1572868
  4.9 3.3 %copy-start.6 = (f32[1,32,512]{2,1,0:T(8,128)S(1)}, f32[1,32,512]{2,1,0:T(8,128)}, u32[]{:S(2)}) copy-start(f32[1,32,512]{2,1,0:T(8,128)} %param.23) | copy-start | bytes 196612
  5.0 1.1 %copy-start = (bf16[1,128,2048]{2,1,0:T(8,128)(2,1)S(1)}, bf16[1,128,2048]{2,1,0:T(8,128)(2,1)}, u32[]{:S(2)}) copy-start(bf16[1,128,2048]{2,1,0:T(8,128)(2,1)} %param.26) | copy-start | bytes 1572868
  5.0 3.3 %copy-start.1 = (bf16[1,2,256,512]{3,2,1,0:T(8,128)(2,1)S(1)}, bf16[1,2,256,512]{3,2,1,0:T(8,128)(2,1)}, u32[]{:S(2)}) copy-start(bf16[1,2,256,512]{3,2,1,0:T(8,128)(2,1)} %param.22) | copy-start | bytes 1572868
  5.1 23.4 %collective-permute-start.7 = (bf16[33,2,32,128]{3,2,1,0:T(8,128)(2,1)S(1)}, bf16[33,2,32,128]{3,2,1,0:T(8,128)(2,1)S(1)}, u32[]{:S(2)}, u32[]{:S(2)}) collective-permute-start(bf16[33,2,32,128]{3,2,1,0:T(8,128)(2,1)S(1)} %pad_maximum_fusion.refs_6_), channel_id=1, source_target_pairs={{0,16},{16,0},{1,17},{17,1},{2,18},{18,2},{3,19},{19,3},{4,20},{20... | collective-permute-start | bytes 1622024 | tf_op jit(solution)/shard_map/ppermute | solution.py:535
  5.3 15.7 %collective-permute-start.4 = (bf16[32,2,32,128]{3,2,1,0:T(8,128)(2,1)S(1)}, bf16[32,2,32,128]{3,2,1,0:T(8,128)(2,1)S(1)}, u32[]{:S(2)}, u32[]{:S(2)}) collective-permute-start(bf16[32,2,32,128]{3,2,1,0:T(8,128)(2,1)S(1)} %slice.13.refs_9_), channel_id=1, source_target_pairs={{0,4},{4,0},{8,12},{12,8},{1,5},{5,1},{9,13},{13,9},{2,6},{6,2},{1... | collective-permute-start | bytes 1572872 | tf_op jit(solution)/shard_map/ppermute | solution.py:519
  6.1 14.9 %collective-permute-start.2 = (bf16[128,2048]{1,0:T(8,128)(2,1)S(1)}, bf16[128,2048]{1,0:T(8,128)(2,1)S(1)}, u32[]{:S(2)}, u32[]{:S(2)}) collective-permute-start(bf16[128,2048]{1,0:T(8,128)(2,1)S(1)} %bitcast.12), channel_id=1, source_target_pairs={{0,8},{4,12},{8,0},{12,4},{1,9},{5,13},{9,1},{13,5},{2,10},{6,14},... | collective-permute-start | bytes 1572872 | tf_op jit(solution)/shard_map/ppermute | solution.py:522
  8.2 0.7 %copy-start.7 = (f32[32]{0:T(128)S(1)}, f32[32]{0:T(128)}, u32[]{:S(2)}) copy-start(f32[32]{0:T(128)} %param.24) | copy-start | bytes 388
  8.2 0.7 %copy-start.8 = (f32[32]{0:T(128)S(1)}, f32[32]{0:T(128)}, u32[]{:S(2)}) copy-start(f32[32]{0:T(128)} %param.25) | copy-start | bytes 388
  8.9 10.6 %copy-start.2 = (bf16[1,2,128,256]{3,2,1,0:T(8,128)(2,1)S(1)}, bf16[1,2,128,256]{3,2,1,0:T(8,128)(2,1)}, u32[]{:S(2)}) copy-start(bf16[1,2,128,256]{3,2,1,0:T(8,128)(2,1)} %param.27) | copy-start | bytes 393220
  8.9 12.1 %copy-start.5 = (bf16[32,16,256]{2,1,0:T(8,128)(2,1)S(1)}, bf16[32,16,256]{2,1,0:T(8,128)(2,1)}, u32[]{:S(2)}) copy-start(bf16[32,16,256]{2,1,0:T(8,128)(2,1)} %refs_8_.1) | copy-start | bytes 786436
  15.5 2.1 %copy-start.10 = (s32[1,64]{1,0:T(1,128)S(1)}, s32[1,64]{1,0:T(1,128)}, u32[]{:S(2)}) copy-start(s32[1,64]{1,0:T(1,128)} %param.17) | copy-start | bytes 772
  15.6 2.0 %copy-start.11 = (s32[1,64]{1,0:T(1,128)S(1)}, s32[1,64]{1,0:T(1,128)}, u32[]{:S(2)}) copy-start(s32[1,64]{1,0:T(1,128)} %param.16) | copy-start | bytes 772
  17.6 3.4 %collective-permute-start.5 = (bf16[32,2,32,128]{3,2,1,0:T(8,128)(2,1)S(1)}, bf16[32,2,32,128]{3,2,1,0:T(8,128)(2,1)S(1)}, u32[]{:S(2)}, u32[]{:S(2)}) collective-permute-start(bf16[32,2,32,128]{3,2,1,0:T(8,128)(2,1)S(1)} %collective-permute-done.1.refs_10_), channel_id=1, source_target_pairs={{0,4},{4,0},{8,12},{12,8},{1,5},{5,1},{9,13},{13,9},{2,6},{6,2},{1... | collective-permute-start | bytes 1572872 | tf_op jit(solution)/shard_map/ppermute | solution.py:519
  17.6 1.9 %collective-permute-start = (s32[1,64]{1,0:T(1,128)S(1)}, s32[1,64]{1,0:T(1,128)S(1)}, u32[]{:S(2)}, u32[]{:S(2)}) collective-permute-start(s32[1,64]{1,0:T(1,128)S(1)} %multiply_add_fusion.refs_1_), channel_id=1, source_target_pairs={{0,4},{4,0},{8,12},{12,8},{1,5},{5,1},{9,13},{13,9},{2,6},{6,2},{1... | collective-permute-start | bytes 776 | tf_op jit(solution)/shard_map/ppermute | solution.py:519
  19.5 1.3 %collective-permute-start.3 = (bf16[2,128,256]{2,1,0:T(8,128)(2,1)S(1)}, bf16[2,128,256]{2,1,0:T(8,128)(2,1)S(1)}, u32[]{:S(2)}, u32[]{:S(2)}) collective-permute-start(bf16[2,128,256]{2,1,0:T(8,128)(2,1)S(1)} %bitcast.17), channel_id=1, source_target_pairs={{0,4},{4,0},{8,12},{12,8},{1,5},{5,1},{9,13},{13,9},{2,6},{6,2},{1... | collective-permute-start | bytes 393224 | tf_op jit(solution)/shard_map/ppermute | solution.py:519
  20.9 11.5 %collective-permute-start.8 = (bf16[33,2,32,128]{3,2,1,0:T(8,128)(2,1)S(1)}, bf16[33,2,32,128]{3,2,1,0:T(8,128)(2,1)S(1)}, u32[]{:S(2)}, u32[]{:S(2)}) collective-permute-start(bf16[33,2,32,128]{3,2,1,0:T(8,128)(2,1)S(1)} %pad_maximum_fusion.refs_6_), channel_id=1, source_target_pairs={{0,4},{4,0},{8,12},{12,8},{1,5},{5,1},{9,13},{13,9},{2,6},{6,2},{1... | collective-permute-start | bytes 1622024 | tf_op jit(solution)/shard_map/ppermute | solution.py:519
  28.4 4.0 %collective-permute-start.9 = (bf16[33,2,32,128]{3,2,1,0:T(8,128)(2,1)S(1)}, bf16[33,2,32,128]{3,2,1,0:T(8,128)(2,1)S(1)}, u32[]{:S(2)}, u32[]{:S(2)}) collective-permute-start(bf16[33,2,32,128]{3,2,1,0:T(8,128)(2,1)S(1)} %collective-permute-done.7.refs_7_), channel_id=1, source_target_pairs={{0,4},{4,0},{8,12},{12,8},{1,5},{5,1},{9,13},{13,9},{2,6},{6,2},{1... | collective-permute-start | bytes 1622024 | tf_op jit(solution)/shard_map/ppermute | solution.py:519
  28.8 13.0 %collective-permute-start.11 = (bf16[1072,128]{1,0:T(8,128)(2,1)S(1)}, bf16[1072,128]{1,0:T(8,128)(2,1)S(1)}, u32[]{:S(2)}, u32[]{:S(2)}) collective-permute-start(bf16[1072,128]{1,0:T(8,128)(2,1)S(1)} %get-tuple-element.48), channel_id=1, source_target_pairs={{0,8},{4,12},{8,0},{12,4},{1,9},{5,13},{9,1},{13,5},{2,10},{6,14},... | collective-permute-start | bytes 823304 | tf_op jit(solution)/shard_map/ppermute | solution.py:522
  30.8 9.5 %collective-permute-start.6 = (bf16[33,16,256]{2,1,0:T(8,128)(2,1)S(1)}, bf16[33,16,256]{2,1,0:T(8,128)(2,1)S(1)}, u32[]{:S(2)}, u32[]{:S(2)}) collective-permute-start(bf16[33,16,256]{2,1,0:T(8,128)(2,1)S(1)} %get-tuple-element.31.refs_1_), channel_id=1, source_target_pairs={{0,16},{16,0},{1,17},{17,1},{2,18},{18,2},{3,19},{19,3},{4,20},{20... | collective-permute-start | bytes 811016 | tf_op jit(solution)/shard_map/ppermute | solution.py:573
  36.0 8.0 %collective-permute-start.10 = (bf16[1056,128]{1,0:T(8,128)(2,1)S(1)}, bf16[1056,128]{1,0:T(8,128)(2,1)S(1)}, u32[]{:S(2)}, u32[]{:S(2)}) collective-permute-start(bf16[1056,128]{1,0:T(8,128)(2,1)S(1)} %attend_1_1_1.1.refs_2_), channel_id=1, source_target_pairs={{0,8},{4,12},{8,0},{12,4},{1,9},{5,13},{9,1},{13,5},{2,10},{6,14},... | collective-permute-start | bytes 811016 | tf_op jit(solution)/shard_map/ppermute | solution.py:522
